TPU v7x, 32 devices: a whole 2x2x4 slice. The times are simulated.
32 devices in a mesh: band: 8 (over z, x), comp: 2 (over y), tile: 2 (over core).
Axes of the slice: x: 2, y: 2, z: 4, core: 2. Of those that a mesh axis runs over, the one named last changes fastest.
Arguments:
- atmosphere: bfloat16 [192, 384, 768], P('band', None, ('comp', 'tile')), may hold values from -6 to 6
- spec_weight: float32 [2, 2, 2, 768, 96], P(None, None, None, ('comp', 'tile')), may hold values from -0.625 to 0.625
- spec_bias: float32 [2, 2, 2, 768], P(None, None, None, ('comp', 'tile')), may hold values from -4 to 4
- norm_gain: float32 [2, 2, 768], replicated, may hold values from 0.25 to 1.75
- norm_shift: float32 [2, 2, 768], replicated, may hold values from -3 to 3
- fc_in: bfloat16 [2, 768, 3072], P(None, None, ('comp', 'tile')), may hold values from -0.21875 to 0.21875
- fc_out: bfloat16 [2, 3072, 768], P(None, ('comp', 'tile')), may hold values from -0.109375 to 0.109375
- flux_head: bfloat16 [768, 8], P(('comp', 'tile')), may hold values from -0.21875 to 0.21875
- flux_embed: float32 [8, 256], replicated, may hold values from -2 to 2
- ocean_state: bfloat16 [384, 768, 256], P('band', ('comp', 'tile')), may hold values from -6 to 6
- sea_mask: int32 [384, 768], P('band', ('comp', 'tile')), may hold values 0 or 1
- depth_kernel: float32 [7, 7, 256], replicated, may hold values from -0.875 to 0.875
- ocean_gain: float32 [256], replicated, may hold values from 0.25 to 1.75
- ocean_shift: float32 [256], replicated, may hold values from -3 to 3
- ocean_in: bfloat16 [256, 1024], replicated, may hold values from -0.375 to 0.375
- ocean_out: bfloat16 [1024, 256], replicated, may hold values from -0.1875 to 0.1875
- layer_scale: float32 [256], replicated, may hold values from 0.3 to 1
- field_head: float32 [256, 4], replicated, may hold values from -0.375 to 0.375
- patch_embed: float32 [16, 768], P(None, ('comp', 'tile')), may hold values from -1.5 to 1.5
Outputs:
- atmosphere_next: bfloat16 [192, 384, 768], P('band', None, ('comp', 'tile'))
- ocean_next: bfloat16 [384, 768, 256], P('band', ('comp', 'tile'))
- surface_fields: float32 [384, 768, 4], P('band', ('comp', 'tile'))
All inputs are finite; a program needn't handle non-finite values. No bound on the sum of `sea_mask` on one device may be relied on, other than what follows from the above.
Results may differ from a plain program's by a relative error of at most 0.0095.
Values may be sent and summed in bfloat16 or wider, within the bound.
No kernel may reach another device: no remote copies, remote signals or barrier semaphores. Data moves between devices by JAX's collectives and lax.ppermute only.
A program may use at most 192 MiB of HBM per device.

v0:
```python
import math

import jax
import jax.numpy as jnp
from jax import lax
from jax.sharding import PartitionSpec as P

full_precision = lax.Precision.HIGHEST
eps_norm = 1e-06
shrink_level = 0.01


def with_halo(cells, sides, width, closed):
    for axis, dim in sides:
        count = lax.axis_size(axis)
        ends = count if closed else count - 1
        head = lax.slice_in_dim(cells, 0, width, axis=dim)
        tail = lax.slice_in_dim(cells, cells.shape[dim] - width, cells.shape[dim], axis=dim)
        cells = jnp.concatenate(
            [
                lax.ppermute(tail, axis, [(i, (i + 1) % count) for i in range(ends)]),
                cells,
                lax.ppermute(head, axis, [((i + 1) % count, i) for i in range(ends)]),
            ],
            axis=dim,
        )
    return cells


def layer_norm(values, scaling, offset):
    average = jnp.mean(values, axis=-1, keepdims=True)
    squares = jnp.mean(values * values, axis=-1, keepdims=True)
    variance = squares - average * average
    return (values - average) * lax.rsqrt(variance + eps_norm) * scaling + offset


def soft_shrink(values):
    zeros = jnp.zeros_like(values)
    return jnp.where(
        values > shrink_level,
        values - shrink_level,
        jnp.where(values < -shrink_level, values + shrink_level, zeros),
    )


def group_product(values, matrix):
    return jnp.einsum("...gi,gio->...go", values, matrix, precision=full_precision)


def mix_modes(real_part, imag_part, weights, biases):
    full_shape = real_part.shape
    group_width = weights.shape[-1]
    groups = weights.shape[-2] // group_width
    real_part = real_part.reshape(full_shape[:-1] + (groups, group_width))
    imag_part = imag_part.reshape(full_shape[:-1] + (groups, group_width))
    for sublayer in range(2):
        w_real = weights[sublayer, 0].reshape(groups, group_width, group_width)
        w_imag = weights[sublayer, 1].reshape(groups, group_width, group_width)
        b_real = biases[sublayer, 0].reshape(groups, group_width)
        b_imag = biases[sublayer, 1].reshape(groups, group_width)
        new_real = group_product(real_part, w_real) - group_product(imag_part, w_imag) + b_real
        new_imag = group_product(imag_part, w_real) + group_product(real_part, w_imag) + b_imag
        if sublayer == 0:
            new_real = jnp.maximum(new_real, 0.0)
            new_imag = jnp.maximum(new_imag, 0.0)
        real_part, imag_part = (new_real, new_imag)
    return (soft_shrink(real_part).reshape(full_shape), soft_shrink(imag_part).reshape(full_shape))


def phases(count_first, count_second, length):
    first_index = lax.broadcasted_iota(jnp.int32, (count_first, count_second), 0)
    second_index = lax.broadcasted_iota(jnp.int32, (count_first, count_second), 1)
    turns = first_index * second_index % length
    return turns.astype(jnp.float32) * (2.0 * math.pi / length)


def along_lat(matrix, values):
    return jnp.einsum("ql,lkc->qkc", matrix, values, precision=full_precision)


def channel_mlp(after_filter, layer_index, norm_gain, norm_shift, fc_in, fc_out):
    tokens = lax.all_to_all(after_filter, ("comp", "tile"), split_axis=1, concat_axis=2, tiled=True)
    flat_tokens = tokens.reshape(-1, tokens.shape[-1]).astype(jnp.float32)
    second = layer_norm(flat_tokens, norm_gain[layer_index, 1], norm_shift[layer_index, 1]).astype(
        jnp.bfloat16
    )
    hidden = jax.nn.gelu(
        jnp.dot(
            second,
            lax.all_gather(fc_in[layer_index], ("comp", "tile"), axis=1, tiled=True),
            preferred_element_type=jnp.float32,
        ),
        approximate=False,
    ).astype(jnp.bfloat16)
    summed = jnp.dot(
        hidden,
        lax.all_gather(fc_out[layer_index], ("comp", "tile"), axis=0, tiled=True),
        preferred_element_type=jnp.float32,
    )
    result = (flat_tokens + summed).astype(jnp.bfloat16).reshape(tokens.shape)
    return lax.all_to_all(result, ("comp", "tile"), split_axis=2, concat_axis=1, tiled=True)


def afno_block(
    stream, layer_index, spec_weight, spec_bias, norm_gain, norm_shift, fc_in, fc_out, column_index
):
    values = stream.astype(jnp.float32)
    slot = values.shape[-1]
    width_full = slot * lax.axis_size(("comp", "tile"))
    totals, squares = lax.psum(
        (jnp.sum(values, axis=-1), jnp.sum(values * values, axis=-1)), ("comp", "tile")
    )
    average = (totals / width_full)[..., None]
    variance = (squares / width_full)[..., None] - average * average
    scaling = lax.dynamic_slice_in_dim(norm_gain[layer_index, 0], column_index * slot, slot)
    offset = lax.dynamic_slice_in_dim(norm_shift[layer_index, 0], column_index * slot, slot)
    normed = (values - average) * lax.rsqrt(variance + eps_norm) * scaling + offset
    longitudes = values.shape[1]
    kept = longitudes // 2
    lon_scale = 1.0 / math.sqrt(longitudes)
    angles = phases(longitudes, kept, longitudes)
    cos_fwd = jnp.cos(angles) * lon_scale
    sin_fwd = jnp.sin(angles) * lon_scale
    real_part = jnp.einsum("lnc,nk->lkc", normed, cos_fwd, precision=full_precision)
    imag_part = -jnp.einsum("lnc,nk->lkc", normed, sin_fwd, precision=full_precision)
    real_part, imag_part = (
        lax.all_to_all(real_part, "band", split_axis=1, concat_axis=0, tiled=True),
        lax.all_to_all(imag_part, "band", split_axis=1, concat_axis=0, tiled=True),
    )
    latitudes = real_part.shape[0]
    lat_angles = phases(latitudes, latitudes, latitudes)
    cos_lat = jnp.cos(lat_angles) / math.sqrt(latitudes)
    sin_lat = jnp.sin(lat_angles) / math.sqrt(latitudes)
    spec_real = along_lat(cos_lat, real_part) + along_lat(sin_lat, imag_part)
    spec_imag = along_lat(cos_lat, imag_part) - along_lat(sin_lat, real_part)
    spec_real, spec_imag = mix_modes(
        spec_real, spec_imag, spec_weight[layer_index], spec_bias[layer_index]
    )
    real_part = along_lat(cos_lat, spec_real) - along_lat(sin_lat, spec_imag)
    imag_part = along_lat(cos_lat, spec_imag) + along_lat(sin_lat, spec_real)
    real_part, imag_part = (
        lax.all_to_all(real_part, "band", split_axis=0, concat_axis=1, tiled=True),
        lax.all_to_all(imag_part, "band", split_axis=0, concat_axis=1, tiled=True),
    )
    back_angles = phases(kept, longitudes, longitudes)
    mode_weight = (
        jnp.where(lax.broadcasted_iota(jnp.int32, (kept, 1), 0) == 0, 1.0, 2.0) * lon_scale
    )
    cos_back = jnp.cos(back_angles) * mode_weight
    sin_back = -jnp.sin(back_angles) * mode_weight
    restored = jnp.einsum("lkc,kn->lnc", real_part, cos_back, precision=full_precision)
    restored = restored + jnp.einsum("lkc,kn->lnc", imag_part, sin_back, precision=full_precision)
    after_filter = (values + restored + normed).astype(jnp.bfloat16)
    return channel_mlp(after_filter, layer_index, norm_gain, norm_shift, fc_in, fc_out)


def on_device(
    atmosphere,
    spec_weight,
    spec_bias,
    norm_gain,
    norm_shift,
    fc_in,
    fc_out,
    flux_head,
    flux_embed,
    ocean_state,
    sea_mask,
    depth_kernel,
    ocean_gain,
    ocean_shift,
    ocean_in,
    ocean_out,
    layer_scale,
    field_head,
    patch_embed,
):
    column_index = lax.axis_index(("comp", "tile"))
    after_one = afno_block(
        atmosphere, 0, spec_weight, spec_bias, norm_gain, norm_shift, fc_in, fc_out, column_index
    )
    flat_tokens = after_one.reshape(-1, after_one.shape[-1])
    flux_part = jnp.dot(flat_tokens, flux_head, preferred_element_type=jnp.float32).reshape(
        after_one.shape[0], after_one.shape[1], flux_head.shape[1]
    )
    fluxes = lax.psum_scatter(flux_part, ("comp", "tile"), scatter_dimension=1, tiled=True)
    upsampled = jnp.repeat(jnp.repeat(fluxes, 2, axis=0), 2, axis=1)
    sea_cells = sea_mask.astype(jnp.float32)[..., None]
    forcing = jnp.einsum("ijf,fc->ijc", upsampled, flux_embed, precision=full_precision)
    start = (ocean_state.astype(jnp.float32) + sea_cells * forcing).astype(jnp.bfloat16)
    widened = with_halo(start, ((("comp", "tile"), 1),), 3, True)
    extended = with_halo(widened, (("band", 0),), 3, False).astype(jnp.float32)
    tile_rows = start.shape[0]
    tile_columns = start.shape[1]
    convolved = jnp.zeros(start.shape, jnp.float32)
    for row_step in range(7):
        for col_step in range(7):
            convolved = (
                convolved
                + extended[row_step : row_step + tile_rows, col_step : col_step + tile_columns]
                * depth_kernel[row_step, col_step]
            )
    normed = layer_norm(convolved, ocean_gain, ocean_shift).astype(jnp.bfloat16)
    flat_cells = normed.reshape(-1, normed.shape[-1])
    hidden = jax.nn.gelu(
        jnp.dot(flat_cells, ocean_in, preferred_element_type=jnp.float32), approximate=False
    ).astype(jnp.bfloat16)
    update = jnp.dot(hidden, ocean_out, preferred_element_type=jnp.float32).reshape(start.shape)
    ocean_next = (start.astype(jnp.float32) + sea_cells * layer_scale * update).astype(jnp.bfloat16)
    surface = sea_cells * jnp.einsum(
        "ijc,cf->ijf", ocean_next.astype(jnp.float32), field_head, precision=full_precision
    )
    half_rows = tile_rows // 2
    half_columns = tile_columns // 2
    patches = (
        surface.reshape(half_rows, 2, half_columns, 2, surface.shape[2])
        .transpose(0, 2, 4, 1, 3)
        .reshape(half_rows, half_columns, -1)
    )
    patches = lax.all_gather(patches, ("comp", "tile"), axis=1, tiled=True)
    embedding = jnp.einsum("pqk,kd->pqd", patches, patch_embed, precision=full_precision)
    middle = (after_one.astype(jnp.float32) + embedding).astype(jnp.bfloat16)
    atmosphere_next = afno_block(
        middle, 1, spec_weight, spec_bias, norm_gain, norm_shift, fc_in, fc_out, column_index
    )
    return (atmosphere_next, ocean_next, surface)


def solution(mesh):
    placed = (
        P("band", None, ("comp", "tile")),
        P(None, None, None, ("comp", "tile"), None),
        P(None, None, None, ("comp", "tile")),
        P(),
        P(),
        P(None, None, ("comp", "tile")),
        P(None, ("comp", "tile"), None),
        P(("comp", "tile"), None),
        P(),
        P("band", ("comp", "tile"), None),
        P("band", ("comp", "tile")),
        P(),
        P(),
        P(),
        P(),
        P(),
        P(),
        P(),
        P(None, ("comp", "tile")),
    )
    return jax.shard_map(
        on_device,
        mesh=mesh,
        in_specs=placed,
        out_specs=(
            P("band", None, ("comp", "tile")),
            P("band", ("comp", "tile"), None),
            P("band", ("comp", "tile"), None),
        ),
        check_vma=False,
    )
```

profile of v0, /device:TPU:0, one launch (start us, length us, event | category | flops | bytes accessed | tf_op | source)
XLA Modules:
  0.0 2238.0 jit_solution(1225555993908723627)
XLA Ops:
  14.9 28.4 %all-reduce.7.cloned.1.call-done = (f32[24,384]{1,0:T(8,128)}, f32[24,384]{1,0:T(8,128)}) async-done(((f32[24,384]{1,0:T(8,128)}, f32[24,384]{1,0:T(8,128)}), (f32[24,384]{1,0:T(8,128)}, f32[24,384]{1,0:T(8,128)})) %all-reduce.7.cloned.1.call-update) | async-done | bytes 73744 | tf_op jit(solution)/shard_map/psum | solution.py:110
  44.1 11.5 fusion.203
  66.7 11.5 negate_bitcast_fusion.1
  78.3 13.9 copy.251
  92.2 79.6 %all-to-all-done = f32[24,192,192]{2,0,1:T(8,128)} async-done(((f32[24,192,192]{2,0,1:T(8,128)}), f32[24,192,192]{2,0,1:T(8,128)}, u32[]{:S(2)}, u32[]{:S(2)}) %all-to-all-start) | async-done | bytes 3538976 | tf_op jit(solution)/shard_map/all_to_all | solution.py:127
  190.7 9.3 fusion.283
  207.0 73.5 %all-to-all-done.1 = f32[24,192,192]{2,0,1:T(8,128)} async-done(((f32[24,192,192]{2,0,1:T(8,128)}), f32[24,192,192]{2,0,1:T(8,128)}, u32[]{:S(2)}, u32[]{:S(2)}) %all-to-all-start.1) | async-done | bytes 3538976 | tf_op jit(solution)/shard_map/all_to_all | solution.py:128
  325.3 9.2 add_maximum_fusion.2
  368.4 9.5 fusion.238
  392.3 9.2 convolution_add_fusion.1
  429.7 85.5 %all-to-all-done.3 = f32[192,24,192]{2,1,0:T(8,128)} async-done(((f32[192,24,192]{2,1,0:T(8,128)}), f32[192,24,192]{2,1,0:T(8,128)}, u32[]{:S(2)}, u32[]{:S(2)}) %all-to-all-start.3) | async-done | bytes 3538976 | tf_op jit(solution)/shard_map/all_to_all | solution.py:143
  533.2 90.3 %all-to-all-done.2 = f32[192,24,192]{2,1,0:T(8,128)} async-done(((f32[192,24,192]{2,1,0:T(8,128)}), f32[192,24,192]{2,1,0:T(8,128)}, u32[]{:S(2)}, u32[]{:S(2)}) %all-to-all-start.2) | async-done | bytes 3538976 | tf_op jit(solution)/shard_map/all_to_all | solution.py:142
  635.0 12.7 fusion.227
  647.7 9.7 fusion.225
  675.5 77.0 %all-to-all-done.4 = bf16[24,384,192]{2,0,1:T(8,128)(2,1)} async-done(((bf16[24,384,192]{2,0,1:T(8,128)(2,1)}), bf16[24,384,192]{2,0,1:T(8,128)(2,1)}, u32[]{:S(2)}, u32[]{:S(2)}) %all-to-all-start.4) | async-done | bytes 3538976 | tf_op jit(solution)/shard_map/all_to_all | solution.py:82
  759.3 9.6 copy.431
  769.0 22.2 fusion.537
  791.3 10.8 reshape.218
  802.2 74.4 %fusion.614 = bf16[2304,3072]{1,0:T(8,128)(2,1)} fusion(bf16[1,768,3072]{2,1,0:T(8,128)(2,1)} %all-gather.9.cloned.1.call-done, f32[2304,768]{1,0:T(8,128)} %reshape.218, f32[768]{0:T(1024)S(1)} %get-tuple-element.109, f32[768]{0:T(1024)S(1)} %get-tuple-element.105, f32[2304]{0:T(1024)S(1)} %add_rsqrt_fusion.4, f32[2304]{0:T(1024)S(1)} %div.79), kind=kOutput, calls=%fused_computation.23.clone.clone.clone.clone | convolution fusion | flops 11340546048 | bytes 25976832 | tf_op jit(solution)/shard_map/dot_general | solution.py:88
  876.6 18.1 add_convert_fusion.6
  901.2 57.6 %all_to_all.198 = bf16[24,96,768]{1,0,2:T(8,128)(2,1)S(1)} all-to-all(bf16[24,96,768]{1,0,2:T(8,128)(2,1)} %copy.283), channel_id=1, replica_groups=mesh['band'=8,'comp'=2,'tile'=2] {'comp','tile'}, dimensions={2} | all-to-all | bytes 7077888 | tf_op jit(solution)/shard_map/all_to_all | solution.py:101
  983.0 19.0 reduce-scatter.4.cloned.1.call-done
  1004.4 11.1 add_convert_fusion.2
  1025.3 12.1 collective-permute-done.2
  1042.5 71.2 %fusion.539 = (f32[48,192]{1,0:T(8,128)S(1)}, f32[48,192]{1,0:T(8,128)S(1)}, f32[48,192,256]{2,1,0:T(8,128)}) fusion(f32[256]{0:T(256)S(1)} %bitcast.520, f32[54,198,256]{2,1,0:T(8,128)S(1)} %maximum_convert_fusion, f32[256]{0:T(256)S(1)} %bitcast.521, f32[256]{0:T(256)S(1)} %bitcast.523, f32[256]{0:T(256)S(1)} %bitcast.524, f32[256]{0:T(256)S(1)} %bitcast.525, ...), kind=kLoop, calls=%fused_computation.633 | loop fusion | flops 235911168 | bytes 471983104 | tf_op jit(solution)/shard_map/reduce_sum | solution.py:31
  1120.2 89.6 %fusion.608 = bf16[9216,1024]{1,0:T(8,128)(2,1)} fusion(bf16[9216,256]{1,0:T(8,128)(2,1)S(1)} %bitcast.458, bf16[256,1024]{1,0:T(8,128)(2,1)S(1)} %copy-done), kind=kOutput, calls=%fused_computation.5.clone.clone.1 | convolution fusion | flops 5445255168 | bytes 24117248 | tf_op jit(solution)/shard_map/dot_general | solution.py:206
  1234.8 21.6 all_gather.17
  1258.8 10.5 convert_reduce_fusion
  1270.1 30.4 %all-reduce.5.cloned.1.call-done = (f32[24,384]{1,0:T(8,128)}, f32[24,384]{1,0:T(8,128)}) async-done(((f32[24,384]{1,0:T(8,128)}, f32[24,384]{1,0:T(8,128)}), (f32[24,384]{1,0:T(8,128)}, f32[24,384]{1,0:T(8,128)})) %all-reduce.5.cloned.1.call-update) | async-done | bytes 73744 | tf_op jit(solution)/shard_map/psum | solution.py:110
  1301.3 11.5 fusion.200
  1324.0 11.5 negate_bitcast_fusion
  1340.7 88.4 %all-to-all-done.6 = f32[24,192,192]{2,0,1:T(8,128)} async-done(((f32[24,192,192]{2,0,1:T(8,128)}), f32[24,192,192]{2,0,1:T(8,128)}, u32[]{:S(2)}, u32[]{:S(2)}) %all-to-all-start.6) | async-done | bytes 3538976 | tf_op jit(solution)/shard_map/all_to_all | solution.py:127
  1446.5 9.3 fusion.277
  1462.8 75.0 %all-to-all-done.7 = f32[24,192,192]{2,0,1:T(8,128)} async-done(((f32[24,192,192]{2,0,1:T(8,128)}), f32[24,192,192]{2,0,1:T(8,128)}, u32[]{:S(2)}, u32[]{:S(2)}) %all-to-all-start.7) | async-done | bytes 3538976 | tf_op jit(solution)/shard_map/all_to_all | solution.py:128
  1583.0 9.2 add_maximum_fusion
  1626.0 9.6 fusion.234
  1650.1 9.2 convolution_add_fusion
  1687.5 85.5 %all-to-all-done.9 = f32[192,24,192]{2,1,0:T(8,128)} async-done(((f32[192,24,192]{2,1,0:T(8,128)}), f32[192,24,192]{2,1,0:T(8,128)}, u32[]{:S(2)}, u32[]{:S(2)}) %all-to-all-start.9) | async-done | bytes 3538976 | tf_op jit(solution)/shard_map/all_to_all | solution.py:143
  1789.9 91.5 %all-to-all-done.8 = f32[192,24,192]{2,1,0:T(8,128)} async-done(((f32[192,24,192]{2,1,0:T(8,128)}), f32[192,24,192]{2,1,0:T(8,128)}, u32[]{:S(2)}, u32[]{:S(2)}) %all-to-all-start.8) | async-done | bytes 3538976 | tf_op jit(solution)/shard_map/all_to_all | solution.py:142
  1892.9 12.7 fusion.226
  1905.6 9.7 fusion.224
  1932.0 78.4 %all-to-all-done.10 = bf16[24,384,192]{2,0,1:T(8,128)(2,1)} async-done(((bf16[24,384,192]{2,0,1:T(8,128)(2,1)}), bf16[24,384,192]{2,0,1:T(8,128)(2,1)}, u32[]{:S(2)}, u32[]{:S(2)}) %all-to-all-start.10) | async-done | bytes 3538976 | tf_op jit(solution)/shard_map/all_to_all | solution.py:82
  2017.1 9.6 copy.430
  2026.8 22.2 fusion.538
  2049.1 10.8 reshape.219
  2060.0 74.2 %fusion.611 = bf16[2304,3072]{1,0:T(8,128)(2,1)} fusion(bf16[1,768,3072]{2,1,0:T(8,128)(2,1)} %all-gather.13.cloned.1.call-done, f32[2304,768]{1,0:T(8,128)} %reshape.219, f32[768]{0:T(1024)S(1)} %copy-done.35, f32[768]{0:T(1024)S(1)} %copy-done.34, f32[2304]{0:T(1024)S(1)} %add_rsqrt_fusion.3, f32[2304]{0:T(1024)S(1)} %div.87), kind=kOutput, calls=%fused_computation.26.clone.clone.clone.clone.1 | convolution fusion | flops 11340546048 | bytes 25976832 | tf_op jit(solution)/shard_map/dot_general | solution.py:88
  2134.2 18.2 add_convert_fusion.3
  2159.0 57.7 %all_to_all.199 = bf16[24,96,768]{1,0,2:T(8,128)(2,1)S(1)} all-to-all(bf16[24,96,768]{1,0,2:T(8,128)(2,1)} %copy.327), channel_id=1, replica_groups=mesh['band'=8,'comp'=2,'tile'=2] {'comp','tile'}, dimensions={2} | all-to-all | bytes 7077888 | tf_op jit(solution)/shard_map/all_to_all | solution.py:101
  (293 shorter events, 538.7 us)
Async XLA Ops:
  7.2 1113.1 %copy-start = (bf16[256,1024]{1,0:T(8,128)(2,1)S(1)}, bf16[256,1024]{1,0:T(8,128)(2,1)}, u32[]{:S(2)}) copy-start(bf16[256,1024]{1,0:T(8,128)(2,1)} %param.33) | copy-start | bytes 1572868
  7.2 36.1 %all-reduce.7.cloned.1.call-start = ((), (), s32[]{:S(2)}) async-start(), calls=%async_computation.19 | async-start | bytes 147456 | tf_op jit(solution)/shard_map/psum | solution.py:110
  60.8 110.9 %all-to-all-start = ((f32[24,192,192]{2,0,1:T(8,128)}), f32[24,192,192]{2,0,1:T(8,128)}, u32[]{:S(2)}, u32[]{:S(2)}) async-start(f32[24,192,192]{2,0,1:T(8,128)} %copy.247), calls=%async_computation | async-start | bytes 9437184 | tf_op jit(solution)/shard_map/all_to_all | solution.py:127
  78.2 98.1 %copy-start.27 = (f32[2,2,2,192]{3,2,1,0:T(2,128)S(1)}, f32[2,2,2,192]{3,2,1,0:T(2,128)}, u32[]{:S(2)}) copy-start(f32[2,2,2,192]{3,2,1,0:T(2,128)} %param.21) | copy-start | bytes 18436
  78.3 99.1 %copy-start.20 = (f32[2,2,2,192,96]{4,3,2,1,0:T(8,128)S(1)}, f32[2,2,2,192,96]{4,3,2,1,0:T(8,128)}, u32[]{:S(2)}) copy-start(f32[2,2,2,192,96]{4,3,2,1,0:T(8,128)} %param.20) | copy-start | bytes 1769476
  171.8 108.7 %all-to-all-start.1 = ((f32[24,192,192]{2,0,1:T(8,128)}), f32[24,192,192]{2,0,1:T(8,128)}, u32[]{:S(2)}, u32[]{:S(2)}) async-start(f32[24,192,192]{2,0,1:T(8,128)} %copy.251), calls=%async_computation.1 | async-start | bytes 9437184 | tf_op jit(solution)/shard_map/all_to_all | solution.py:128
  307.0 17.6 copy-start.7
  362.0 15.9 slice-start.12
  406.3 108.9 %all-to-all-start.3 = ((f32[192,24,192]{2,1,0:T(8,128)}), f32[192,24,192]{2,1,0:T(8,128)}, u32[]{:S(2)}, u32[]{:S(2)}) async-start(f32[192,24,192]{2,1,0:T(8,128)} %copy.278), calls=%async_computation.3 | async-start | bytes 9437184 | tf_op jit(solution)/shard_map/all_to_all | solution.py:143
  424.8 95.1 %copy-start.13 = (bf16[2,768,768]{2,1,0:T(8,128)(2,1)S(1)}, bf16[2,768,768]{2,1,0:T(8,128)(2,1)}, u32[]{:S(2)}) copy-start(bf16[2,768,768]{2,1,0:T(8,128)(2,1)} %param.24) | copy-start | bytes 7077892
  515.2 108.3 %all-to-all-start.2 = ((f32[192,24,192]{2,1,0:T(8,128)}), f32[192,24,192]{2,1,0:T(8,128)}, u32[]{:S(2)}, u32[]{:S(2)}) async-start(f32[192,24,192]{2,1,0:T(8,128)} %copy.273), calls=%async_computation.2 | async-start | bytes 9437184 | tf_op jit(solution)/shard_map/all_to_all | solution.py:142
  519.8 282.4 %all-gather.9.cloned.1.call-start = ((), (), s32[]{:S(2)}) async-start(), calls=%async_computation.13 | async-start | bytes 5898240 | tf_op jit(solution)/shard_map/all_gather | solution.py:90
  521.5 126.2 %copy-start.23 = (f32[192]{0:T(256)}, f32[192]{0:T(256)S(1)}, u32[]{:S(2)}) copy-start(f32[192]{0:T(256)S(1)} %fusion.354) | copy-start | bytes 2308
  635.0 22.4 copy-start.11
  668.5 84.1 %all-to-all-start.4 = ((bf16[24,384,192]{2,0,1:T(8,128)(2,1)}), bf16[24,384,192]{2,0,1:T(8,128)(2,1)}, u32[]{:S(2)}, u32[]{:S(2)}) async-start(bf16[24,384,192]{2,0,1:T(8,128)(2,1)} %copy.281), calls=%async_computation.4 | async-start | bytes 9437184 | tf_op jit(solution)/shard_map/all_to_all | solution.py:82
  673.5 203.1 %all-gather.11.cloned.1.call-start = ((), (), s32[]{:S(2)}) async-start(), calls=%async_computation.14 | async-start | bytes 5898240 | tf_op jit(solution)/shard_map/all_gather | solution.py:97
  675.1 327.0 %reduce-scatter.4.cloned.1.call-start = ((), (), s32[]{:S(2)}) async-start(), calls=%async_computation.17 | async-start | bytes 491520
  958.8 14.0 copy-start.29
  964.7 18.3 copy-start.25
  972.9 31.6 %copy-start.28 = (f32[8,256]{1,0:T(8,128)S(1)}, f32[8,256]{1,0:T(8,128)}, u32[]{:S(2)}) copy-start(f32[8,256]{1,0:T(8,128)} %param.27) | copy-start | bytes 24580
  982.9 34.6 %copy-start.26 = (f32[7,7,256]{2,1,0:T(8,128)S(1)}, f32[7,7,256]{2,1,0:T(8,128)}, u32[]{:S(2)}) copy-start(f32[7,7,256]{2,1,0:T(8,128)} %param.30) | copy-start | bytes 150532
  982.9 317.5 %all-reduce.5.cloned.1.call-start = ((), (), s32[]{:S(2)}) async-start(), calls=%async_computation.18 | async-start | bytes 147456 | tf_op jit(solution)/shard_map/psum | solution.py:110
  983.0 37.4 %copy-start.21 = (f32[48,192]{1,0:T(8,128)}, f32[48,192]{1,0:T(8,128)S(1)}, u32[]{:S(2)}) copy-start(f32[48,192]{1,0:T(8,128)S(1)} %convert_element_type.165) | copy-start | bytes 110596
  1015.6 26.9 %copy-start.2 = (bf16[48,192,256]{2,1,0:T(8,128)(2,1)}, bf16[48,192,256]{2,1,0:T(8,128)(2,1)S(1)}, u32[]{:S(2)}) copy-start(bf16[48,192,256]{2,1,0:T(8,128)(2,1)S(1)} %add_convert_fusion.2) | copy-start | bytes 14155780
  1015.7 4.6 collective-permute-start
  1015.7 4.5 collective-permute-start.1
  1020.4 17.0 collective-permute-start.2
  1023.5 13.9 collective-permute-start.3
  1042.5 71.3 %copy-start.38 = (f32[256]{0:T(256)S(1)}, f32[256]{0:T(256)}, u32[]{:S(2)}) copy-start(f32[256]{0:T(256)} %param.32) | copy-start | bytes 3076
  1042.5 71.3 %copy-start.39 = (f32[256]{0:T(256)S(1)}, f32[256]{0:T(256)}, u32[]{:S(2)}) copy-start(f32[256]{0:T(256)} %param.31) | copy-start | bytes 3076
  1120.2 89.6 %copy-start.40 = (bf16[1024,256]{1,0:T(8,128)(2,1)S(1)}, bf16[1024,256]{1,0:T(8,128)(2,1)}, u32[]{:S(2)}) copy-start(bf16[1024,256]{1,0:T(8,128)(2,1)} %param.34) | copy-start | bytes 1572868
  1226.8 42.6 %copy-start.19 = (f32[48,192,4]{1,2,0:T(4,128)}, f32[48,192,4]{1,2,0:T(4,128)S(1)}, u32[]{:S(2)}) copy-start(f32[48,192,4]{1,2,0:T(4,128)S(1)} %convolution_multiply_fusion) | copy-start | bytes 442372
  1226.8 32.0 %copy-start.41 = (f32[16,192]{1,0:T(8,128)S(1)}, f32[16,192]{1,0:T(8,128)}, u32[]{:S(2)}) copy-start(f32[16,192]{1,0:T(8,128)} %param.37) | copy-start | bytes 36868
  1318.2 110.9 %all-to-all-start.6 = ((f32[24,192,192]{2,0,1:T(8,128)}), f32[24,192,192]{2,0,1:T(8,128)}, u32[]{:S(2)}, u32[]{:S(2)}) async-start(f32[24,192,192]{2,0,1:T(8,128)} %copy.291), calls=%async_computation.6 | async-start | bytes 9437184 | tf_op jit(solution)/shard_map/all_to_all | solution.py:127
  1335.6 98.1 %copy-start.33 = (f32[192]{0:T(256)S(1)}, f32[192]{0:T(256)}, u32[]{:S(2)}) copy-start(f32[192]{0:T(256)} %get-tuple-element.20) | copy-start | bytes 2308
  1335.6 98.2 %copy-start.32 = (f32[192]{0:T(256)S(1)}, f32[192]{0:T(256)}, u32[]{:S(2)}) copy-start(f32[192]{0:T(256)} %get-tuple-element.19) | copy-start | bytes 2308
  1335.6 98.3 %copy-start.31 = (f32[192]{0:T(256)S(1)}, f32[192]{0:T(256)}, u32[]{:S(2)}) copy-start(f32[192]{0:T(256)} %get-tuple-element.17) | copy-start | bytes 2308
  1335.6 98.4 %copy-start.30 = (f32[192]{0:T(256)S(1)}, f32[192]{0:T(256)}, u32[]{:S(2)}) copy-start(f32[192]{0:T(256)} %get-tuple-element.18) | copy-start | bytes 2308
  1429.1 108.7 %all-to-all-start.7 = ((f32[24,192,192]{2,0,1:T(8,128)}), f32[24,192,192]{2,0,1:T(8,128)}, u32[]{:S(2)}, u32[]{:S(2)}) async-start(f32[24,192,192]{2,0,1:T(8,128)} %copy.295), calls=%async_computation.7 | async-start | bytes 9437184 | tf_op jit(solution)/shard_map/all_to_all | solution.py:128
  1564.6 17.6 copy-start.6
  1619.6 16.0 slice-start.14
  1664.1 108.9 %all-to-all-start.9 = ((f32[192,24,192]{2,1,0:T(8,128)}), f32[192,24,192]{2,1,0:T(8,128)}, u32[]{:S(2)}, u32[]{:S(2)}) async-start(f32[192,24,192]{2,1,0:T(8,128)} %copy.322), calls=%async_computation.9 | async-start | bytes 9437184 | tf_op jit(solution)/shard_map/all_to_all | solution.py:143
  1773.0 108.3 %all-to-all-start.8 = ((f32[192,24,192]{2,1,0:T(8,128)}), f32[192,24,192]{2,1,0:T(8,128)}, u32[]{:S(2)}, u32[]{:S(2)}) async-start(f32[192,24,192]{2,1,0:T(8,128)} %copy.317), calls=%async_computation.8 | async-start | bytes 9437184 | tf_op jit(solution)/shard_map/all_to_all | solution.py:142
  1777.7 282.3 %all-gather.13.cloned.1.call-start = ((), (), s32[]{:S(2)}) async-start(), calls=%async_computation.15 | async-start | bytes 5898240 | tf_op jit(solution)/shard_map/all_gather | solution.py:90
  1892.9 22.4 copy-start.12
  1926.3 84.1 %all-to-all-start.10 = ((bf16[24,384,192]{2,0,1:T(8,128)(2,1)}), bf16[24,384,192]{2,0,1:T(8,128)(2,1)}, u32[]{:S(2)}, u32[]{:S(2)}) async-start(bf16[24,384,192]{2,0,1:T(8,128)(2,1)} %copy.325), calls=%async_computation.10 | async-start | bytes 9437184 | tf_op jit(solution)/shard_map/all_to_all | solution.py:82
  1931.2 203.0 %all-gather.15.cloned.1.call-start = ((), (), s32[]{:S(2)}) async-start(), calls=%async_computation.16 | async-start | bytes 5898240 | tf_op jit(solution)/shard_map/all_gather | solution.py:97
  2159.0 71.7 %copy-start.1 = (bf16[256,1024]{1,0:T(8,128)(2,1)S(1)}, bf16[256,1024]{1,0:T(8,128)(2,1)}, u32[]{:S(2)}) copy-start(bf16[256,1024]{1,0:T(8,128)(2,1)} %param.33) | copy-start | bytes 1572868
  (35 other events, 322.7 us)
Sparse Core Ops, SparseCore 0:
  11.1 32.1 all-reduce.6
  522.3 37.8 all-gather.8
  676.5 62.3 all-gather.10
  983.1 18.9 reduce-scatter.3
  1269.5 30.9 all-reduce.4
  1779.7 37.8 all-gather.12
  1933.6 62.3 all-gather.14
where the time goes:
time: 2250 us; the launch traced here: 2240 us
  waiting for transfers between devices  918 us (41%)
  matrix products  644 us (29%)
  local copies, waits for them, and re-layouts  305 us (14%)
  other arithmetic  159 us (7%)
  blocking collectives  137 us (6%)
  starting transfers between devices  58.2 us (3%)
    all_to_all x2, waiting for transfers between devices, afno_block(): lax.all_to_all(real_part, 'band', split_axis=0, concat_axis=1, tiled=True)  182 us
    all_to_all x2, waiting for transfers between devices, afno_block(): lax.all_to_all(imag_part, 'band', split_axis=0, concat_axis=1, tiled=True)  171 us
    all_to_all x2, waiting for transfers between devices, afno_block(): lax.all_to_all(real_part, 'band', split_axis=1, concat_axis=0, tiled=True)  168 us
    all_to_all x2, waiting for transfers between devices, channel_mlp(): lax.all_to_all(after_filter, ('comp', 'tile'), split_axis=1, concat_axis=...  155 us
    dot_general x2, matrix products, channel_mlp(): jnp.dot(second, lax.all_gather(fc_in[layer_index], ('comp', 'tile'), axis...  149 us
    all_to_all x2, waiting for transfers between devices, afno_block(): lax.all_to_all(imag_part, 'band', split_axis=1, concat_axis=0, tiled=True)  148 us
    dot_general x16, matrix products, group_product(): jnp.einsum('...gi,gio->...go', values, matrix, precision=full_precision)  120 us
    reduce_sum x3, other arithmetic, layer_norm(): average = jnp.mean(values, axis=-1, keepdims=True)  116 us
  transfers between devices with their start and end apart: 21, of which 15 were waited for; matrix products, arithmetic and copies ran while one was open for 23% of the time, Pallas kernels for 0%

commit v1 on v0

v1 whole, which is shorter than its diff:
```python
import functools
import math

import jax
import jax.numpy as jnp
from jax import lax
from jax.experimental import pallas as pl
from jax.experimental.pallas import tpu as pltpu
from jax.sharding import PartitionSpec as P

full_precision = lax.Precision.HIGHEST
eps_norm = 1e-06
shrink_level = 0.01
f32 = jnp.float32
bf16 = jnp.bfloat16
quarter = ("comp", "tile")
vmem_bytes = 56 * 1024 * 1024

tail_log2 = (
    -0.9999930608094244,
    -1.1512017040487785,
    -0.45877096697476855,
    -0.053412112881497276,
    0.008080722210665518,
    -0.0007692214388919801,
    3.309301407796759e-05,
)
tail_end = 6.0


def gelu(x):
    a = jnp.minimum(jnp.abs(x), tail_end)
    power = tail_log2[-1] * a + tail_log2[-2]
    for c in tail_log2[-3::-1]:
        power = power * a + c
    return jnp.maximum(x, 0.0) - a * jnp.exp2(power)


def pick(n, cap):
    for t in range(cap, 0, -16):
        if n % t == 0:
            return t
    return n


def dot(a, b):
    return jnp.dot(a, b, preferred_element_type=f32)


def layer_norm(values, scaling, offset):
    average = jnp.mean(values, axis=-1, keepdims=True)
    squares = jnp.mean(values * values, axis=-1, keepdims=True)
    variance = squares - average * average
    return (values - average) * lax.rsqrt(variance + eps_norm) * scaling + offset


def split3(x, axis):
    high = lax.reduce_precision(x, 8, 7)
    low = x - high
    return high.astype(bf16), lax.reduce_precision(low, 8, 7).astype(bf16)


def product_left(x):
    high, low = split3(x, -1)
    return jnp.concatenate([high, low, high], axis=-1)


def product_right(x):
    high, low = split3(x, 0)
    return jnp.concatenate([high, high, low], axis=0)


def whole(shape):
    return pl.BlockSpec(shape, lambda *_: (0,) * len(shape))


def shift_sum(x, axes):
    for axis in axes:
        n = lax.axis_size(axis)
        mine = x
        for d in range(1, n):
            x = x + lax.ppermute(mine, axis, [(i, (i + d) % n) for i in range(n)])
    return x


def gathered(x, axes):
    parts = [x]
    for axis in axes:
        n = lax.axis_size(axis)
        parts = parts + [
            lax.ppermute(part, axis, [(i, (i + d) % n) for i in range(n)])
            for d in range(1, n)
            for part in parts
        ]
    return parts


def gathered_pairs(x, y, axes):
    return gathered(x, axes), gathered(y, axes)


def mlp_rows(filtered, gain, shift, w_in, w_out):
    n2 = layer_norm(filtered, gain, shift).astype(bf16)
    total = filtered
    for a, b in zip(w_in, w_out):
        total = total + dot(gelu(dot(n2, a[...])).astype(bf16), b[...])
    return total.astype(bf16)


def first_mlp_kernel(n, u_ref, gain, shift, head, *refs):
    w_in, w_out, (out_ref, flux_ref) = refs[:n], refs[n : 2 * n], refs[2 * n :]
    u = jnp.concatenate([u_ref[i].astype(f32) for i in range(u_ref.shape[0])], axis=-1)
    out = mlp_rows(u, gain[...], shift[...], w_in, w_out)
    out_ref[...] = out
    flux_ref[...] = dot(out, head[...])


def first_mlp(u, gain, shift, head, w_in, w_out):
    slots, tokens, width = u.shape
    full = slots * width
    tile = pick(tokens, 384)
    n = len(w_in)
    hidden = sum(w.shape[1] for w in w_in)
    return pl.pallas_call(
        functools.partial(first_mlp_kernel, n),
        grid=(tokens // tile,),
        in_specs=[
            pl.BlockSpec((slots, tile, width), lambda i: (0, i, 0)),
            whole((1, full)),
            whole((1, full)),
            whole(head.shape),
        ]
        + [whole(w.shape) for w in w_in]
        + [whole(w.shape) for w in w_out],
        out_specs=[
            pl.BlockSpec((tile, full), lambda i: (i, 0)),
            pl.BlockSpec((tile, head.shape[1]), lambda i: (i, 0)),
        ],
        out_shape=[
            jax.ShapeDtypeStruct((tokens, full), bf16),
            jax.ShapeDtypeStruct((tokens, head.shape[1]), f32),
        ],
        compiler_params=pltpu.CompilerParams(vmem_limit_bytes=vmem_bytes),
        cost_estimate=pl.CostEstimate(
            flops=4 * tokens * full * hidden,
            bytes_accessed=4 * tokens * full + 4 * full * hidden,
            transcendentals=tokens * hidden,
        ),
    )(u, gain, shift, head, *w_in, *w_out)


def second_mlp_kernel(n, v_ref, r_ref, gain0, shift0, gain, shift, *refs):
    w_in, w_out, out_ref = refs[:n], refs[n : 2 * n], refs[2 * n]
    v = v_ref[...].astype(f32)
    r = jnp.concatenate([r_ref[i].astype(f32) for i in range(r_ref.shape[0])], axis=-1)
    u = (v + r + layer_norm(v, gain0[...], shift0[...])).astype(bf16).astype(f32)
    out = mlp_rows(u, gain[...], shift[...], w_in, w_out)
    width = out_ref.shape[2]
    for i in range(out_ref.shape[0]):
        out_ref[i] = out[:, i * width : (i + 1) * width]


def second_mlp(v, r, gain0, shift0, gain, shift, w_in, w_out):
    slots, tokens, width = r.shape
    full = slots * width
    tile = pick(tokens, 384)
    n = len(w_in)
    hidden = sum(w.shape[1] for w in w_in)
    return pl.pallas_call(
        functools.partial(second_mlp_kernel, n),
        grid=(tokens // tile,),
        in_specs=[
            pl.BlockSpec((tile, full), lambda i: (i, 0)),
            pl.BlockSpec((slots, tile, width), lambda i: (0, i, 0)),
        ]
        + [whole((1, full))] * 4
        + [whole(w.shape) for w in w_in]
        + [whole(w.shape) for w in w_out],
        out_specs=pl.BlockSpec((slots, tile, width), lambda i: (0, i, 0)),
        out_shape=jax.ShapeDtypeStruct((slots, tokens, width), bf16),
        compiler_params=pltpu.CompilerParams(vmem_limit_bytes=vmem_bytes),
        cost_estimate=pl.CostEstimate(
            flops=4 * tokens * full * hidden,
            bytes_accessed=6 * tokens * full + 4 * full * hidden,
            transcendentals=tokens * hidden,
        ),
    )(v, r, gain0, shift0, gain, shift, *w_in, *w_out)


def middle_kernel(a_ref, p_ref, e_ref, gain, shift, v_ref, n_ref):
    v = (a_ref[...].astype(f32) + dot(p_ref[...], e_ref[...])).astype(bf16)
    v_ref[...] = v
    normed = layer_norm(v.astype(f32), gain[...], shift[...]).astype(bf16)
    width = n_ref.shape[2]
    for i in range(n_ref.shape[0]):
        n_ref[i] = normed[:, i * width : (i + 1) * width]


def make_middle(a, patches, embed, gain, shift, slots):
    tokens, full = a.shape
    tile = pick(tokens, 384)
    return pl.pallas_call(
        middle_kernel,
        grid=(tokens // tile,),
        in_specs=[
            pl.BlockSpec((tile, full), lambda i: (i, 0)),
            pl.BlockSpec((tile, patches.shape[1]), lambda i: (i, 0)),
            whole(embed.shape),
            whole((1, full)),
            whole((1, full)),
        ],
        out_specs=[
            pl.BlockSpec((tile, full), lambda i: (i, 0)),
            pl.BlockSpec((slots, tile, full // slots), lambda i: (0, i, 0)),
        ],
        out_shape=[
            jax.ShapeDtypeStruct((tokens, full), bf16),
            jax.ShapeDtypeStruct((slots, tokens, full // slots), bf16),
        ],
        compiler_params=pltpu.CompilerParams(vmem_limit_bytes=vmem_bytes),
    )(a, patches, embed, gain, shift)


def soft_shrink(y):
    return y - jnp.clip(y, -shrink_level, shrink_level)


def modes_kernel(x_ref, fwd, back, weights, biases, z_ref):
    lats = x_ref.shape[1] // 2
    for k in range(x_ref.shape[0]):
        s = dot(fwd[...], x_ref[k]).astype(bf16)
        for layer in range(2):
            s_re, s_im = s[:lats], s[lats:]
            y_re = dot(s_re, weights[layer, 0]) - dot(s_im, weights[layer, 1])
            y_im = dot(s_im, weights[layer, 0]) + dot(s_re, weights[layer, 1])
            y_re = y_re + biases[layer, 0]
            y_im = y_im + biases[layer, 1]
            if layer == 0:
                y_re, y_im = jnp.maximum(y_re, 0.0), jnp.maximum(y_im, 0.0)
            else:
                y_re, y_im = soft_shrink(y_re), soft_shrink(y_im)
            s = jnp.concatenate([y_re.astype(bf16), y_im.astype(bf16)], axis=0)
        z_ref[k] = dot(back[...], s).astype(bf16)


def mix_modes(x, fwd, back, weights, biases):
    waves, rows, width = x.shape
    step = 3 if waves % 3 == 0 else 1
    return pl.pallas_call(
        modes_kernel,
        grid=(waves // step,),
        in_specs=[
            pl.BlockSpec((step, rows, width), lambda i: (i, 0, 0)),
            whole(fwd.shape),
            whole(back.shape),
            whole(weights.shape),
            whole(biases.shape),
        ],
        out_specs=pl.BlockSpec((step, rows, width), lambda i: (i, 0, 0)),
        out_shape=jax.ShapeDtypeStruct(x.shape, bf16),
        compiler_params=pltpu.CompilerParams(vmem_limit_bytes=vmem_bytes),
        cost_estimate=pl.CostEstimate(
            flops=waves * 4 * (rows * rows * width + 2 * rows * width * width),
            bytes_accessed=4 * waves * rows * width,
            transcendentals=0,
        ),
    )(x, fwd, back, weights, biases)


def ocean_kernel(on_ref, start_ref, mask_ref, w_in, w_out, scale, head, next_ref, field_ref):
    half = w_in.shape[1] // 2
    fields = field_ref.shape[1]
    total = None
    for i in range(2):
        h = gelu(dot(on_ref[...], w_in[:, i * half : (i + 1) * half])).astype(bf16)
        part = dot(h, w_out[i * half : (i + 1) * half, :])
        total = part if total is None else total + part
    mask = mask_ref[...]
    out = (start_ref[...].astype(f32) + mask * (scale[...] * total)).astype(bf16)
    next_ref[...] = out
    parts = dot(out, head[...])
    field_ref[...] = mask * (
        parts[:, :fields] + parts[:, fields : 2 * fields] + parts[:, 2 * fields :]
    )


def ocean_mlp(on, start, mask, w_in, w_out, scale, head):
    cells, width = on.shape
    tile = pick(cells, 768)
    fields = head.shape[1]
    high = lax.reduce_precision(head, 8, 7)
    mid = lax.reduce_precision(head - high, 8, 7)
    heads = jnp.concatenate([high, mid, head - high - mid], axis=1).astype(bf16)
    rows = lambda n: pl.BlockSpec((tile, n), lambda i: (i, 0))
    return pl.pallas_call(
        ocean_kernel,
        grid=(cells // tile,),
        in_specs=[
            rows(width),
            rows(width),
            rows(1),
            whole(w_in.shape),
            whole(w_out.shape),
            whole((1, width)),
            whole(heads.shape),
        ],
        out_specs=[rows(width), rows(fields)],
        out_shape=[
            jax.ShapeDtypeStruct((cells, width), bf16),
            jax.ShapeDtypeStruct((cells, fields), f32),
        ],
        compiler_params=pltpu.CompilerParams(vmem_limit_bytes=vmem_bytes),
        cost_estimate=pl.CostEstimate(
            flops=4 * cells * width * w_in.shape[1],
            bytes_accessed=8 * cells * width,
            transcendentals=cells * w_in.shape[1],
        ),
    )(on, start, mask, w_in, w_out, scale[None], heads)


def phases(count_first, count_second, length):
    first_index = lax.broadcasted_iota(jnp.int32, (count_first, count_second), 0)
    second_index = lax.broadcasted_iota(jnp.int32, (count_first, count_second), 1)
    turns = first_index * second_index % length
    return turns.astype(f32) * (2.0 * math.pi / length)


def lon_matrices(longitudes, bands):
    kept = longitudes // 2
    scale = 1.0 / math.sqrt(longitudes)
    angles = phases(longitudes, kept, longitudes)
    cos, sin = jnp.cos(angles) * scale, jnp.sin(angles) * scale
    weight = jnp.where(lax.broadcasted_iota(jnp.int32, (1, kept), 1) == 0, 1.0, 2.0)
    shape = (longitudes, bands, kept // bands, 1)

    def laid(re, im):
        both = jnp.concatenate([re.reshape(shape), im.reshape(shape)], axis=-1)
        return both.reshape(longitudes, -1).astype(bf16)

    return laid(cos, -sin), laid(cos * weight, -sin * weight)


def lat_matrices(lats):
    angles = phases(lats, lats, lats)
    cos = jnp.cos(angles) / math.sqrt(lats)
    sin = jnp.sin(angles) / math.sqrt(lats)
    fwd = jnp.concatenate(
        [jnp.concatenate([cos, sin], axis=1), jnp.concatenate([-sin, cos], axis=1)], axis=0
    )
    back = jnp.concatenate(
        [jnp.concatenate([cos, -sin], axis=1), jnp.concatenate([sin, cos], axis=1)], axis=0
    )
    return fwd.astype(bf16), back.astype(bf16)


def dense_groups(weights):
    width, group = weights.shape[-2], weights.shape[-1]
    groups = width // group
    tiled = jnp.concatenate([weights] * groups, axis=-1)
    row = lax.broadcasted_iota(jnp.int32, (width, width), 0) // group
    column = lax.broadcasted_iota(jnp.int32, (width, width), 1) // group
    return jnp.where(row == column, tiled, 0.0).astype(bf16)


def spectral_filter(normed, lon_fwd, lon_back, lat_fwd, lat_back, weights, biases):
    rows, longitudes, width = normed.shape
    bands = lax.axis_size("band")
    waves = longitudes // 2 // bands
    lats = rows * bands
    x = jnp.einsum("lnc,nx->xlc", normed, lon_fwd, preferred_element_type=f32).astype(bf16)
    x = lax.all_to_all(
        x.reshape(bands, waves, 2, rows, width), "band", split_axis=0, concat_axis=0, tiled=True
    )
    x = x.transpose(1, 2, 0, 3, 4).reshape(waves, 2 * lats, width)
    z = mix_modes(x, lat_fwd, lat_back, weights, biases)
    z = z.reshape(waves, 2, bands, rows, width).transpose(2, 0, 1, 3, 4)
    z = lax.all_to_all(z, "band", split_axis=0, concat_axis=0, tiled=True)
    z = z.reshape(bands * waves * 2, rows, width)
    return jnp.einsum("xlc,nx->lnc", z, lon_back, preferred_element_type=f32)


def with_halo(cells, sides, width, closed):
    for axis, dim in sides:
        count = lax.axis_size(axis)
        ends = count if closed else count - 1
        head = lax.slice_in_dim(cells, 0, width, axis=dim)
        tail = lax.slice_in_dim(cells, cells.shape[dim] - width, cells.shape[dim], axis=dim)
        cells = jnp.concatenate(
            [
                lax.ppermute(tail, axis, [(i, (i + 1) % count) for i in range(ends)]),
                cells,
                lax.ppermute(head, axis, [((i + 1) % count, i) for i in range(ends)]),
            ],
            axis=dim,
        )
    return cells


def on_device(
    atmosphere,
    spec_weight,
    spec_bias,
    norm_gain,
    norm_shift,
    fc_in,
    fc_out,
    flux_head,
    flux_embed,
    ocean_state,
    sea_mask,
    depth_kernel,
    ocean_gain,
    ocean_shift,
    ocean_in,
    ocean_out,
    layer_scale,
    field_head,
    patch_embed,
):
    column_index = lax.axis_index(quarter)
    slots = lax.axis_size(quarter)
    bands = lax.axis_size("band")
    rows, longitudes, slot = atmosphere.shape
    width_full = slot * slots
    part = longitudes // slots
    lon_fwd, lon_back = lon_matrices(longitudes, bands)
    lat_fwd, lat_back = lat_matrices(rows * bands)
    weights = dense_groups(spec_weight)
    biases = spec_bias[:, :, :, None, :]
    heads = lax.all_gather(flux_head, quarter, axis=0, tiled=True)
    embed = lax.all_gather(patch_embed, quarter, axis=1, tiled=True)
    gain = lambda b, i: norm_gain[b, i][None]
    shift = lambda b, i: norm_shift[b, i][None]

    values = atmosphere.astype(f32)
    sums = jnp.stack([jnp.sum(values, axis=-1), jnp.sum(values * values, axis=-1)])
    sums = shift_sum(sums, ("tile", "comp")) / width_full
    average = sums[0][..., None]
    variance = sums[1][..., None] - average * average
    scaling = lax.dynamic_slice_in_dim(norm_gain[0, 0], column_index * slot, slot)
    offset = lax.dynamic_slice_in_dim(norm_shift[0, 0], column_index * slot, slot)
    normed = (values - average) * lax.rsqrt(variance + eps_norm) * scaling + offset
    restored = spectral_filter(
        normed.astype(bf16), lon_fwd, lon_back, lat_fwd, lat_back, weights[0], biases[0]
    )
    u = (values + restored + normed).astype(bf16)
    u = u.reshape(rows, slots, part, slot).transpose(1, 0, 2, 3)
    u = lax.all_to_all(u, quarter, split_axis=0, concat_axis=0, tiled=True)
    w_in, w_out = gathered_pairs(fc_in[0], fc_out[0], ("comp", "tile"))
    after_one, fluxes = first_mlp(
        u.reshape(slots, rows * part, slot), gain(0, 1), shift(0, 1), heads, w_in, w_out
    )

    upsampled = jnp.repeat(jnp.repeat(fluxes.reshape(rows, part, -1), 2, axis=0), 2, axis=1)
    sea_cells = sea_mask.astype(f32)[..., None]
    forcing = jnp.einsum("ijf,fc->ijc", upsampled, flux_embed, precision=full_precision)
    start = (ocean_state.astype(f32) + sea_cells * forcing).astype(bf16)
    widened = with_halo(start, ((quarter, 1),), 3, True)
    extended = with_halo(widened, (("band", 0),), 3, False).astype(f32)
    tile_rows = start.shape[0]
    tile_columns = start.shape[1]
    convolved = jnp.zeros(start.shape, f32)
    for row_step in range(7):
        for col_step in range(7):
            convolved = (
                convolved
                + extended[row_step : row_step + tile_rows, col_step : col_step + tile_columns]
                * depth_kernel[row_step, col_step]
            )
    normed = layer_norm(convolved, ocean_gain, ocean_shift).astype(bf16)
    cells = tile_rows * tile_columns
    ocean_next, surface = ocean_mlp(
        normed.reshape(cells, -1),
        start.reshape(cells, -1),
        sea_cells.reshape(cells, 1),
        ocean_in,
        ocean_out,
        layer_scale,
        field_head,
    )
    ocean_next = ocean_next.reshape(start.shape)
    surface = surface.reshape(tile_rows, tile_columns, -1)

    patches = (
        surface.reshape(rows, 2, part, 2, surface.shape[2])
        .transpose(0, 2, 4, 1, 3)
        .reshape(rows * part, -1)
    )
    middle, normed = make_middle(
        after_one,
        product_left(patches),
        product_right(embed),
        gain(1, 0),
        shift(1, 0),
        slots,
    )
    normed = lax.all_to_all(normed, quarter, split_axis=0, concat_axis=0, tiled=True)
    normed = normed.reshape(slots, rows, part, slot).transpose(1, 0, 2, 3)
    restored = spectral_filter(
        normed.reshape(rows, longitudes, slot),
        lon_fwd,
        lon_back,
        lat_fwd,
        lat_back,
        weights[1],
        biases[1],
    ).astype(bf16)
    restored = restored.reshape(rows, slots, part, slot).transpose(1, 0, 2, 3)
    restored = lax.all_to_all(restored, quarter, split_axis=0, concat_axis=0, tiled=True)
    w_in, w_out = gathered_pairs(fc_in[1], fc_out[1], ("comp", "tile"))
    out = second_mlp(
        middle,
        restored.reshape(slots, rows * part, slot),
        gain(1, 0),
        shift(1, 0),
        gain(1, 1),
        shift(1, 1),
        w_in,
        w_out,
    )
    out = lax.all_to_all(out, quarter, split_axis=0, concat_axis=0, tiled=True)
    out = out.reshape(slots, rows, part, slot).transpose(1, 0, 2, 3)
    return (out.reshape(rows, longitudes, slot), ocean_next, surface)


def solution(mesh):
    placed = (
        P("band", None, ("comp", "tile")),
        P(None, None, None, ("comp", "tile"), None),
        P(None, None, None, ("comp", "tile")),
        P(),
        P(),
        P(None, None, ("comp", "tile")),
        P(None, ("comp", "tile"), None),
        P(("comp", "tile"), None),
        P(),
        P("band", ("comp", "tile"), None),
        P("band", ("comp", "tile")),
        P(),
        P(),
        P(),
        P(),
        P(),
        P(),
        P(),
        P(None, ("comp", "tile")),
    )
    return jax.shard_map(
        on_device,
        mesh=mesh,
        in_specs=placed,
        out_specs=(
            P("band", None, ("comp", "tile")),
            P("band", ("comp", "tile"), None),
            P("band", ("comp", "tile"), None),
        ),
        check_vma=False,
    )
```

time: 2250 us -> 1210 us (0.54)
  matrix products: 644 us -> 27.7 us
  waiting for transfers between devices: 918 us -> 427 us
  Pallas kernels: 0 us -> 167 us
  local copies, waits for them, and re-layouts: 305 us -> 161 us
  blocking collectives: 137 us -> 271 us
  other arithmetic: 159 us -> 102 us
    all_to_all x10 -> x5, waiting for transfers between devices: 825 us -> 233 us  [the longest x1 99.6 us: spectral_filter(): lax.all_to_all(x.reshape(bands, waves, 2, rows, width), 'band', split_axi...]
    dot_general x37 -> x2, matrix products: 530 us -> 10.9 us  [spectral_filter(): return jnp.einsum('xlc,nx->lnc', z, lon_back, preferred_element_type=f32)]
    ppermute x0 -> x14, waiting for transfers between devices: none -> 180 us  [the longest x12 177 us: gathered(): lax.ppermute(part, axis, [(i, (i + d) % n) for i in range(n)])]
    pallas_call x0 -> x6, Pallas kernels: none -> 167 us  [the longest x1 42 us: second_mlp(): pl.pallas_call(functools.partial(second_mlp_kernel, n), grid=(tokens // t...]
    all_to_all x2 -> x3, blocking collectives: 115 us -> 260 us  [the longest x1 108 us: spectral_filter(): lax.all_to_all(x.reshape(bands, waves, 2, rows, width), 'band', split_axi...]
    all_to_all x20 -> x0, local copies, waits for them, and re-layouts: 125 us -> none  [the longest x4 28 us: channel_mlp(): lax.all_to_all(result, ('comp', 'tile'), split_axis=2, concat_axis=1, til...]
    unnamed x12 -> x2, matrix products: 103 us -> 5.68 us
    reshape x5 -> x15, local copies, waits for them, and re-layouts: 14.1 us -> 90.3 us  [the longest x2 19.4 us: on_device(): u = u.reshape(rows, slots, part, slot).transpose(1, 0, 2, 3)]
  transfers between devices with their start and end apart: 21 -> 23, of which waited for: 15 -> 12; matrix products, arithmetic and copies ran while one was open for 23% -> 5% of each run, Pallas kernels for 0% -> 0%
where the time goes in v1:
time: 1210 us; the launch traced here: 1200 us
  waiting for transfers between devices  427 us (35%)
  blocking collectives  271 us (22%)
  Pallas kernels  167 us (14%)
  local copies, waits for them, and re-layouts  161 us (13%)
  other arithmetic  102 us (8%)
  starting transfers between devices  42.8 us (4%)
  matrix products  27.7 us (2%)
    ppermute x12, waiting for transfers between devices, gathered(): lax.ppermute(part, axis, [(i, (i + d) % n) for i in range(n)])  177 us
    all_to_all x1, blocking collectives, spectral_filter(): lax.all_to_all(x.reshape(bands, waves, 2, rows, width), 'band', split_axi...  108 us
    all_to_all x1, blocking collectives, spectral_filter(): z = lax.all_to_all(z, 'band', split_axis=0, concat_axis=0, tiled=True)  107 us
    all_to_all x1, waiting for transfers between devices, spectral_filter(): lax.all_to_all(x.reshape(bands, waves, 2, rows, width), 'band', split_axi...  99.6 us
    all_to_all x1, waiting for transfers between devices, spectral_filter(): z = lax.all_to_all(z, 'band', split_axis=0, concat_axis=0, tiled=True)  96.8 us
    reduce_sum x1, other arithmetic, layer_norm(): average = jnp.mean(values, axis=-1, keepdims=True)  71.2 us
    all_to_all x1, blocking collectives, on_device(): lax.all_to_all(normed, quarter, split_axis=0, concat_axis=0, tiled=True)  44.7 us
    pallas_call x1, Pallas kernels, second_mlp(): pl.pallas_call(functools.partial(second_mlp_kernel, n), grid=(tokens // t...  42 us
  transfers between devices with their start and end apart: 23, of which 12 were waited for; matrix products, arithmetic and copies ran while one was open for 5% of the time, Pallas kernels for 0%

profile of v1, /device:TPU:0, one launch (start us, length us, event | category | flops | bytes accessed | tf_op | source)
XLA Modules:
  0.0 1200.4 jit_solution(1384654556516427566)
XLA Ops:
  20.9 4.7 copy.95
  25.6 6.8 all-to-all-start
  37.1 99.6 %all-to-all-done = bf16[8,24,2,24,192]{4,3,2,1,0:T(8,128)(2,1)} async-done(((bf16[8,24,2,24,192]{4,3,2,1,0:T(8,128)(2,1)}), bf16[8,24,2,24,192]{4,3,2,1,0:T(8,128)(2,1)}, u32[]{:S(2)}, u32[]{:S(2)}) %all-to-all-start) | async-done | bytes 3538976 | tf_op jit(solution)/shard_map/all_to_all | solution.py:371
  136.7 5.1 copy.96
  141.9 20.9 %shard_map.202 = bf16[24,384,192]{2,1,0:T(8,128)(2,1)} custom-call(bf16[24,384,192]{2,1,0:T(8,128)(2,1)} %bitcast.209, bf16[384,384]{1,0:T(8,128)(2,1)} %get-tuple-element.43.fwd, bf16[384,384]{1,0:T(8,128)(2,1)} %get-tuple-element.42.back, bf16[2,2,192,192]{3,2,1,0:T(8,128)(2,1)} %get-tuple-element.41.weights, f32[2,2,1,192]{3,2,1,0:T(1,128)} %get-tuple-element.123.biases), custom_call_target="tpu_custom_call" | custom-call | flops 5435817984 | bytes 7077888 | tf_op jit(solution)/shard_map/pallas_call | solution.py:249
  162.8 7.2 copy.134
  169.9 5.1 all-to-all-start.1
  181.9 96.8 %all-to-all-done.1 = bf16[8,24,2,24,192]{4,1,2,3,0:T(8,128)(2,1)} async-done(((bf16[8,24,2,24,192]{4,1,2,3,0:T(8,128)(2,1)}), bf16[8,24,2,24,192]{4,1,2,3,0:T(8,128)(2,1)}, u32[]{:S(2)}, u32[]{:S(2)}) %all-to-all-start.1) | async-done | bytes 3538976 | tf_op jit(solution)/shard_map/all_to_all | solution.py:377
  278.7 8.2 fusion.54
  286.9 9.6 reshape.244
  296.5 9.8 copy.99
  306.3 5.1 all-to-all-start.2
  315.1 75.5 %collective-permute-done.5.refs_5_ = bf16[768,768]{1,0:T(8,128)(2,1)} collective-permute-done((bf16[768,768]{1,0:T(8,128)(2,1)S(1)}, bf16[768,768]{1,0:T(8,128)(2,1)}, u32[]{:S(2)}, u32[]{:S(2)}) %collective-permute-start.5) | collective-permute-done | bytes 1179680 | tf_op jit(solution)/shard_map/ppermute | solution.py:91
  390.6 5.2 all-gather
  397.3 5.7 reshape_broadcast_in_dim.4.mask_ref
  403.1 5.7 all-gather.1
  410.9 40.1 %shard_map.203 = (bf16[2304,768]{1,0:T(8,128)(2,1)}, f32[2304,8]{1,0:T(8,128)}) custom-call(bf16[4,2304,192]{2,1,0:T(8,128)(2,1)} %bitcast.22.u_ref, f32[1,768]{1,0:T(1,128)} %get-tuple-element.104.gain, f32[1,768]{1,0:T(1,128)} %get-tuple-element.100.shift, bf16[768,8]{1,0:T(8,128)(2,1)} %bitcast.222, bf16[768,768]{1,0:T(8,128)(2,1)} %get-tuple-element.39.refs_0_, ...), custom_call_target="tpu_custom_call" | custom-call | flops 21743271936 | bytes 16515072 | tf_op jit(solution)/shard_map/pallas_call | solution.py:124
  453.3 11.1 add_convert_fusion.1
  474.6 5.0 collective-permute-start.10
  484.5 6.5 collective-permute-done.10
  491.0 6.3 maximum_convert_fusion
  497.3 71.2 %fusion.84 = (f32[48,192]{1,0:T(8,128)S(1)}, f32[48,192]{1,0:T(8,128)S(1)}, f32[48,192,256]{2,1,0:T(8,128)}) fusion(f32[256]{0:T(256)S(1)} %bitcast.238, f32[54,198,256]{2,1,0:T(8,128)S(1)} %maximum_convert_fusion, f32[256]{0:T(256)S(1)} %bitcast.239, f32[256]{0:T(256)S(1)} %bitcast.241, f32[256]{0:T(256)S(1)} %bitcast.242, f32[256]{0:T(256)S(1)} %bitcast.243, ...), kind=kLoop, calls=%fused_computation.207 | loop fusion | flops 235911168 | bytes 471983104 | tf_op jit(solution)/shard_map/reduce_sum | solution.py:51
  568.5 7.4 add_convert_fusion
  575.8 34.6 %shard_map.204 = (bf16[9216,256]{1,0:T(8,128)(2,1)}, f32[9216,4]{1,0:T(8,128)}) custom-call(bf16[9216,256]{1,0:T(8,128)(2,1)} %bitcast.211, bf16[9216,256]{1,0:T(8,128)(2,1)} %bitcast.191, f32[9216,1]{1,0:T(8,128)} %reshape_broadcast_in_dim.4.mask_ref, bf16[256,1024]{1,0:T(8,128)(2,1)} %w_in.1, bf16[1024,256]{1,0:T(8,128)(2,1)} %w_out.1, ...), custom_call_target="tpu_custom_call" | custom-call | flops 9663676416 | bytes 18874368 | tf_op jit(solution)/shard_map/pallas_call | solution.py:295
  610.4 4.6 copy.106
  616.3 8.2 shard_map.205
  624.5 4.6 copy.109
  629.2 44.7 %all_to_all.40 = bf16[4,2304,192]{1,2,0:T(8,128)(2,1)} all-to-all(bf16[4,2304,192]{1,2,0:T(8,128)(2,1)S(1)} %copy.109), channel_id=1, replica_groups=mesh['band'=8,'comp'=2,'tile'=2] {'comp','tile'}, dimensions={0} | all-to-all | bytes 7077888 | tf_op jit(solution)/shard_map/all_to_all | solution.py:497
  673.8 10.0 reshape.252
  683.8 8.2 copy.133
  692.0 6.9 reshape.253
  702.8 4.9 copy.112
  707.7 108.4 %all_to_all.41 = bf16[8,24,2,24,192]{4,3,2,1,0:T(8,128)(2,1)S(1)} all-to-all(bf16[8,24,2,24,192]{4,3,2,1,0:T(8,128)(2,1)} %bitcast.203), channel_id=1, replica_groups=mesh['band'=8,'comp'=2,'tile'=2] {'band'}, dimensions={0} | all-to-all | bytes 7077888 | tf_op jit(solution)/shard_map/all_to_all | solution.py:371
  818.8 20.9 %shard_map.206 = bf16[24,384,192]{2,1,0:T(8,128)(2,1)} custom-call(bf16[24,384,192]{2,1,0:T(8,128)(2,1)} %bitcast.207, bf16[384,384]{1,0:T(8,128)(2,1)} %get-tuple-element.43.fwd, bf16[384,384]{1,0:T(8,128)(2,1)} %get-tuple-element.42.back, bf16[2,2,192,192]{3,2,1,0:T(8,128)(2,1)} %get-tuple-element.40.weights, f32[2,2,1,192]{3,2,1,0:T(1,128)} %get-tuple-element.122.biases), custom_call_target="tpu_custom_call" | custom-call | flops 5435817984 | bytes 7077888 | tf_op jit(solution)/shard_map/pallas_call | solution.py:249
  839.7 5.0 copy.132
  844.8 107.0 %all_to_all.42 = bf16[8,24,2,24,192]{4,1,2,3,0:T(8,128)(2,1)S(1)} all-to-all(bf16[8,24,2,24,192]{4,1,2,3,0:T(8,128)(2,1)S(1)} %bitcast.200), channel_id=1, replica_groups=mesh['band'=8,'comp'=2,'tile'=2] {'band'}, dimensions={0} | all-to-all | bytes 7077888 | tf_op jit(solution)/shard_map/all_to_all | solution.py:377
  954.5 5.1 reshape.257
  959.6 9.8 copy.116
  969.5 5.2 all-to-all-start.6
  977.3 76.8 %collective-permute-done.12.refs_1_ = bf16[768,768]{1,0:T(8,128)(2,1)S(1)} collective-permute-done((bf16[768,768]{1,0:T(8,128)(2,1)S(1)}, bf16[768,768]{1,0:T(8,128)(2,1)S(1)}, u32[]{:S(2)}, u32[]{:S(2)}) %collective-permute-start.12) | collective-permute-done | bytes 1179680 | tf_op jit(solution)/shard_map/ppermute | solution.py:91
  1054.2 24.8 %collective-permute-done.15.refs_5_ = bf16[768,768]{1,0:T(8,128)(2,1)S(1)} collective-permute-done((bf16[768,768]{1,0:T(8,128)(2,1)S(1)}, bf16[768,768]{1,0:T(8,128)(2,1)S(1)}, u32[]{:S(2)}, u32[]{:S(2)}) %collective-permute-start.15) | collective-permute-done | bytes 1179680 | tf_op jit(solution)/shard_map/ppermute | solution.py:91
  1081.9 42.0 %shard_map.207 = bf16[4,2304,192]{2,1,0:T(8,128)(2,1)} custom-call(bf16[2304,768]{1,0:T(8,128)(2,1)} %get-tuple-element.12.v_ref, bf16[4,2304,192]{2,1,0:T(8,128)(2,1)} %bitcast.108.r_ref, f32[1,768]{1,0:T(1,128)} %get-tuple-element.106.gain.gain0, f32[1,768]{1,0:T(1,128)} %get-tuple-element.102.shift.shift0, f32[1,768]{1,0:T(1,128)} %get-tuple-element.103.gain, ...), custom_call_target="tpu_custom_call" | custom-call | flops 21743271936 | bytes 20054016 | tf_op jit(solution)/shard_map/pallas_call | solution.py:169
  1124.0 6.3 copy.117
  1134.3 4.1 copy.119
  1138.5 37.0 %all-to-all-done.7 = bf16[4,2304,192]{1,2,0:T(8,128)(2,1)S(1)} async-done(((bf16[4,2304,192]{1,2,0:T(8,128)(2,1)}), bf16[4,2304,192]{1,2,0:T(8,128)(2,1)S(1)}, u32[]{:S(2)}, u32[]{:S(2)}) %all-to-all-start.7) | async-done | bytes 3538976 | tf_op jit(solution)/shard_map/all_to_all | solution.py:521
  1175.4 8.1 reshape.259
  1183.5 8.2 copy.118
  1191.7 8.2 reshape.260
  (143 shorter events, 76.6 us)
Async XLA Ops:
  0.6 452.7 %copy-start = (f32[8,256]{1,0:T(8,128)S(1)}, f32[8,256]{1,0:T(8,128)}, u32[]{:S(2)}) copy-start(f32[8,256]{1,0:T(8,128)} %param.27) | copy-start | bytes 24580
  3.7 5.1 collective-permute-start
  8.8 11.5 copy-start.4
  8.8 5.5 collective-permute-start.1
  11.5 8.8 copy-start.15
  14.4 5.9 copy-start.12
  14.4 5.9 copy-start.13
  25.6 9.5 copy-start.14
  25.6 10.2 copy-start.9
  25.6 111.1 %all-to-all-start = ((bf16[8,24,2,24,192]{4,3,2,1,0:T(8,128)(2,1)}), bf16[8,24,2,24,192]{4,3,2,1,0:T(8,128)(2,1)}, u32[]{:S(2)}, u32[]{:S(2)}) async-start(bf16[8,24,2,24,192]{4,3,2,1,0:T(8,128)(2,1)} %bitcast.201), calls=%async_computation | async-start | bytes 9437184 | tf_op jit(solution)/shard_map/all_to_all | solution.py:371
  169.9 108.8 %copy-start.3 = (bf16[24,384,192]{1,2,0:T(8,128)(2,1)S(1)}, bf16[24,384,192]{1,2,0:T(8,128)(2,1)}, u32[]{:S(2)}) copy-start(bf16[24,384,192]{1,2,0:T(8,128)(2,1)} %param.19) | copy-start | bytes 10616836
  169.9 108.8 %all-to-all-start.1 = ((bf16[8,24,2,24,192]{4,1,2,3,0:T(8,128)(2,1)}), bf16[8,24,2,24,192]{4,1,2,3,0:T(8,128)(2,1)}, u32[]{:S(2)}, u32[]{:S(2)}) async-start(bf16[8,24,2,24,192]{4,1,2,3,0:T(8,128)(2,1)} %bitcast.198), calls=%async_computation.1 | async-start | bytes 9437184 | tf_op jit(solution)/shard_map/all_to_all | solution.py:377
  178.3 136.8 %collective-permute-start.2 = (bf16[768,768]{1,0:T(8,128)(2,1)}, bf16[768,768]{1,0:T(8,128)(2,1)}, u32[]{:S(2)}, u32[]{:S(2)}) collective-permute-start(bf16[768,768]{1,0:T(8,128)(2,1)} %get-tuple-element.39.refs_0_), channel_id=1, source_target_pairs={{0,2},{2,0},{1,3},{3,1},{4,6},{6,4},{5,7},{7,5},{8,10},{10,8},{9,1... | collective-permute-start | bytes 3538952 | tf_op jit(solution)/shard_map/ppermute | solution.py:91
  296.5 14.9 %copy-start.5 = (bf16[2,768,768]{2,1,0:T(8,128)(2,1)S(1)}, bf16[2,768,768]{2,1,0:T(8,128)(2,1)}, u32[]{:S(2)}) copy-start(bf16[2,768,768]{2,1,0:T(8,128)(2,1)} %param.25) | copy-start | bytes 7077892
  306.3 84.2 %copy-start.16 = (bf16[192,8]{0,1:T(8,128)(2,1)S(1)}, bf16[192,8]{0,1:T(8,128)(2,1)}, u32[]{:S(2)}) copy-start(bf16[192,8]{0,1:T(8,128)(2,1)} %param.26) | copy-start | bytes 9220
  306.3 102.5 %copy-start.17 = (f32[256,4]{0,1:T(4,128)S(1)}, f32[256,4]{0,1:T(4,128)}, u32[]{:S(2)}) copy-start(f32[256,4]{0,1:T(4,128)} %param.36) | copy-start | bytes 12292
  306.3 104.5 %all-to-all-start.2 = ((bf16[4,24,96,192]{3,2,1,0:T(8,128)(2,1)}), bf16[4,24,96,192]{3,2,1,0:T(8,128)(2,1)}, u32[]{:S(2)}, u32[]{:S(2)}) async-start(bf16[4,24,96,192]{3,2,1,0:T(8,128)(2,1)} %bitcast.196), calls=%async_computation.2 | async-start | bytes 9437184 | tf_op jit(solution)/shard_map/all_to_all | solution.py:448
  312.6 98.2 %copy-start.8 = (bf16[768,768]{1,0:T(8,128)(2,1)}, bf16[768,768]{1,0:T(8,128)(2,1)S(1)}, u32[]{:S(2)}) copy-start(bf16[768,768]{1,0:T(8,128)(2,1)S(1)} %get-tuple-element.37.refs_4_) | copy-start | bytes 3538948
  312.6 77.9 %collective-permute-start.5 = (bf16[768,768]{1,0:T(8,128)(2,1)S(1)}, bf16[768,768]{1,0:T(8,128)(2,1)}, u32[]{:S(2)}, u32[]{:S(2)}) collective-permute-start(bf16[768,768]{1,0:T(8,128)(2,1)S(1)} %get-tuple-element.37.refs_4_), channel_id=1, source_target_pairs={{0,2},{2,0},{1,3},{3,1},{4,6},{6,4},{5,7},{7,5},{8,10},{10,8},{9,1... | collective-permute-start | bytes 3538952 | tf_op jit(solution)/shard_map/ppermute | solution.py:91
  314.6 96.2 %collective-permute-start.3 = (bf16[768,768]{1,0:T(8,128)(2,1)}, bf16[768,768]{1,0:T(8,128)(2,1)}, u32[]{:S(2)}, u32[]{:S(2)}) collective-permute-start(bf16[768,768]{1,0:T(8,128)(2,1)} %get-tuple-element.39.refs_0_), channel_id=1, source_target_pairs={{0,1},{1,0},{2,3},{3,2},{4,5},{5,4},{6,7},{7,6},{8,9},{9,8},{10,11... | collective-permute-start | bytes 3538952 | tf_op jit(solution)/shard_map/ppermute | solution.py:91
  314.6 96.2 %collective-permute-start.6 = (bf16[768,768]{1,0:T(8,128)(2,1)S(1)}, bf16[768,768]{1,0:T(8,128)(2,1)}, u32[]{:S(2)}, u32[]{:S(2)}) collective-permute-start(bf16[768,768]{1,0:T(8,128)(2,1)S(1)} %get-tuple-element.37.refs_4_), channel_id=1, source_target_pairs={{0,1},{1,0},{2,3},{3,2},{4,5},{5,4},{6,7},{7,6},{8,9},{9,8},{10,11... | collective-permute-start | bytes 3538952 | tf_op jit(solution)/shard_map/ppermute | solution.py:91
  315.1 95.7 %collective-permute-start.4 = (bf16[768,768]{1,0:T(8,128)(2,1)}, bf16[768,768]{1,0:T(8,128)(2,1)}, u32[]{:S(2)}, u32[]{:S(2)}) collective-permute-start(bf16[768,768]{1,0:T(8,128)(2,1)} %collective-permute-done.2.refs_1_), channel_id=1, source_target_pairs={{0,1},{1,0},{2,3},{3,2},{4,5},{5,4},{6,7},{7,6},{8,9},{9,8},{10,11... | collective-permute-start | bytes 3538952 | tf_op jit(solution)/shard_map/ppermute | solution.py:91
  390.6 20.3 %collective-permute-start.7 = (bf16[768,768]{1,0:T(8,128)(2,1)}, bf16[768,768]{1,0:T(8,128)(2,1)}, u32[]{:S(2)}, u32[]{:S(2)}) collective-permute-start(bf16[768,768]{1,0:T(8,128)(2,1)} %collective-permute-done.5.refs_5_), channel_id=1, source_target_pairs={{0,1},{1,0},{2,3},{3,2},{4,5},{5,4},{6,7},{7,6},{8,9},{9,8},{10,11... | collective-permute-start | bytes 3538952 | tf_op jit(solution)/shard_map/ppermute | solution.py:91
  464.5 2.1 copy-start.2
  466.7 2.7 collective-permute-start.9
  467.1 5.0 collective-permute-start.8
  473.3 11.2 collective-permute-start.11
  474.6 16.3 %collective-permute-start.10 = (bf16[3,198,256]{2,1,0:T(8,128)(2,1)S(1)}, bf16[3,198,256]{2,1,0:T(8,128)(2,1)S(1)}, u32[]{:S(2)}, u32[]{:S(2)}) collective-permute-start(bf16[3,198,256]{2,1,0:T(8,128)(2,1)S(1)} %get-tuple-element.32), channel_id=1, source_target_pairs={{0,4},{4,8},{8,12},{12,16},{16,20},{20,24},{24,28},{1,5},{5,9},{9,... | collective-permute-start | bytes 912392 | tf_op jit(solution)/shard_map/ppermute | solution.py:390
  497.3 71.2 %copy-start.18 = (f32[256]{0:T(256)S(1)}, f32[256]{0:T(256)}, u32[]{:S(2)}) copy-start(f32[256]{0:T(256)} %param.32) | copy-start | bytes 3076
  497.3 71.2 %copy-start.19 = (f32[256]{0:T(256)S(1)}, f32[256]{0:T(256)}, u32[]{:S(2)}) copy-start(f32[256]{0:T(256)} %param.31) | copy-start | bytes 3076
  839.7 112.1 %copy-start.10 = (bf16[384,8,24,1]{0,2,3,1:T(8,128)(2,1)S(1)}, bf16[384,8,24,1]{0,2,3,1:T(8,128)(2,1)}, u32[]{:S(2)}) copy-start(bf16[384,8,24,1]{0,2,3,1:T(8,128)(2,1)} %get-tuple-element.112) | copy-start | bytes 442372
  839.7 112.1 %copy-start.11 = (bf16[384,8,24,1]{0,2,3,1:T(8,128)(2,1)S(1)}, bf16[384,8,24,1]{0,2,3,1:T(8,128)(2,1)}, u32[]{:S(2)}) copy-start(bf16[384,8,24,1]{0,2,3,1:T(8,128)(2,1)} %get-tuple-element.113) | copy-start | bytes 442372
  959.6 15.1 %copy-start.6 = (bf16[768,768]{1,0:T(8,128)(2,1)S(1)}, bf16[768,768]{1,0:T(8,128)(2,1)}, u32[]{:S(2)}) copy-start(bf16[768,768]{1,0:T(8,128)(2,1)} %get-tuple-element.38.refs_0_) | copy-start | bytes 3538948
  959.6 17.1 %copy-start.7 = (bf16[768,768]{1,0:T(8,128)(2,1)S(1)}, bf16[768,768]{1,0:T(8,128)(2,1)}, u32[]{:S(2)}) copy-start(bf16[768,768]{1,0:T(8,128)(2,1)} %get-tuple-element.36.refs_4_) | copy-start | bytes 3538948
  969.5 112.5 %all-to-all-start.6 = ((bf16[4,24,96,192]{3,2,1,0:T(8,128)(2,1)}), bf16[4,24,96,192]{3,2,1,0:T(8,128)(2,1)}, u32[]{:S(2)}, u32[]{:S(2)}) async-start(bf16[4,24,96,192]{3,2,1,0:T(8,128)(2,1)} %bitcast.197), calls=%async_computation.6 | async-start | bytes 9437184 | tf_op jit(solution)/shard_map/all_to_all | solution.py:509
  974.7 79.5 %collective-permute-start.12 = (bf16[768,768]{1,0:T(8,128)(2,1)S(1)}, bf16[768,768]{1,0:T(8,128)(2,1)S(1)}, u32[]{:S(2)}, u32[]{:S(2)}) collective-permute-start(bf16[768,768]{1,0:T(8,128)(2,1)S(1)} %copy-done.6), channel_id=1, source_target_pairs={{0,2},{2,0},{1,3},{3,1},{4,6},{6,4},{5,7},{7,5},{8,10},{10,8},{9,1... | collective-permute-start | bytes 3538952 | tf_op jit(solution)/shard_map/ppermute | solution.py:91
  976.7 102.2 %collective-permute-start.15 = (bf16[768,768]{1,0:T(8,128)(2,1)S(1)}, bf16[768,768]{1,0:T(8,128)(2,1)S(1)}, u32[]{:S(2)}, u32[]{:S(2)}) collective-permute-start(bf16[768,768]{1,0:T(8,128)(2,1)S(1)} %copy-done.7), channel_id=1, source_target_pairs={{0,2},{2,0},{1,3},{3,1},{4,6},{6,4},{5,7},{7,5},{8,10},{10,8},{9,1... | collective-permute-start | bytes 3538952 | tf_op jit(solution)/shard_map/ppermute | solution.py:91
  976.8 102.1 %collective-permute-start.13 = (bf16[768,768]{1,0:T(8,128)(2,1)S(1)}, bf16[768,768]{1,0:T(8,128)(2,1)S(1)}, u32[]{:S(2)}, u32[]{:S(2)}) collective-permute-start(bf16[768,768]{1,0:T(8,128)(2,1)S(1)} %copy-done.6), channel_id=1, source_target_pairs={{0,1},{1,0},{2,3},{3,2},{4,5},{5,4},{6,7},{7,6},{8,9},{9,8},{10,11... | collective-permute-start | bytes 3538952 | tf_op jit(solution)/shard_map/ppermute | solution.py:91
  976.8 102.2 %collective-permute-start.16 = (bf16[768,768]{1,0:T(8,128)(2,1)S(1)}, bf16[768,768]{1,0:T(8,128)(2,1)S(1)}, u32[]{:S(2)}, u32[]{:S(2)}) collective-permute-start(bf16[768,768]{1,0:T(8,128)(2,1)S(1)} %copy-done.7), channel_id=1, source_target_pairs={{0,1},{1,0},{2,3},{3,2},{4,5},{5,4},{6,7},{7,6},{8,9},{9,8},{10,11... | collective-permute-start | bytes 3538952 | tf_op jit(solution)/shard_map/ppermute | solution.py:91
  1054.2 27.8 %copy-start.20 = (bf16[768,768]{1,0:T(8,128)(2,1)}, bf16[768,768]{1,0:T(8,128)(2,1)S(1)}, u32[]{:S(2)}) copy-start(bf16[768,768]{1,0:T(8,128)(2,1)S(1)} %collective-permute-done.12.refs_1_) | copy-start | bytes 3538948
  1054.2 24.8 %collective-permute-start.14 = (bf16[768,768]{1,0:T(8,128)(2,1)S(1)}, bf16[768,768]{1,0:T(8,128)(2,1)S(1)}, u32[]{:S(2)}, u32[]{:S(2)}) collective-permute-start(bf16[768,768]{1,0:T(8,128)(2,1)S(1)} %collective-permute-done.12.refs_1_), channel_id=1, source_target_pairs={{0,1},{1,0},{2,3},{3,2},{4,5},{5,4},{6,7},{7,6},{8,9},{9,8},{10,11... | collective-permute-start | bytes 3538952 | tf_op jit(solution)/shard_map/ppermute | solution.py:91
  1079.0 1.0 copy-start.21
  1079.0 3.0 collective-permute-start.17
  1079.0 1.4 copy-start.22
  1079.0 1.8 copy-start.23
  1080.8 1.0 copy-start.24
  1130.3 45.1 %all-to-all-start.7 = ((bf16[4,2304,192]{1,2,0:T(8,128)(2,1)}), bf16[4,2304,192]{1,2,0:T(8,128)(2,1)S(1)}, u32[]{:S(2)}, u32[]{:S(2)}) async-start(bf16[4,2304,192]{1,2,0:T(8,128)(2,1)} %copy.117), calls=%async_computation.7 | async-start | bytes 7077888 | tf_op jit(solution)/shard_map/all_to_all | solution.py:521
  1175.4 24.5 %copy-start.1 = (f32[8,256]{1,0:T(8,128)S(1)}, f32[8,256]{1,0:T(8,128)}, u32[]{:S(2)}) copy-start(f32[8,256]{1,0:T(8,128)} %param.27) | copy-start | bytes 24580

commit v2 on v1

--- a/solution.py
+++ b/solution.py
@@ -225,10 +225,21 @@
     return y - jnp.clip(y, -shrink_level, shrink_level)
 
 
-def modes_kernel(x_ref, fwd, back, weights, biases, z_ref):
-    lats = x_ref.shape[1] // 2
-    for k in range(x_ref.shape[0]):
-        s = dot(fwd[...], x_ref[k]).astype(bf16)
+def modes_kernel(halves, pair, x_refs, fwd, back, weights, biases, z_refs):
+    width = weights.shape[2]
+    waves = z_refs[0].shape[0]
+    for k in range(waves):
+        x = jnp.concatenate(
+            [
+                x_refs[h][2 * k + part, :, j * width : (j + 1) * width]
+                for part in range(2)
+                for h in range(halves)
+                for j in range(pair)
+            ],
+            axis=0,
+        )
+        lats = x.shape[0] // 2
+        s = dot(fwd[...], x).astype(bf16)
         for layer in range(2):
             s_re, s_im = s[:lats], s[lats:]
             y_re = dot(s_re, weights[layer, 0]) - dot(s_im, weights[layer, 1])
@@ -240,31 +251,189 @@
             else:
                 y_re, y_im = soft_shrink(y_re), soft_shrink(y_im)
             s = jnp.concatenate([y_re.astype(bf16), y_im.astype(bf16)], axis=0)
-        z_ref[k] = dot(back[...], s).astype(bf16)
-
-
-def mix_modes(x, fwd, back, weights, biases):
-    waves, rows, width = x.shape
+        z = dot(back[...], s)
+        rows = z.shape[0] // (halves * pair)
+        for h in range(halves):
+            cut = [z[(h * pair + j) * rows : (h * pair + j + 1) * rows] for j in range(pair)]
+            z_refs[h][k] = jnp.concatenate(cut, axis=-1).astype(bf16)
+
+
+def mix_modes(xs, fwd, back, weights, biases, pair, early):
+    halves = len(xs)
+    parts, rows, lanes = xs[0].shape
+    waves = parts // 2
+    lats = fwd.shape[0] // 2
+    width = lanes // pair
     step = 3 if waves % 3 == 0 else 1
+
+    def kernel(*refs):
+        x_refs, refs = refs[:halves], refs[halves:]
+        z_refs = refs[4 + len(early) :]
+        modes_kernel(halves, pair, x_refs, *refs[:4], z_refs)
+
     return pl.pallas_call(
-        modes_kernel,
+        kernel,
         grid=(waves // step,),
-        in_specs=[
-            pl.BlockSpec((step, rows, width), lambda i: (i, 0, 0)),
-            whole(fwd.shape),
-            whole(back.shape),
-            whole(weights.shape),
-            whole(biases.shape),
-        ],
-        out_specs=pl.BlockSpec((step, rows, width), lambda i: (i, 0, 0)),
-        out_shape=jax.ShapeDtypeStruct(x.shape, bf16),
+        in_specs=[pl.BlockSpec((2 * step, rows, lanes), lambda i: (i, 0, 0))] * halves
+        + [whole(fwd.shape), whole(back.shape), whole(weights.shape), whole(biases.shape)]
+        + [pl.BlockSpec(memory_space=pl.ANY)] * len(early),
+        out_specs=[pl.BlockSpec((step, 2 * rows, lanes), lambda i: (i, 0, 0))] * halves,
+        out_shape=[jax.ShapeDtypeStruct((waves, 2 * rows, lanes), bf16)] * halves,
         compiler_params=pltpu.CompilerParams(vmem_limit_bytes=vmem_bytes),
         cost_estimate=pl.CostEstimate(
-            flops=waves * 4 * (rows * rows * width + 2 * rows * width * width),
-            bytes_accessed=4 * waves * rows * width,
+            flops=waves * 16 * (lats * lats * width + lats * width * width),
+            bytes_accessed=8 * waves * lats * width,
             transcendentals=0,
         ),
-    )(x, fwd, back, weights, biases)
+    )(*xs, fwd, back, weights, biases, *early)
+
+
+def norm_with(values, stats, scaling, offset):
+    column = jnp.transpose(stats)
+    return (values - column[:, 0:1]) * column[:, 1:2] * scaling + offset
+
+
+def aligned(waves):
+    return 2 * waves % 16 == 0
+
+
+def spectrum_block(bands, waves, lanes):
+    if aligned(waves):
+        return pl.BlockSpec((bands, 1, 2 * waves, lanes), lambda i: (0, i, 0, 0))
+    return pl.BlockSpec((1, bands * 2 * waves, lanes), lambda i: (i, 0, 0))
+
+
+def lon_forward(source, matrix, bands, waves, pair, stats=None):
+    if stats is None:
+        _, rows, part, width = source.shape
+    else:
+        rows, longitudes, width = source.shape
+    lanes = pair * width
+
+    def kernel(*refs):
+        x_ref, f_ref, out_ref = refs[0], refs[1], refs[-1]
+        columns = []
+        for j in range(pair):
+            if stats is None:
+                columns.append(
+                    jnp.concatenate([x_ref[i, j] for i in range(x_ref.shape[0])], axis=0)
+                )
+            else:
+                st_ref, gain, shift = refs[2:5]
+                normed = norm_with(x_ref[j].astype(f32), st_ref[j], gain[...], shift[...])
+                columns.append(normed.astype(bf16))
+        y = dot(f_ref[...], jnp.concatenate(columns, axis=-1)).astype(bf16)
+        if aligned(waves):
+            out_ref[:, 0] = y.reshape(bands, 2 * waves, lanes)
+        else:
+            out_ref[0] = y
+
+    if stats is None:
+        args = (source, matrix)
+        specs = [
+            pl.BlockSpec((source.shape[0], pair, part, width), lambda i: (0, i, 0, 0)),
+            whole(matrix.shape),
+        ]
+    else:
+        st, gain, shift = stats
+        args = (source, matrix, st, gain, shift)
+        specs = [
+            pl.BlockSpec((pair, longitudes, width), lambda i: (i, 0, 0)),
+            whole(matrix.shape),
+            pl.BlockSpec((pair, st.shape[1], longitudes), lambda i: (i, 0, 0)),
+            whole(gain.shape),
+            whole(shift.shape),
+        ]
+    count = rows // pair
+    if aligned(waves):
+        shape = (bands, count, 2 * waves, lanes)
+    else:
+        shape = (count, bands * 2 * waves, lanes)
+    out = pl.pallas_call(
+        kernel,
+        grid=(count,),
+        in_specs=specs,
+        out_specs=spectrum_block(bands, waves, lanes),
+        out_shape=jax.ShapeDtypeStruct(shape, bf16),
+        compiler_params=pltpu.CompilerParams(vmem_limit_bytes=vmem_bytes),
+        cost_estimate=pl.CostEstimate(
+            flops=2 * rows * matrix.shape[0] * matrix.shape[1] * width,
+            bytes_accessed=4 * rows * matrix.shape[0] * width,
+            transcendentals=0,
+        ),
+    )(*args)
+    if not aligned(waves):
+        out = out.reshape(count, bands, 2 * waves, lanes).transpose(1, 0, 2, 3)
+    return out
+
+
+def lon_back_call(z, matrix, slots, pair, source=None, stats=None, early=()):
+    bands, count, parts, lanes = z.shape
+    waves = parts // 2
+    width = lanes // pair
+    longitudes = matrix.shape[0]
+    part = longitudes // slots
+    if not aligned(waves):
+        z = z.transpose(1, 0, 2, 3).reshape(count, bands * parts, lanes)
+
+    def kernel(*refs):
+        z_ref, g_ref, out_ref = refs[0], refs[1], refs[-1]
+        spectra = z_ref[:, 0].reshape(bands * parts, lanes) if aligned(waves) else z_ref[0]
+        r = dot(g_ref[...], spectra)
+        for j in range(pair):
+            u = r[:, j * width : (j + 1) * width]
+            if stats is not None:
+                v_ref, st_ref, gain, shift = refs[2:6]
+                v = v_ref[j].astype(f32)
+                u = v + u + norm_with(v, st_ref[j], gain[...], shift[...])
+            u = u.astype(bf16)
+            for i in range(slots):
+                out_ref[i, j] = u[i * part : (i + 1) * part]
+
+    args = [z, matrix]
+    specs = [spectrum_block(bands, waves, lanes), whole(matrix.shape)]
+    if stats is not None:
+        st, gain, shift = stats
+        args += [source, st, gain, shift]
+        specs += [
+            pl.BlockSpec((pair, longitudes, width), lambda i: (i, 0, 0)),
+            pl.BlockSpec((pair, st.shape[1], longitudes), lambda i: (i, 0, 0)),
+            whole(gain.shape),
+            whole(shift.shape),
+        ]
+    return pl.pallas_call(
+        kernel,
+        grid=(count,),
+        in_specs=specs + [pl.BlockSpec(memory_space=pl.ANY)] * len(early),
+        out_specs=pl.BlockSpec((slots, pair, part, width), lambda i: (0, i, 0, 0)),
+        out_shape=jax.ShapeDtypeStruct((slots, count * pair, part, width), bf16),
+        compiler_params=pltpu.CompilerParams(vmem_limit_bytes=vmem_bytes),
+        cost_estimate=pl.CostEstimate(
+            flops=2 * count * longitudes * bands * parts * lanes,
+            bytes_accessed=6 * count * longitudes * lanes,
+            transcendentals=0,
+        ),
+    )(*args, *early)
+
+
+def assemble_kernel(halves, *refs):
+    out_ref = refs[halves]
+    rows = refs[0].shape[1]
+    for h in range(halves):
+        out_ref[h * rows : (h + 1) * rows] = refs[h][0]
+
+
+def assemble(outs):
+    halves = len(outs)
+    slots, rows, part, width = outs[0].shape
+    return pl.pallas_call(
+        functools.partial(assemble_kernel, halves),
+        grid=(slots,),
+        in_specs=[pl.BlockSpec((1, rows, part, width), lambda i: (i, 0, 0, 0))] * halves,
+        out_specs=pl.BlockSpec((halves * rows, part, width), lambda i: (0, i, 0)),
+        out_shape=jax.ShapeDtypeStruct((halves * rows, slots * part, width), bf16),
+        compiler_params=pltpu.CompilerParams(vmem_limit_bytes=vmem_bytes),
+    )(*outs)
 
 
 def ocean_kernel(on_ref, start_ref, mask_ref, w_in, w_out, scale, head, next_ref, field_ref):
@@ -337,19 +506,28 @@
         both = jnp.concatenate([re.reshape(shape), im.reshape(shape)], axis=-1)
         return both.reshape(longitudes, -1).astype(bf16)
 
-    return laid(cos, -sin), laid(cos * weight, -sin * weight)
-
-
-def lat_matrices(lats):
-    angles = phases(lats, lats, lats)
+    return laid(cos, -sin).T, laid(cos * weight, -sin * weight)
+
+
+def lat_matrices(lats, bands, halves, pair):
+    order = jnp.arange(lats).reshape(bands, halves, lats // (bands * halves * pair), pair)
+    order = order.transpose(1, 3, 0, 2).reshape(halves * pair, -1)
+    turns = jnp.arange(lats)[:, None] * order.reshape(1, lats) % lats
+    angles = turns.astype(f32) * (2.0 * math.pi / lats)
     cos = jnp.cos(angles) / math.sqrt(lats)
     sin = jnp.sin(angles) / math.sqrt(lats)
     fwd = jnp.concatenate(
         [jnp.concatenate([cos, sin], axis=1), jnp.concatenate([-sin, cos], axis=1)], axis=0
     )
+    cos_t = cos.T.reshape(halves * pair, -1, lats)
+    sin_t = sin.T.reshape(halves * pair, -1, lats)
     back = jnp.concatenate(
-        [jnp.concatenate([cos, -sin], axis=1), jnp.concatenate([sin, cos], axis=1)], axis=0
-    )
+        [
+            jnp.concatenate([cos_t, -sin_t], axis=2),
+            jnp.concatenate([sin_t, cos_t], axis=2),
+        ],
+        axis=1,
+    ).reshape(2 * lats, 2 * lats)
     return fwd.astype(bf16), back.astype(bf16)
 
 
@@ -362,21 +540,21 @@
     return jnp.where(row == column, tiled, 0.0).astype(bf16)
 
 
-def spectral_filter(normed, lon_fwd, lon_back, lat_fwd, lat_back, weights, biases):
-    rows, longitudes, width = normed.shape
-    bands = lax.axis_size("band")
-    waves = longitudes // 2 // bands
-    lats = rows * bands
-    x = jnp.einsum("lnc,nx->xlc", normed, lon_fwd, preferred_element_type=f32).astype(bf16)
-    x = lax.all_to_all(
-        x.reshape(bands, waves, 2, rows, width), "band", split_axis=0, concat_axis=0, tiled=True
-    )
-    x = x.transpose(1, 2, 0, 3, 4).reshape(waves, 2 * lats, width)
-    z = mix_modes(x, lat_fwd, lat_back, weights, biases)
-    z = z.reshape(waves, 2, bands, rows, width).transpose(2, 0, 1, 3, 4)
-    z = lax.all_to_all(z, "band", split_axis=0, concat_axis=0, tiled=True)
-    z = z.reshape(bands * waves * 2, rows, width)
-    return jnp.einsum("xlc,nx->lnc", z, lon_back, preferred_element_type=f32)
+def to_band(x):
+    return lax.all_to_all(x, "band", split_axis=0, concat_axis=0, tiled=True)
+
+
+def to_quarter(x):
+    return lax.all_to_all(x, quarter, split_axis=0, concat_axis=0, tiled=True)
+
+
+def modes_of_bands(xs, fwd, back, weights, biases, pair, early):
+    bands, count, parts, lanes = xs[0].shape
+    xs = [to_band(x) for x in xs]
+    xs = [x.transpose(2, 0, 1, 3).reshape(parts, bands * count, lanes) for x in xs]
+    zs = mix_modes(xs, fwd, back, weights, biases, pair, early)
+    zs = [z.reshape(parts // 2, 2, bands, count, lanes).transpose(2, 3, 0, 1, 4) for z in zs]
+    return [z.reshape(bands, count, parts, lanes) for z in zs]
 
 
 def with_halo(cells, sides, width, closed):
@@ -423,104 +601,115 @@
     rows, longitudes, slot = atmosphere.shape
     width_full = slot * slots
     part = longitudes // slots
+    waves = longitudes // 2 // bands
+    halves = 2 if rows % 4 == 0 else 1
+    pair = 2 if rows % (2 * halves) == 0 else 1
+    half = rows // halves
     lon_fwd, lon_back = lon_matrices(longitudes, bands)
-    lat_fwd, lat_back = lat_matrices(rows * bands)
+    lat_fwd, lat_back = lat_matrices(rows * bands, bands, halves, pair)
     weights = dense_groups(spec_weight)
     biases = spec_bias[:, :, :, None, :]
     heads = lax.all_gather(flux_head, quarter, axis=0, tiled=True)
     embed = lax.all_gather(patch_embed, quarter, axis=1, tiled=True)
     gain = lambda b, i: norm_gain[b, i][None]
     shift = lambda b, i: norm_shift[b, i][None]
+    cut = lambda x, h: lax.slice_in_dim(x, h * half, (h + 1) * half)
+    in0, out0 = gathered_pairs(fc_in[0], fc_out[0], ("comp", "tile"))
+    in1, out1 = gathered_pairs(fc_in[1], fc_out[1], ("comp", "tile"))
 
     values = atmosphere.astype(f32)
     sums = jnp.stack([jnp.sum(values, axis=-1), jnp.sum(values * values, axis=-1)])
     sums = shift_sum(sums, ("tile", "comp")) / width_full
-    average = sums[0][..., None]
-    variance = sums[1][..., None] - average * average
-    scaling = lax.dynamic_slice_in_dim(norm_gain[0, 0], column_index * slot, slot)
-    offset = lax.dynamic_slice_in_dim(norm_shift[0, 0], column_index * slot, slot)
-    normed = (values - average) * lax.rsqrt(variance + eps_norm) * scaling + offset
-    restored = spectral_filter(
-        normed.astype(bf16), lon_fwd, lon_back, lat_fwd, lat_back, weights[0], biases[0]
+    rstd = lax.rsqrt(sums[1] - sums[0] * sums[0] + eps_norm)
+    stats = jnp.stack([sums[0], rstd] + [jnp.zeros_like(rstd)] * 6, axis=1)
+    scaling = lax.dynamic_slice_in_dim(norm_gain[0, 0], column_index * slot, slot)[None]
+    offset = lax.dynamic_slice_in_dim(norm_shift[0, 0], column_index * slot, slot)[None]
+    streams = [cut(atmosphere, h) for h in range(halves)]
+    stats = [(cut(stats, h), scaling, offset) for h in range(halves)]
+    spectra = [
+        lon_forward(streams[h], lon_fwd, bands, waves, pair, stats[h]) for h in range(halves)
+    ]
+    spectra = modes_of_bands(
+        spectra, lat_fwd, lat_back, weights[0], biases[0], pair, in0 + out0
     )
-    u = (values + restored + normed).astype(bf16)
-    u = u.reshape(rows, slots, part, slot).transpose(1, 0, 2, 3)
-    u = lax.all_to_all(u, quarter, split_axis=0, concat_axis=0, tiled=True)
-    w_in, w_out = gathered_pairs(fc_in[0], fc_out[0], ("comp", "tile"))
-    after_one, fluxes = first_mlp(
-        u.reshape(slots, rows * part, slot), gain(0, 1), shift(0, 1), heads, w_in, w_out
-    )
-
-    upsampled = jnp.repeat(jnp.repeat(fluxes.reshape(rows, part, -1), 2, axis=0), 2, axis=1)
+    spectra = [to_band(z) for z in spectra]
+    after_one, fluxes = [], []
+    for h in range(halves):
+        u = lon_back_call(
+            spectra[h], lon_back, slots, pair, streams[h], stats[h], in1 + out1 if h == 0 else ()
+        )
+        u = to_quarter(u).reshape(slots, half * part, slot)
+        a, f = first_mlp(u, gain(0, 1), shift(0, 1), heads, in0, out0)
+        after_one.append(a)
+        fluxes.append(f.reshape(half, part, -1))
+
+    fluxes = jnp.concatenate(fluxes, axis=0)
+    upsampled = jnp.repeat(jnp.repeat(fluxes, 2, axis=0), 2, axis=1)
     sea_cells = sea_mask.astype(f32)[..., None]
     forcing = jnp.einsum("ijf,fc->ijc", upsampled, flux_embed, precision=full_precision)
     start = (ocean_state.astype(f32) + sea_cells * forcing).astype(bf16)
     widened = with_halo(start, ((quarter, 1),), 3, True)
-    extended = with_halo(widened, (("band", 0),), 3, False).astype(f32)
-    tile_rows = start.shape[0]
+    extended = with_halo(widened, (("band", 0),), 3, False)
+    tile_rows = start.shape[0] // halves
     tile_columns = start.shape[1]
-    convolved = jnp.zeros(start.shape, f32)
-    for row_step in range(7):
-        for col_step in range(7):
-            convolved = (
-                convolved
-                + extended[row_step : row_step + tile_rows, col_step : col_step + tile_columns]
-                * depth_kernel[row_step, col_step]
-            )
-    normed = layer_norm(convolved, ocean_gain, ocean_shift).astype(bf16)
     cells = tile_rows * tile_columns
-    ocean_next, surface = ocean_mlp(
-        normed.reshape(cells, -1),
-        start.reshape(cells, -1),
-        sea_cells.reshape(cells, 1),
-        ocean_in,
-        ocean_out,
-        layer_scale,
-        field_head,
-    )
-    ocean_next = ocean_next.reshape(start.shape)
-    surface = surface.reshape(tile_rows, tile_columns, -1)
-
-    patches = (
-        surface.reshape(rows, 2, part, 2, surface.shape[2])
-        .transpose(0, 2, 4, 1, 3)
-        .reshape(rows * part, -1)
-    )
-    middle, normed = make_middle(
-        after_one,
-        product_left(patches),
-        product_right(embed),
-        gain(1, 0),
-        shift(1, 0),
-        slots,
-    )
-    normed = lax.all_to_all(normed, quarter, split_axis=0, concat_axis=0, tiled=True)
-    normed = normed.reshape(slots, rows, part, slot).transpose(1, 0, 2, 3)
-    restored = spectral_filter(
-        normed.reshape(rows, longitudes, slot),
-        lon_fwd,
-        lon_back,
-        lat_fwd,
-        lat_back,
-        weights[1],
-        biases[1],
-    ).astype(bf16)
-    restored = restored.reshape(rows, slots, part, slot).transpose(1, 0, 2, 3)
-    restored = lax.all_to_all(restored, quarter, split_axis=0, concat_axis=0, tiled=True)
-    w_in, w_out = gathered_pairs(fc_in[1], fc_out[1], ("comp", "tile"))
-    out = second_mlp(
-        middle,
-        restored.reshape(slots, rows * part, slot),
-        gain(1, 0),
-        shift(1, 0),
-        gain(1, 1),
-        shift(1, 1),
-        w_in,
-        w_out,
-    )
-    out = lax.all_to_all(out, quarter, split_axis=0, concat_axis=0, tiled=True)
-    out = out.reshape(slots, rows, part, slot).transpose(1, 0, 2, 3)
-    return (out.reshape(rows, longitudes, slot), ocean_next, surface)
+    nexts, surfaces, middles, spectra = [], [], [], []
+    for h in range(halves):
+        first = h * tile_rows
+        convolved = jnp.zeros((tile_rows,) + start.shape[1:], f32)
+        for row_step in range(7):
+            for col_step in range(7):
+                convolved = (
+                    convolved
+                    + extended[
+                        first + row_step : first + row_step + tile_rows,
+                        col_step : col_step + tile_columns,
+                    ].astype(f32)
+                    * depth_kernel[row_step, col_step]
+                )
+        normed = layer_norm(convolved, ocean_gain, ocean_shift).astype(bf16)
+        ocean_next, surface = ocean_mlp(
+            normed.reshape(cells, -1),
+            start[first : first + tile_rows].reshape(cells, -1),
+            sea_cells[first : first + tile_rows].reshape(cells, 1),
+            ocean_in,
+            ocean_out,
+            layer_scale,
+            field_head,
+        )
+        nexts.append(ocean_next.reshape((tile_rows,) + start.shape[1:]))
+        surface = surface.reshape(tile_rows, tile_columns, -1)
+        surfaces.append(surface)
+        patches = (
+            surface.reshape(half, 2, part, 2, surface.shape[2])
+            .transpose(0, 2, 4, 1, 3)
+            .reshape(half * part, -1)
+        )
+        middle, normed = make_middle(
+            after_one[h],
+            product_left(patches),
+            product_right(embed),
+            gain(1, 0),
+            shift(1, 0),
+            slots,
+        )
+        middles.append(middle)
+        normed = to_quarter(normed).reshape(slots, half, part, slot)
+        spectra.append(lon_forward(normed, lon_fwd, bands, waves, pair))
+    ocean_next = jnp.concatenate(nexts, axis=0)
+    surface = jnp.concatenate(surfaces, axis=0)
+
+    spectra = modes_of_bands(spectra, lat_fwd, lat_back, weights[1], biases[1], pair, [])
+    spectra = [to_band(z) for z in spectra]
+    outs = []
+    for h in range(halves):
+        restored = lon_back_call(spectra[h], lon_back, slots, pair)
+        restored = to_quarter(restored).reshape(slots, half * part, slot)
+        out = second_mlp(
+            middles[h], restored, gain(1, 0), shift(1, 0), gain(1, 1), shift(1, 1), in1, out1
+        )
+        outs.append(to_quarter(out).reshape(slots, half, part, slot))
+    return (assemble(outs), ocean_next, surface)
 
 
 def solution(mesh):

time: 1210 us -> 1030 us (0.85)
  blocking collectives: 271 us -> 53.8 us
  waiting for transfers between devices: 427 us -> 350 us
  Pallas kernels: 167 us -> 241 us
  other arithmetic: 102 us -> 159 us
  local copies, waits for them, and re-layouts: 161 us -> 119 us
  starting transfers between devices: 42.8 us -> 84.5 us
  matrix products: 27.7 us -> 11.3 us
    all_to_all x3 -> x0, blocking collectives: 260 us -> none  [the longest x1 108 us: spectral_filter(): lax.all_to_all(x.reshape(bands, waves, 2, rows, width), 'band', split_axi...]
    ppermute x12, waiting for transfers between devices: 177 us -> 50.4 us  [gathered(): lax.ppermute(part, axis, [(i, (i + d) % n) for i in range(n)])]
    pallas_call x2 -> x11, Pallas kernels: 41.8 us -> 103 us  [the longest x2 44 us: mix_modes(): pl.pallas_call(kernel, grid=(waves // step,), in_specs=[pl.BlockSpec((2 *...]
    reshape x15 -> x20, local copies, waits for them, and re-layouts: 90.3 us -> 31 us  [the longest x4 8.41 us: modes_of_bands(): return [z.reshape(bands, count, parts, lanes) for z in zs]]
    all_to_all x5 -> x16, waiting for transfers between devices: 233 us -> 284 us  [the longest x8 237 us: to_band(): return lax.all_to_all(x, 'band', split_axis=0, concat_axis=0, tiled=True)]
    reduce_sum x1 -> x2, other arithmetic: 71.2 us -> 117 us  [layer_norm(): average = jnp.mean(values, axis=-1, keepdims=True)]
    all_to_all x5 -> x16, starting transfers between devices: 26.2 us -> 69.5 us  [the longest x8 36.6 us: to_band(): return lax.all_to_all(x, 'band', split_axis=0, concat_axis=0, tiled=True)]
    all_gather x1, blocking collectives: 5.65 us -> 28.9 us  [on_device(): embed = lax.all_gather(patch_embed, quarter, axis=1, tiled=True)]
  transfers between devices with their start and end apart: 23 -> 34, of which waited for: 12 -> 19; matrix products, arithmetic and copies ran while one was open for 5% -> 10% of each run, Pallas kernels for 0% -> 14%
where the time goes in v2:
time: 1030 us; the launch traced here: 1020 us
  waiting for transfers between devices  350 us (34%)
  Pallas kernels  241 us (23%)
  other arithmetic  159 us (15%)
  local copies, waits for them, and re-layouts  119 us (12%)
  starting transfers between devices  84.5 us (8%)
  blocking collectives  53.8 us (5%)
  matrix products  11.3 us (1%)
    all_to_all x8, waiting for transfers between devices, to_band(): return lax.all_to_all(x, 'band', split_axis=0, concat_axis=0, tiled=True)  237 us
    reduce_sum x2, other arithmetic, layer_norm(): average = jnp.mean(values, axis=-1, keepdims=True)  117 us
    ppermute x12, waiting for transfers between devices, gathered(): lax.ppermute(part, axis, [(i, (i + d) % n) for i in range(n)])  50.4 us
    pallas_call x2, Pallas kernels, second_mlp(): pl.pallas_call(functools.partial(second_mlp_kernel, n), grid=(tokens // t...  47 us
    all_to_all x8, waiting for transfers between devices, to_quarter(): return lax.all_to_all(x, quarter, split_axis=0, concat_axis=0, tiled=True)  46.4 us
    pallas_call x2, Pallas kernels, first_mlp(): pl.pallas_call(functools.partial(first_mlp_kernel, n), grid=(tokens // ti...  44.8 us
    pallas_call x2, Pallas kernels, mix_modes(): pl.pallas_call(kernel, grid=(waves // step,), in_specs=[pl.BlockSpec((2 *...  44 us
    pallas_call x2, Pallas kernels, ocean_mlp(): pl.pallas_call(ocean_kernel, grid=(cells // tile,), in_specs=[rows(width)...  37 us
  transfers between devices with their start and end apart: 34, of which 19 were waited for; matrix products, arithmetic and copies ran while one was open for 10% of the time, Pallas kernels for 14%

profile of v2, /device:TPU:0, one launch (start us, length us, event | category | flops | bytes accessed | tf_op | source)
XLA Modules:
  0.0 1020.4 jit_solution(11109931345194995001)
XLA Ops:
  23.9 7.4 shard_map.202
  31.4 6.0 all-to-all-start
  39.8 7.4 shard_map.203
  47.3 31.2 %all-to-all-done = bf16[8,6,48,384]{3,2,1,0:T(8,128)(2,1)S(1)} async-done(((bf16[8,6,48,384]{3,2,1,0:T(8,128)(2,1)}), bf16[8,6,48,384]{3,2,1,0:T(8,128)(2,1)S(1)}, u32[]{:S(2)}, u32[]{:S(2)}) %all-to-all-start) | async-done | bytes 1769504 | tf_op jit(solution)/shard_map/all_to_all | solution.py:544
  96.3 18.7 %collective-permute-done.2.refs_7_.refs_1_ = bf16[768,768]{1,0:T(8,128)(2,1)} collective-permute-done((bf16[768,768]{1,0:T(8,128)(2,1)}, bf16[768,768]{1,0:T(8,128)(2,1)}, u32[]{:S(2)}, u32[]{:S(2)}) %collective-permute-start.2) | collective-permute-done | bytes 1179680 | tf_op jit(solution)/shard_map/ppermute | solution.py:91
  115.0 24.0 %collective-permute-done.5.refs_11_.refs_5_ = bf16[768,768]{1,0:T(8,128)(2,1)} collective-permute-done((bf16[768,768]{1,0:T(8,128)(2,1)}, bf16[768,768]{1,0:T(8,128)(2,1)}, u32[]{:S(2)}, u32[]{:S(2)}) %collective-permute-start.5) | collective-permute-done | bytes 1179680 | tf_op jit(solution)/shard_map/ppermute | solution.py:91
  147.0 22.0 %shard_map.204 = (bf16[24,96,384]{2,1,0:T(8,128)(2,1)}, bf16[24,96,384]{2,1,0:T(8,128)(2,1)}) custom-call(bf16[48,48,384]{2,1,0:T(8,128)(2,1)} %copy.169.refs_0_, bf16[48,48,384]{2,1,0:T(8,128)(2,1)} %copy.170.refs_1_, bf16[384,384]{1,0:T(8,128)(2,1)} %maximum_maximum_fusion.2.refs_2_, bf16[384,384]{1,0:T(8,128)(2,1)} %bitcast.206, ...), custom_call_target="tpu_custom_call" | custom-call | flops 5435817984 | bytes 7077888 | tf_op jit(solution)/shard_map/pallas_call | solution.py:274
  175.1 5.7 all-to-all-start.4
  186.8 35.9 %all-to-all-done.4.refs_0_ = bf16[8,6,48,384]{3,2,1,0:T(8,128)(2,1)S(1)} async-done(((bf16[8,6,48,384]{3,2,1,0:T(8,128)(2,1)}), bf16[8,6,48,384]{3,2,1,0:T(8,128)(2,1)S(1)}, u32[]{:S(2)}, u32[]{:S(2)}) %all-to-all-start.4) | async-done | bytes 1769504 | tf_op jit(solution)/shard_map/all_to_all | solution.py:544
  234.4 7.5 shard_map.207
  241.9 26.3 %all-to-all-done.2.refs_0_ = bf16[8,6,48,384]{3,2,1,0:T(8,128)(2,1)S(1)} async-done(((bf16[8,6,48,384]{3,2,1,0:T(8,128)(2,1)}), bf16[8,6,48,384]{3,2,1,0:T(8,128)(2,1)S(1)}, u32[]{:S(2)}, u32[]{:S(2)}) %all-to-all-start.2) | async-done | bytes 1769504 | tf_op jit(solution)/shard_map/all_to_all | solution.py:544
  273.7 7.6 collective-permute-done.11.refs_11_.refs_5_
  281.3 24.9 %all-gather = bf16[4,192,8]{1,2,0:T(8,128)(2,1)S(1)} all-gather(bf16[1,192,8]{1,2,0:T(8,128)(2,1)S(1)} %bitcast.309), channel_id=1, replica_groups=mesh['band'=8,'comp'=2,'tile'=2] {'comp','tile'}, dimensions={0}, use_global_device_ids=true | all-gather | bytes 15360 | tf_op jit(solution)/shard_map/all_gather | solution.py:612
  310.8 7.5 shard_map.205
  322.7 28.9 %all-gather.1 = f32[4,192,16]{1,2,0:T(8,128)S(1)} all-gather(f32[1,192,16]{1,2,0:T(8,128)S(1)} %bitcast.210), channel_id=1, replica_groups=mesh['band'=8,'comp'=2,'tile'=2] {'comp','tile'}, dimensions={0}, use_global_device_ids=true | all-gather | bytes 61440 | tf_op jit(solution)/shard_map/all_gather | solution.py:613
  351.8 22.4 %shard_map.208 = (bf16[1152,768]{1,0:T(8,128)(2,1)}, f32[1152,8]{1,0:T(8,128)}) custom-call(bf16[4,1152,192]{2,1,0:T(8,128)(2,1)} %bitcast.26.u_ref, f32[1,768]{1,0:T(1,128)} %get-tuple-element.142.gain, f32[1,768]{1,0:T(1,128)} %get-tuple-element.138.shift, bf16[768,8]{1,0:T(8,128)(2,1)} %bitcast.208, bf16[768,768]{1,0:T(8,128)(2,1)} %get-tuple-element.71.refs_6_.refs_0_, ...), custom_call_target="tpu_custom_call" | custom-call | flops 10871635968 | bytes 12976128 | tf_op jit(solution)/shard_map/pallas_call | solution.py:124
  376.9 22.4 %shard_map.206 = (bf16[1152,768]{1,0:T(8,128)(2,1)}, f32[1152,8]{1,0:T(8,128)}) custom-call(bf16[4,1152,192]{2,1,0:T(8,128)(2,1)} %bitcast.193, f32[1,768]{1,0:T(1,128)} %get-tuple-element.142.gain, f32[1,768]{1,0:T(1,128)} %get-tuple-element.138.shift, bf16[768,8]{1,0:T(8,128)(2,1)} %bitcast.209, bf16[768,768]{1,0:T(8,128)(2,1)} %get-tuple-element.71.refs_6_.refs_0_, ...), custom_call_target="tpu_custom_call" | custom-call | flops 10871635968 | bytes 12976128 | tf_op jit(solution)/shard_map/pallas_call | solution.py:124
  401.3 11.3 %add_convert_fusion = bf16[48,192,256]{2,1,0:T(8,128)(2,1)S(1)} fusion(bf16[48,192,256]{2,1,0:T(8,128)(2,1)} %param.28, f32[48,192]{1,0:T(8,128)S(1)} %convert_element_type.406, f32[48,192,8]{1,2,0:T(8,128)S(1)} %copy.182, f32[8,256]{1,0:T(8,128)S(1)} %copy-done), kind=kOutput, calls=%fused_computation.46 | convolution fusion | flops 235929600 | bytes 9777152 | tf_op jit(solution)/shard_map/ijf,fc->ijc/dot_general | solution.py:649
  419.4 4.6 collective-permute-start.16
  429.3 6.7 collective-permute-done.16
  436.0 11.6 %pad_maximum_fusion = (bf16[51,198,256]{2,1,0:T(8,128)(2,1)S(1)}, bf16[51,198,256]{2,1,0:T(8,128)(2,1)S(1)}) fusion(bf16[3,198,256]{2,1,0:T(8,128)(2,1)S(1)} %collective-permute-done.17, bf16[48,3,256]{2,1,0:T(4,128)(2,1)S(1)} %collective-permute-done.15, bf16[48,192,256]{2,1,0:T(8,128)(2,1)S(1)} %add_convert_fusion, ...), kind=kLoop, calls=%fused_computation.51 | loop fusion | flops 41361408 | bytes 15814656 | tf_op jit(solution)/shard_map/concatenate | solution.py:566
  447.6 59.5 %fusion.79 = (f32[24,192]{1,0:T(8,128)S(1)}, f32[24,192]{1,0:T(8,128)S(1)}, f32[24,192,256]{2,1,0:T(8,128)}) fusion(f32[256]{0:T(256)S(1)} %bitcast.229, bf16[51,198,256]{2,1,0:T(8,128)(2,1)S(1)} %get-tuple-element.58, f32[256]{0:T(256)S(1)} %bitcast.231, f32[256]{0:T(256)S(1)} %bitcast.235, f32[256]{0:T(256)S(1)} %bitcast.237, f32[256]{0:T(256)S(1)} %bitcast.239, ...), kind=kLoop, calls=%fused_computation.243 | loop fusion | flops 260692992 | bytes 68654080 | tf_op jit(solution)/shard_map/reduce_sum | solution.py:51
  507.2 57.6 %fusion.80 = (f32[24,192]{1,0:T(8,128)S(1)}, f32[24,192]{1,0:T(8,128)S(1)}, f32[24,192,256]{2,1,0:T(8,128)}) fusion(f32[256]{0:T(256)S(1)} %bitcast.230, f32[256]{0:T(256)S(1)} %bitcast.232, f32[256]{0:T(256)S(1)} %bitcast.236, f32[256]{0:T(256)S(1)} %bitcast.238, bf16[48,192,256]{2,1,0:T(8,128)(2,1)} %copy-done.2, f32[256]{0:T(256)S(1)} %bitcast.240, ...), kind=kLoop, calls=%fused_computation.244 | loop fusion | flops 260692992 | bytes 68654080 | tf_op jit(solution)/shard_map/reduce_sum | solution.py:51
  564.8 7.1 add_convert_fusion.1
  571.9 18.5 %shard_map.209 = (bf16[4608,256]{1,0:T(8,128)(2,1)}, f32[4608,4]{1,0:T(8,128)}) custom-call(bf16[4608,256]{1,0:T(8,128)(2,1)} %bitcast.200, bf16[4608,256]{1,0:T(8,128)(2,1)} %bitcast.198, f32[4608,1]{1,0:T(8,128)} %reshape.545.mask_ref, bf16[256,1024]{1,0:T(8,128)(2,1)} %w_in.3, bf16[1024,256]{1,0:T(8,128)(2,1)} %w_out.3, f32[1,256]{1,0:T(1,128)} %bitcast.312, ...), custom_call_target="tpu_custom_call" | custom-call | flops 4831838208 | bytes 9437184 | tf_op jit(solution)/shard_map/pallas_call | solution.py:464
  594.5 5.1 shard_map.210
  611.1 18.5 %shard_map.212 = (bf16[4608,256]{1,0:T(8,128)(2,1)}, f32[4608,4]{1,0:T(8,128)}) custom-call(bf16[4608,256]{1,0:T(8,128)(2,1)} %bitcast.199, bf16[4608,256]{1,0:T(8,128)(2,1)} %bitcast.197, f32[4608,1]{1,0:T(8,128)} %reshape.546.mask_ref, bf16[256,1024]{1,0:T(8,128)(2,1)} %w_in.3, bf16[1024,256]{1,0:T(8,128)(2,1)} %w_out.3, f32[1,256]{1,0:T(1,128)} %bitcast.313, ...), custom_call_target="tpu_custom_call" | custom-call | flops 4831838208 | bytes 9437184 | tf_op jit(solution)/shard_map/pallas_call | solution.py:464
  633.8 5.1 shard_map.213
  649.0 5.9 shard_map.211
  654.8 13.8 %all-to-all-done.8 = bf16[4,1152,192]{1,2,0:T(8,128)(2,1)S(1)} async-done(((bf16[4,1152,192]{1,2,0:T(8,128)(2,1)}), bf16[4,1152,192]{1,2,0:T(8,128)(2,1)S(1)}, u32[]{:S(2)}, u32[]{:S(2)}) %all-to-all-start.8) | async-done | bytes 1769504 | tf_op jit(solution)/shard_map/all_to_all | solution.py:548
  668.7 5.6 all-to-all-start.7
  676.7 5.9 shard_map.214
  682.6 32.7 %all-to-all-done.7 = bf16[8,6,48,384]{3,2,1,0:T(8,128)(2,1)S(1)} async-done(((bf16[8,6,48,384]{3,2,1,0:T(8,128)(2,1)}), bf16[8,6,48,384]{3,2,1,0:T(8,128)(2,1)S(1)}, u32[]{:S(2)}, u32[]{:S(2)}) %all-to-all-start.7) | async-done | bytes 1769504 | tf_op jit(solution)/shard_map/all_to_all | solution.py:544
  721.5 39.2 %all-to-all-done.9 = bf16[8,6,48,384]{3,2,1,0:T(8,128)(2,1)S(1)} async-done(((bf16[8,6,48,384]{3,2,1,0:T(8,128)(2,1)}), bf16[8,6,48,384]{3,2,1,0:T(8,128)(2,1)S(1)}, u32[]{:S(2)}, u32[]{:S(2)}) %all-to-all-start.9) | async-done | bytes 1769504 | tf_op jit(solution)/shard_map/all_to_all | solution.py:544
  762.3 21.9 %shard_map.215 = (bf16[24,96,384]{2,1,0:T(8,128)(2,1)}, bf16[24,96,384]{2,1,0:T(8,128)(2,1)}) custom-call(bf16[48,48,384]{2,1,0:T(8,128)(2,1)} %copy.197.refs_0_, bf16[48,48,384]{2,1,0:T(8,128)(2,1)} %copy.198.refs_1_, bf16[384,384]{1,0:T(8,128)(2,1)} %maximum_maximum_fusion.2.refs_2_, bf16[384,384]{1,0:T(8,128)(2,1)} %bitcast.207, ...), custom_call_target="tpu_custom_call" | custom-call | flops 5435817984 | bytes 7077888 | tf_op jit(solution)/shard_map/pallas_call | solution.py:274
  798.4 36.8 %all-to-all-done.10.refs_0_ = bf16[8,6,48,384]{3,2,1,0:T(8,128)(2,1)S(1)} async-done(((bf16[8,6,48,384]{3,2,1,0:T(8,128)(2,1)}), bf16[8,6,48,384]{3,2,1,0:T(8,128)(2,1)S(1)}, u32[]{:S(2)}, u32[]{:S(2)}) %all-to-all-start.10) | async-done | bytes 1769504 | tf_op jit(solution)/shard_map/all_to_all | solution.py:544
  838.9 5.9 shard_map.216
  844.8 35.5 %all-to-all-done.13.refs_0_ = bf16[8,6,48,384]{3,2,1,0:T(8,128)(2,1)S(1)} async-done(((bf16[8,6,48,384]{3,2,1,0:T(8,128)(2,1)}), bf16[8,6,48,384]{3,2,1,0:T(8,128)(2,1)S(1)}, u32[]{:S(2)}, u32[]{:S(2)}) %all-to-all-start.13) | async-done | bytes 1769504 | tf_op jit(solution)/shard_map/all_to_all | solution.py:544
  880.3 4.5 all-to-all-start.11
  884.8 5.9 shard_map.218
  890.8 22.6 %all-to-all-done.11 = bf16[4,12,96,192]{3,2,1,0:T(8,128)(2,1)} async-done(((bf16[4,12,96,192]{3,2,1,0:T(8,128)(2,1)}), bf16[4,12,96,192]{3,2,1,0:T(8,128)(2,1)}, u32[]{:S(2)}, u32[]{:S(2)}) %all-to-all-start.11) | async-done | bytes 1769504 | tf_op jit(solution)/shard_map/all_to_all | solution.py:548
  917.2 23.5 %shard_map.217 = bf16[4,1152,192]{2,1,0:T(8,128)(2,1)} custom-call(bf16[1152,768]{1,0:T(8,128)(2,1)} %get-tuple-element.25.v_ref, bf16[4,1152,192]{2,1,0:T(8,128)(2,1)} %bitcast.104.r_ref, f32[1,768]{1,0:T(1,128)} %get-tuple-element.144.gain.gain0, f32[1,768]{1,0:T(1,128)} %get-tuple-element.140.shift.shift0, f32[1,768]{1,0:T(1,128)} %get-tuple-element.141.gain, ...), custom_call_target="tpu_custom_call" | custom-call | flops 10871635968 | bytes 14745600 | tf_op jit(solution)/shard_map/pallas_call | solution.py:169
  945.7 4.6 all-to-all-start.12
  950.3 23.5 %shard_map.219 = bf16[4,1152,192]{2,1,0:T(8,128)(2,1)} custom-call(bf16[1152,768]{1,0:T(8,128)(2,1)} %get-tuple-element.31.v_ref, bf16[4,1152,192]{2,1,0:T(8,128)(2,1)} %bitcast.194, f32[1,768]{1,0:T(1,128)} %get-tuple-element.144.gain.gain0, f32[1,768]{1,0:T(1,128)} %get-tuple-element.140.shift.shift0, f32[1,768]{1,0:T(1,128)} %get-tuple-element.141.gain, ...), custom_call_target="tpu_custom_call" | custom-call | flops 10871635968 | bytes 14745600 | tf_op jit(solution)/shard_map/pallas_call | solution.py:169
  986.8 5.0 pad_maximum_fusion.1
  995.7 9.1 all-to-all-done.15
  1008.8 5.0 shard_map.220
  1013.8 6.3 copy.211
  (207 shorter events, 194.1 us)
Async XLA Ops:
  0.6 400.6 %copy-start = (f32[8,256]{1,0:T(8,128)S(1)}, f32[8,256]{1,0:T(8,128)}, u32[]{:S(2)}) copy-start(f32[8,256]{1,0:T(8,128)} %param.27) | copy-start | bytes 24580
  4.6 10.8 %collective-permute-start = (f32[2,24,384]{2,0,1:T(2,128)}, f32[2,24,384]{2,0,1:T(2,128)}, u32[]{:S(2)}, u32[]{:S(2)}) collective-permute-start(f32[2,24,384]{2,0,1:T(2,128)} %pad_maximum_fusion.13), channel_id=1, source_target_pairs={{0,1},{1,0},{2,3},{3,2},{4,5},{5,4},{6,7},{7,6},{8,9},{9,8},{10,11... | collective-permute-start | bytes 221192 | tf_op jit(solution)/shard_map/ppermute | solution.py:82
  16.4 5.5 collective-permute-start.1
  31.4 47.1 %all-to-all-start = ((bf16[8,6,48,384]{3,2,1,0:T(8,128)(2,1)}), bf16[8,6,48,384]{3,2,1,0:T(8,128)(2,1)S(1)}, u32[]{:S(2)}, u32[]{:S(2)}) async-start(bf16[8,6,48,384]{3,2,1,0:T(8,128)(2,1)} %shard_map.202), calls=%async_computation | async-start | bytes 3538944 | tf_op jit(solution)/shard_map/all_to_all | solution.py:544
  78.5 66.8 %all-to-all-start.1 = ((bf16[8,6,48,384]{3,2,1,0:T(8,128)(2,1)}), bf16[8,6,48,384]{3,2,1,0:T(8,128)(2,1)S(1)}, u32[]{:S(2)}, u32[]{:S(2)}) async-start(bf16[8,6,48,384]{3,2,1,0:T(8,128)(2,1)} %shard_map.203), calls=%async_computation.1 | async-start | bytes 3538944 | tf_op jit(solution)/shard_map/all_to_all | solution.py:544
  85.8 29.2 %collective-permute-start.2 = (bf16[768,768]{1,0:T(8,128)(2,1)}, bf16[768,768]{1,0:T(8,128)(2,1)}, u32[]{:S(2)}, u32[]{:S(2)}) collective-permute-start(bf16[768,768]{1,0:T(8,128)(2,1)} %get-tuple-element.71.refs_6_.refs_0_), channel_id=1, source_target_pairs={{0,2},{2,0},{1,3},{3,1},{4,6},{6,4},{5,7},{7,5},{8,10},{10,8},{9,1... | collective-permute-start | bytes 3538952 | tf_op jit(solution)/shard_map/ppermute | solution.py:91
  88.9 50.1 %collective-permute-start.5 = (bf16[768,768]{1,0:T(8,128)(2,1)}, bf16[768,768]{1,0:T(8,128)(2,1)}, u32[]{:S(2)}, u32[]{:S(2)}) collective-permute-start(bf16[768,768]{1,0:T(8,128)(2,1)} %get-tuple-element.69.refs_10_.refs_4_), channel_id=1, source_target_pairs={{0,2},{2,0},{1,3},{3,1},{4,6},{6,4},{5,7},{7,5},{8,10},{10,8},{9,1... | collective-permute-start | bytes 3538952 | tf_op jit(solution)/shard_map/ppermute | solution.py:91
  89.4 57.6 %collective-permute-start.3 = (bf16[768,768]{1,0:T(8,128)(2,1)}, bf16[768,768]{1,0:T(8,128)(2,1)}, u32[]{:S(2)}, u32[]{:S(2)}) collective-permute-start(bf16[768,768]{1,0:T(8,128)(2,1)} %get-tuple-element.71.refs_6_.refs_0_), channel_id=1, source_target_pairs={{0,1},{1,0},{2,3},{3,2},{4,5},{5,4},{6,7},{7,6},{8,9},{9,8},{10,11... | collective-permute-start | bytes 3538952 | tf_op jit(solution)/shard_map/ppermute | solution.py:91
  89.4 57.6 %collective-permute-start.6 = (bf16[768,768]{1,0:T(8,128)(2,1)}, bf16[768,768]{1,0:T(8,128)(2,1)}, u32[]{:S(2)}, u32[]{:S(2)}) collective-permute-start(bf16[768,768]{1,0:T(8,128)(2,1)} %get-tuple-element.69.refs_10_.refs_4_), channel_id=1, source_target_pairs={{0,1},{1,0},{2,3},{3,2},{4,5},{5,4},{6,7},{7,6},{8,9},{9,8},{10,11... | collective-permute-start | bytes 3538952 | tf_op jit(solution)/shard_map/ppermute | solution.py:91
  115.0 32.0 %collective-permute-start.4 = (bf16[768,768]{1,0:T(8,128)(2,1)}, bf16[768,768]{1,0:T(8,128)(2,1)}, u32[]{:S(2)}, u32[]{:S(2)}) collective-permute-start(bf16[768,768]{1,0:T(8,128)(2,1)} %collective-permute-done.2.refs_7_.refs_1_), channel_id=1, source_target_pairs={{0,1},{1,0},{2,3},{3,2},{4,5},{5,4},{6,7},{7,6},{8,9},{9,8},{10,11... | collective-permute-start | bytes 3538952 | tf_op jit(solution)/shard_map/ppermute | solution.py:91
  139.0 8.0 collective-permute-start.7
  175.1 47.6 %all-to-all-start.4 = ((bf16[8,6,48,384]{3,2,1,0:T(8,128)(2,1)}), bf16[8,6,48,384]{3,2,1,0:T(8,128)(2,1)S(1)}, u32[]{:S(2)}, u32[]{:S(2)}) async-start(bf16[8,6,48,384]{3,2,1,0:T(8,128)(2,1)} %reshape.511), calls=%async_computation.4 | async-start | bytes 3538944 | tf_op jit(solution)/shard_map/all_to_all | solution.py:544
  222.7 11.7 %copy-start.7 = (bf16[8,6,48,384]{3,2,1,0:T(8,128)(2,1)}, bf16[8,6,48,384]{3,2,1,0:T(8,128)(2,1)S(1)}, u32[]{:S(2)}) copy-start(bf16[8,6,48,384]{3,2,1,0:T(8,128)(2,1)S(1)} %all-to-all-done.4.refs_0_) | copy-start | bytes 5308420
  222.7 45.5 %all-to-all-start.2 = ((bf16[8,6,48,384]{3,2,1,0:T(8,128)(2,1)}), bf16[8,6,48,384]{3,2,1,0:T(8,128)(2,1)S(1)}, u32[]{:S(2)}, u32[]{:S(2)}) async-start(bf16[8,6,48,384]{3,2,1,0:T(8,128)(2,1)} %reshape.507), calls=%async_computation.2 | async-start | bytes 3538944 | tf_op jit(solution)/shard_map/all_to_all | solution.py:544
  226.8 46.5 %collective-permute-start.8 = (bf16[768,768]{1,0:T(8,128)(2,1)}, bf16[768,768]{1,0:T(8,128)(2,1)}, u32[]{:S(2)}, u32[]{:S(2)}) collective-permute-start(bf16[768,768]{1,0:T(8,128)(2,1)} %get-tuple-element.70.refs_6_.refs_0_), channel_id=1, source_target_pairs={{0,2},{2,0},{1,3},{3,1},{4,6},{6,4},{5,7},{7,5},{8,10},{10,8},{9,1... | collective-permute-start | bytes 3538952 | tf_op jit(solution)/shard_map/ppermute | solution.py:91
  228.3 53.0 %collective-permute-start.11 = (bf16[768,768]{1,0:T(8,128)(2,1)}, bf16[768,768]{1,0:T(8,128)(2,1)}, u32[]{:S(2)}, u32[]{:S(2)}) collective-permute-start(bf16[768,768]{1,0:T(8,128)(2,1)} %get-tuple-element.68.refs_10_.refs_4_), channel_id=1, source_target_pairs={{0,2},{2,0},{1,3},{3,1},{4,6},{6,4},{5,7},{7,5},{8,10},{10,8},{9,1... | collective-permute-start | bytes 3538952 | tf_op jit(solution)/shard_map/ppermute | solution.py:91
  234.4 46.9 %copy-start.20 = (bf16[192,8]{0,1:T(8,128)(2,1)S(1)}, bf16[192,8]{0,1:T(8,128)(2,1)}, u32[]{:S(2)}) copy-start(bf16[192,8]{0,1:T(8,128)(2,1)} %param.26) | copy-start | bytes 9220
  241.9 30.8 %copy-start.10 = (bf16[768,768]{1,0:T(8,128)(2,1)S(1)}, bf16[768,768]{1,0:T(8,128)(2,1)}, u32[]{:S(2)}) copy-start(bf16[768,768]{1,0:T(8,128)(2,1)} %get-tuple-element.70.refs_6_.refs_0_) | copy-start | bytes 3538948
  241.9 65.1 %copy-start.17 = (s32[48,192]{1,0:T(8,128)S(1)}, s32[48,192]{1,0:T(8,128)}, u32[]{:S(2)}) copy-start(s32[48,192]{1,0:T(8,128)} %param.29) | copy-start | bytes 110596
  241.9 68.8 %copy-start.21 = (f32[256,4]{0,1:T(4,128)S(1)}, f32[256,4]{0,1:T(4,128)}, u32[]{:S(2)}) copy-start(f32[256,4]{0,1:T(4,128)} %param.36) | copy-start | bytes 12292
  241.9 68.8 %copy-start.18 = (f32[7,7,256]{2,1,0:T(8,128)S(1)}, f32[7,7,256]{2,1,0:T(8,128)}, u32[]{:S(2)}) copy-start(f32[7,7,256]{2,1,0:T(8,128)} %param.30) | copy-start | bytes 150532
  268.2 42.6 %copy-start.6 = (bf16[8,6,48,384]{3,2,1,0:T(8,128)(2,1)}, bf16[8,6,48,384]{3,2,1,0:T(8,128)(2,1)S(1)}, u32[]{:S(2)}) copy-start(bf16[8,6,48,384]{3,2,1,0:T(8,128)(2,1)S(1)} %all-to-all-done.2.refs_0_) | copy-start | bytes 5308420
  268.2 50.1 %all-to-all-start.5 = ((bf16[4,12,96,192]{3,2,1,0:T(8,128)(2,1)}), bf16[4,12,96,192]{3,2,1,0:T(8,128)(2,1)}, u32[]{:S(2)}, u32[]{:S(2)}) async-start(bf16[4,12,96,192]{3,2,1,0:T(8,128)(2,1)} %shard_map.207), calls=%async_computation.5 | async-start | bytes 4718592 | tf_op jit(solution)/shard_map/all_to_all | solution.py:548
  272.7 38.1 %collective-permute-start.9 = (bf16[768,768]{1,0:T(8,128)(2,1)S(1)}, bf16[768,768]{1,0:T(8,128)(2,1)}, u32[]{:S(2)}, u32[]{:S(2)}) collective-permute-start(bf16[768,768]{1,0:T(8,128)(2,1)S(1)} %copy-done.10), channel_id=1, source_target_pairs={{0,1},{1,0},{2,3},{3,2},{4,5},{5,4},{6,7},{7,6},{8,9},{9,8},{10,11... | collective-permute-start | bytes 3538952 | tf_op jit(solution)/shard_map/ppermute | solution.py:91
  273.2 37.6 %collective-permute-start.12 = (bf16[768,768]{1,0:T(8,128)(2,1)}, bf16[768,768]{1,0:T(8,128)(2,1)}, u32[]{:S(2)}, u32[]{:S(2)}) collective-permute-start(bf16[768,768]{1,0:T(8,128)(2,1)} %get-tuple-element.68.refs_10_.refs_4_), channel_id=1, source_target_pairs={{0,1},{1,0},{2,3},{3,2},{4,5},{5,4},{6,7},{7,6},{8,9},{9,8},{10,11... | collective-permute-start | bytes 3538952 | tf_op jit(solution)/shard_map/ppermute | solution.py:91
  273.3 37.5 %collective-permute-start.10 = (bf16[768,768]{1,0:T(8,128)(2,1)}, bf16[768,768]{1,0:T(8,128)(2,1)}, u32[]{:S(2)}, u32[]{:S(2)}) collective-permute-start(bf16[768,768]{1,0:T(8,128)(2,1)} %collective-permute-done.8.refs_7_.refs_1_), channel_id=1, source_target_pairs={{0,1},{1,0},{2,3},{3,2},{4,5},{5,4},{6,7},{7,6},{8,9},{9,8},{10,11... | collective-permute-start | bytes 3538952 | tf_op jit(solution)/shard_map/ppermute | solution.py:91
  281.3 29.5 %collective-permute-start.13 = (bf16[768,768]{1,0:T(8,128)(2,1)}, bf16[768,768]{1,0:T(8,128)(2,1)}, u32[]{:S(2)}, u32[]{:S(2)}) collective-permute-start(bf16[768,768]{1,0:T(8,128)(2,1)} %collective-permute-done.11.refs_11_.refs_5_), channel_id=1, source_target_pairs={{0,1},{1,0},{2,3},{3,2},{4,5},{5,4},{6,7},{7,6},{8,9},{9,8},{10,11... | collective-permute-start | bytes 3538952 | tf_op jit(solution)/shard_map/ppermute | solution.py:91
  318.3 57.1 %all-to-all-start.3 = ((bf16[4,12,96,192]{3,2,1,0:T(8,128)(2,1)}), bf16[4,12,96,192]{3,2,1,0:T(8,128)(2,1)S(1)}, u32[]{:S(2)}, u32[]{:S(2)}) async-start(bf16[4,12,96,192]{3,2,1,0:T(8,128)(2,1)} %shard_map.205), calls=%async_computation.3 | async-start | bytes 4718592 | tf_op jit(solution)/shard_map/all_to_all | solution.py:548
  412.6 23.4 %copy-start.2 = (bf16[48,192,256]{2,1,0:T(8,128)(2,1)}, bf16[48,192,256]{2,1,0:T(8,128)(2,1)S(1)}, u32[]{:S(2)}) copy-start(bf16[48,192,256]{2,1,0:T(8,128)(2,1)S(1)} %add_convert_fusion) | copy-start | bytes 14155780
  412.7 2.6 collective-permute-start.15
  413.1 4.9 collective-permute-start.14
  418.1 11.2 %collective-permute-start.17 = (bf16[3,198,256]{2,1,0:T(8,128)(2,1)S(1)}, bf16[3,198,256]{2,1,0:T(8,128)(2,1)S(1)}, u32[]{:S(2)}, u32[]{:S(2)}) collective-permute-start(bf16[3,198,256]{2,1,0:T(8,128)(2,1)S(1)} %get-tuple-element.60), channel_id=1, source_target_pairs={{4,0},{8,4},{12,8},{16,12},{20,16},{24,20},{28,24},{5,1},{9,5},{13... | collective-permute-start | bytes 912392 | tf_op jit(solution)/shard_map/ppermute | solution.py:570
  419.4 16.6 %collective-permute-start.16 = (bf16[3,198,256]{2,1,0:T(8,128)(2,1)S(1)}, bf16[3,198,256]{2,1,0:T(8,128)(2,1)S(1)}, u32[]{:S(2)}, u32[]{:S(2)}) collective-permute-start(bf16[3,198,256]{2,1,0:T(8,128)(2,1)S(1)} %get-tuple-element.61), channel_id=1, source_target_pairs={{0,4},{4,8},{8,12},{12,16},{16,20},{20,24},{24,28},{1,5},{5,9},{9,... | collective-permute-start | bytes 912392 | tf_op jit(solution)/shard_map/ppermute | solution.py:568
  507.1 57.7 %copy-start.3 = (f32[24,192,256]{2,1,0:T(8,128)S(1)}, f32[24,192,256]{2,1,0:T(8,128)}, u32[]{:S(2)}) copy-start(f32[24,192,256]{2,1,0:T(8,128)} %get-tuple-element.56) | copy-start | bytes 14155780
  507.1 57.7 %copy-start.22 = (f32[256]{0:T(256)S(1)}, f32[256]{0:T(256)}, u32[]{:S(2)}) copy-start(f32[256]{0:T(256)} %param.32) | copy-start | bytes 3076
  507.2 57.6 %copy-start.23 = (f32[256]{0:T(256)S(1)}, f32[256]{0:T(256)}, u32[]{:S(2)}) copy-start(f32[256]{0:T(256)} %param.31) | copy-start | bytes 3076
  603.7 39.2 %all-to-all-start.6 = ((bf16[4,1152,192]{1,2,0:T(8,128)(2,1)}), bf16[4,1152,192]{1,2,0:T(8,128)(2,1)S(1)}, u32[]{:S(2)}, u32[]{:S(2)}) async-start(bf16[4,1152,192]{1,2,0:T(8,128)(2,1)} %copy.188), calls=%async_computation.6 | async-start | bytes 3538944 | tf_op jit(solution)/shard_map/all_to_all | solution.py:548
  642.9 25.7 %all-to-all-start.8 = ((bf16[4,1152,192]{1,2,0:T(8,128)(2,1)}), bf16[4,1152,192]{1,2,0:T(8,128)(2,1)S(1)}, u32[]{:S(2)}, u32[]{:S(2)}) async-start(bf16[4,1152,192]{1,2,0:T(8,128)(2,1)} %copy.194), calls=%async_computation.8 | async-start | bytes 3538944 | tf_op jit(solution)/shard_map/all_to_all | solution.py:548
  668.7 46.6 %all-to-all-start.7 = ((bf16[8,6,48,384]{3,2,1,0:T(8,128)(2,1)}), bf16[8,6,48,384]{3,2,1,0:T(8,128)(2,1)S(1)}, u32[]{:S(2)}, u32[]{:S(2)}) async-start(bf16[8,6,48,384]{3,2,1,0:T(8,128)(2,1)} %shard_map.211), calls=%async_computation.7 | async-start | bytes 3538944 | tf_op jit(solution)/shard_map/all_to_all | solution.py:544
  715.3 45.4 %all-to-all-start.9 = ((bf16[8,6,48,384]{3,2,1,0:T(8,128)(2,1)}), bf16[8,6,48,384]{3,2,1,0:T(8,128)(2,1)S(1)}, u32[]{:S(2)}, u32[]{:S(2)}) async-start(bf16[8,6,48,384]{3,2,1,0:T(8,128)(2,1)} %shard_map.214), calls=%async_computation.9 | async-start | bytes 3538944 | tf_op jit(solution)/shard_map/all_to_all | solution.py:544
  790.2 45.0 %all-to-all-start.10 = ((bf16[8,6,48,384]{3,2,1,0:T(8,128)(2,1)}), bf16[8,6,48,384]{3,2,1,0:T(8,128)(2,1)S(1)}, u32[]{:S(2)}, u32[]{:S(2)}) async-start(bf16[8,6,48,384]{3,2,1,0:T(8,128)(2,1)} %reshape.529), calls=%async_computation.10 | async-start | bytes 3538944 | tf_op jit(solution)/shard_map/all_to_all | solution.py:544
  835.3 45.0 %all-to-all-start.13 = ((bf16[8,6,48,384]{3,2,1,0:T(8,128)(2,1)}), bf16[8,6,48,384]{3,2,1,0:T(8,128)(2,1)S(1)}, u32[]{:S(2)}, u32[]{:S(2)}) async-start(bf16[8,6,48,384]{3,2,1,0:T(8,128)(2,1)} %reshape.533), calls=%async_computation.13 | async-start | bytes 3538944 | tf_op jit(solution)/shard_map/all_to_all | solution.py:544
  880.3 33.1 %all-to-all-start.11 = ((bf16[4,12,96,192]{3,2,1,0:T(8,128)(2,1)}), bf16[4,12,96,192]{3,2,1,0:T(8,128)(2,1)}, u32[]{:S(2)}, u32[]{:S(2)}) async-start(bf16[4,12,96,192]{3,2,1,0:T(8,128)(2,1)} %shard_map.216), calls=%async_computation.11 | async-start | bytes 4718592 | tf_op jit(solution)/shard_map/all_to_all | solution.py:548
  913.4 32.3 %all-to-all-start.14 = ((bf16[4,12,96,192]{3,2,1,0:T(8,128)(2,1)}), bf16[4,12,96,192]{3,2,1,0:T(8,128)(2,1)S(1)}, u32[]{:S(2)}, u32[]{:S(2)}) async-start(bf16[4,12,96,192]{3,2,1,0:T(8,128)(2,1)} %shard_map.218), calls=%async_computation.14 | async-start | bytes 4718592 | tf_op jit(solution)/shard_map/all_to_all | solution.py:548
  945.7 32.4 %all-to-all-start.12 = ((bf16[4,1152,192]{1,2,0:T(8,128)(2,1)}), bf16[4,1152,192]{1,2,0:T(8,128)(2,1)}, u32[]{:S(2)}, u32[]{:S(2)}) async-start(bf16[4,1152,192]{1,2,0:T(8,128)(2,1)} %copy.202), calls=%async_computation.12 | async-start | bytes 3538944 | tf_op jit(solution)/shard_map/all_to_all | solution.py:548
  973.8 11.3 %copy-start.5 = (f32[4608,4]{1,0:T(8,128)S(1)}, f32[4608,4]{1,0:T(8,128)}, u32[]{:S(2)}) copy-start(f32[4608,4]{1,0:T(8,128)} %get-tuple-element.24) | copy-start | bytes 221188
  978.1 26.7 %all-to-all-start.15 = ((bf16[4,1152,192]{1,2,0:T(8,128)(2,1)}), bf16[4,1152,192]{1,2,0:T(8,128)(2,1)}, u32[]{:S(2)}, u32[]{:S(2)}) async-start(bf16[4,1152,192]{1,2,0:T(8,128)(2,1)} %copy.207), calls=%async_computation.15 | async-start | bytes 3538944 | tf_op jit(solution)/shard_map/all_to_all | solution.py:548
  1008.8 11.4 %copy-start.1 = (f32[8,256]{1,0:T(8,128)S(1)}, f32[8,256]{1,0:T(8,128)}, u32[]{:S(2)}) copy-start(f32[8,256]{1,0:T(8,128)} %param.27) | copy-start | bytes 24580
  (10 other events, 37.1 us)

commit v3 on v2

--- a/solution.py
+++ b/solution.py
@@ -3,6 +3,7 @@
 
 import jax
 import jax.numpy as jnp
+import numpy as np
 from jax import lax
 from jax.experimental import pallas as pl
 from jax.experimental.pallas import tpu as pltpu
@@ -43,6 +44,11 @@
     return n
 
 
+def pick_rows(tokens, part):
+    rows = tokens // part
+    return part * max(n for n in range(1, rows + 1) if rows % n == 0 and n * part <= 384)
+
+
 def dot(a, b):
     return jnp.dot(a, b, preferred_element_type=f32)
 
@@ -81,6 +87,11 @@
         for d in range(1, n):
             x = x + lax.ppermute(mine, axis, [(i, (i + d) % n) for i in range(n)])
     return x
+
+
+def spread(x, index, count):
+    mine = lax.broadcasted_iota(jnp.int32, (count,) + (1,) * x.ndim, 0) == index
+    return shift_sum(jnp.where(mine, x[None], jnp.zeros((), x.dtype)), ("tile", "comp"))
 
 
 def gathered(x, axes):
@@ -155,15 +166,15 @@
     r = jnp.concatenate([r_ref[i].astype(f32) for i in range(r_ref.shape[0])], axis=-1)
     u = (v + r + layer_norm(v, gain0[...], shift0[...])).astype(bf16).astype(f32)
     out = mlp_rows(u, gain[...], shift[...], w_in, w_out)
-    width = out_ref.shape[2]
+    width = out_ref.shape[3]
     for i in range(out_ref.shape[0]):
-        out_ref[i] = out[:, i * width : (i + 1) * width]
-
-
-def second_mlp(v, r, gain0, shift0, gain, shift, w_in, w_out):
+        out_ref[i] = out[:, i * width : (i + 1) * width].reshape(out_ref.shape[1:])
+
+
+def second_mlp(v, r, gain0, shift0, gain, shift, w_in, w_out, part):
     slots, tokens, width = r.shape
     full = slots * width
-    tile = pick(tokens, 384)
+    tile = pick_rows(tokens, part)
     n = len(w_in)
     hidden = sum(w.shape[1] for w in w_in)
     return pl.pallas_call(
@@ -176,8 +187,8 @@
         + [whole((1, full))] * 4
         + [whole(w.shape) for w in w_in]
         + [whole(w.shape) for w in w_out],
-        out_specs=pl.BlockSpec((slots, tile, width), lambda i: (0, i, 0)),
-        out_shape=jax.ShapeDtypeStruct((slots, tokens, width), bf16),
+        out_specs=pl.BlockSpec((slots, tile // part, part, width), lambda i: (0, i, 0, 0)),
+        out_shape=jax.ShapeDtypeStruct((slots, tokens // part, part, width), bf16),
         compiler_params=pltpu.CompilerParams(vmem_limit_bytes=vmem_bytes),
         cost_estimate=pl.CostEstimate(
             flops=4 * tokens * full * hidden,
@@ -191,14 +202,14 @@
     v = (a_ref[...].astype(f32) + dot(p_ref[...], e_ref[...])).astype(bf16)
     v_ref[...] = v
     normed = layer_norm(v.astype(f32), gain[...], shift[...]).astype(bf16)
-    width = n_ref.shape[2]
+    width = n_ref.shape[3]
     for i in range(n_ref.shape[0]):
-        n_ref[i] = normed[:, i * width : (i + 1) * width]
-
-
-def make_middle(a, patches, embed, gain, shift, slots):
+        n_ref[i] = normed[:, i * width : (i + 1) * width].reshape(n_ref.shape[1:])
+
+
+def make_middle(a, patches, embed, gain, shift, slots, part):
     tokens, full = a.shape
-    tile = pick(tokens, 384)
+    tile = pick_rows(tokens, part)
     return pl.pallas_call(
         middle_kernel,
         grid=(tokens // tile,),
@@ -211,11 +222,11 @@
         ],
         out_specs=[
             pl.BlockSpec((tile, full), lambda i: (i, 0)),
-            pl.BlockSpec((slots, tile, full // slots), lambda i: (0, i, 0)),
+            pl.BlockSpec((slots, tile // part, part, full // slots), lambda i: (0, i, 0, 0)),
         ],
         out_shape=[
             jax.ShapeDtypeStruct((tokens, full), bf16),
-            jax.ShapeDtypeStruct((slots, tokens, full // slots), bf16),
+            jax.ShapeDtypeStruct((slots, tokens // part, part, full // slots), bf16),
         ],
         compiler_params=pltpu.CompilerParams(vmem_limit_bytes=vmem_bytes),
     )(a, patches, embed, gain, shift)
@@ -436,99 +447,160 @@
     )(*outs)
 
 
-def ocean_kernel(on_ref, start_ref, mask_ref, w_in, w_out, scale, head, next_ref, field_ref):
-    half = w_in.shape[1] // 2
-    fields = field_ref.shape[1]
-    total = None
-    for i in range(2):
-        h = gelu(dot(on_ref[...], w_in[:, i * half : (i + 1) * half])).astype(bf16)
-        part = dot(h, w_out[i * half : (i + 1) * half, :])
-        total = part if total is None else total + part
-    mask = mask_ref[...]
-    out = (start_ref[...].astype(f32) + mask * (scale[...] * total)).astype(bf16)
-    next_ref[...] = out
-    parts = dot(out, head[...])
-    field_ref[...] = mask * (
-        parts[:, :fields] + parts[:, fields : 2 * fields] + parts[:, 2 * fields :]
-    )
-
-
-def ocean_mlp(on, start, mask, w_in, w_out, scale, head):
-    cells, width = on.shape
-    tile = pick(cells, 768)
+def ocean_block(extended, taps, gain, shift, mask, w_in, w_out, scale, head, early):
+    lane = 128
+    size = taps.shape[0]
+    reach = size // 2
+    side = -(-reach // 8) * 8
+    columns = extended.shape[1] - 2 * side
+    rows = extended.shape[0] - 2 * reach
+    width = extended.shape[2]
+    lane_parts = width // lane
+    blocks = 16 // lane_parts
+    block = columns // blocks
+    span = block + 2 * side
+    tile = blocks * lane_parts
     fields = head.shape[1]
+    step = max(n for n in range(1, 5) if rows % n == 0)
+    group = 4
+
+    taps = taps.reshape(size * size, 1, lane_parts, lane)
+    taps = jnp.broadcast_to(taps, (size * size, blocks, lane_parts, lane))
+    taps = taps.reshape(size * size, tile, lane).astype(bf16)
     high = lax.reduce_precision(head, 8, 7)
     mid = lax.reduce_precision(head - high, 8, 7)
     heads = jnp.concatenate([high, mid, head - high - mid], axis=1).astype(bf16)
-    rows = lambda n: pl.BlockSpec((tile, n), lambda i: (i, 0))
+
+    def kernel(*refs):
+        x_ref, t_ref, gain, shift, mask_ref, w_in, w_out, scale, head = refs[:9]
+        next_ref, field_ref, laid, held, summed, normed = refs[9 + len(early) :]
+        at = pl.program_id(0)
+
+        @pl.when(at == 0)
+        def _():
+            def lay(r, carry):
+                row = x_ref[r].astype(f32)
+                for b in range(blocks):
+                    for p in range(lane_parts):
+                        held[pl.ds(b * lane_parts + p, span, stride=tile), :] = row[
+                            b * block : b * block + span, p * lane : (p + 1) * lane
+                        ]
+                laid[r] = held[...].astype(bf16)
+                return carry
+
+            lax.fori_loop(0, rows + 2 * reach, lay, 0)
+
+        def correlate(r, carry):
+            for first in range(0, block, group):
+                count = min(group, block - first)
+                total = [None] * count
+                for a in range(size):
+                    near = [
+                        laid[at * step + r + a, pl.ds((side - reach + first + t) * tile, tile), :]
+                        for t in range(count + size - 1)
+                    ]
+                    for q in range(count):
+                        part = near[q] * t_ref[a * size]
+                        for e in range(1, size):
+                            part = part + near[q + e] * t_ref[a * size + e]
+                        part = part.astype(f32)
+                        total[q] = part if total[q] is None else total[q] + part
+                for q in range(count):
+                    summed[pl.ds((first + q) * tile, tile), :] = total[q]
+            for b in range(blocks):
+                cut = [
+                    summed[pl.ds(b * lane_parts + p, block, stride=tile), :]
+                    for p in range(lane_parts)
+                ]
+                cells = jnp.concatenate(cut, axis=-1)
+                normed[r, b * block : (b + 1) * block] = layer_norm(cells, gain[...], shift[...])
+            return carry
+
+        lax.fori_loop(0, step, correlate, 0)
+        cells = normed[...].reshape(step * columns, width).astype(bf16)
+        half = w_in.shape[1] // 2
+        update = None
+        for i in range(2):
+            h = gelu(dot(cells, w_in[:, i * half : (i + 1) * half])).astype(bf16)
+            part = dot(h, w_out[i * half : (i + 1) * half, :])
+            update = part if update is None else update + part
+        mask = mask_ref[...]
+        first = at * step + reach
+        start = x_ref[pl.ds(first, step), side : side + columns, :].astype(f32)
+        start = start.reshape(step * columns, width)
+        out = (start + mask * (scale[...] * update)).astype(bf16)
+        next_ref[...] = out
+        parts = dot(out, head[...])
+        field_ref[...] = mask * (
+            parts[:, :fields] + parts[:, fields : 2 * fields] + parts[:, 2 * fields :]
+        )
+
+    cells = rows * columns
+    by_cell = lambda n: pl.BlockSpec((step * columns, n), lambda i: (i, 0))
     return pl.pallas_call(
-        ocean_kernel,
-        grid=(cells // tile,),
+        kernel,
+        grid=(rows // step,),
         in_specs=[
-            rows(width),
-            rows(width),
-            rows(1),
+            whole(extended.shape),
+            whole(taps.shape),
+            whole((1, width)),
+            whole((1, width)),
+            by_cell(1),
             whole(w_in.shape),
             whole(w_out.shape),
             whole((1, width)),
             whole(heads.shape),
-        ],
-        out_specs=[rows(width), rows(fields)],
+        ]
+        + [pl.BlockSpec(memory_space=pl.ANY)] * len(early),
+        out_specs=[by_cell(width), by_cell(fields)],
         out_shape=[
             jax.ShapeDtypeStruct((cells, width), bf16),
             jax.ShapeDtypeStruct((cells, fields), f32),
         ],
+        scratch_shapes=[
+            pltpu.VMEM((rows + 2 * reach, span * tile, lane), bf16),
+            pltpu.VMEM((span * tile, lane), f32),
+            pltpu.VMEM((block * tile, lane), f32),
+            pltpu.VMEM((step, columns, width), f32),
+        ],
         compiler_params=pltpu.CompilerParams(vmem_limit_bytes=vmem_bytes),
         cost_estimate=pl.CostEstimate(
-            flops=4 * cells * width * w_in.shape[1],
+            flops=4 * cells * width * w_in.shape[1] + 100 * cells * width,
             bytes_accessed=8 * cells * width,
             transcendentals=cells * w_in.shape[1],
         ),
-    )(on, start, mask, w_in, w_out, scale[None], heads)
-
-
-def phases(count_first, count_second, length):
-    first_index = lax.broadcasted_iota(jnp.int32, (count_first, count_second), 0)
-    second_index = lax.broadcasted_iota(jnp.int32, (count_first, count_second), 1)
-    turns = first_index * second_index % length
-    return turns.astype(f32) * (2.0 * math.pi / length)
+    )(extended, taps, gain[None], shift[None], mask, w_in, w_out, scale[None], heads, *early)
 
 
 def lon_matrices(longitudes, bands):
     kept = longitudes // 2
     scale = 1.0 / math.sqrt(longitudes)
-    angles = phases(longitudes, kept, longitudes)
-    cos, sin = jnp.cos(angles) * scale, jnp.sin(angles) * scale
-    weight = jnp.where(lax.broadcasted_iota(jnp.int32, (1, kept), 1) == 0, 1.0, 2.0)
-    shape = (longitudes, bands, kept // bands, 1)
+    turns = np.arange(longitudes)[:, None] * np.arange(kept)[None] % longitudes
+    angles = turns * (2.0 * math.pi / longitudes)
+    cos, sin = np.cos(angles) * scale, np.sin(angles) * scale
+    weight = np.where(np.arange(kept) == 0, 1.0, 2.0)[None]
 
     def laid(re, im):
-        both = jnp.concatenate([re.reshape(shape), im.reshape(shape)], axis=-1)
-        return both.reshape(longitudes, -1).astype(bf16)
-
-    return laid(cos, -sin).T, laid(cos * weight, -sin * weight)
+        return np.stack([re, im], axis=-1).reshape(longitudes, -1)
+
+    fwd = np.ascontiguousarray(laid(cos, -sin).T)
+    back = laid(cos * weight, -sin * weight)
+    return jnp.asarray(fwd, bf16), jnp.asarray(back, bf16)
 
 
 def lat_matrices(lats, bands, halves, pair):
-    order = jnp.arange(lats).reshape(bands, halves, lats // (bands * halves * pair), pair)
-    order = order.transpose(1, 3, 0, 2).reshape(halves * pair, -1)
-    turns = jnp.arange(lats)[:, None] * order.reshape(1, lats) % lats
-    angles = turns.astype(f32) * (2.0 * math.pi / lats)
-    cos = jnp.cos(angles) / math.sqrt(lats)
-    sin = jnp.sin(angles) / math.sqrt(lats)
-    fwd = jnp.concatenate(
-        [jnp.concatenate([cos, sin], axis=1), jnp.concatenate([-sin, cos], axis=1)], axis=0
-    )
+    order = np.arange(lats).reshape(bands, halves, lats // (bands * halves * pair), pair)
+    order = order.transpose(1, 3, 0, 2).reshape(1, lats)
+    angles = (np.arange(lats)[:, None] * order % lats) * (2.0 * math.pi / lats)
+    cos = np.cos(angles) / math.sqrt(lats)
+    sin = np.sin(angles) / math.sqrt(lats)
+    fwd = np.block([[cos, sin], [-sin, cos]])
     cos_t = cos.T.reshape(halves * pair, -1, lats)
     sin_t = sin.T.reshape(halves * pair, -1, lats)
-    back = jnp.concatenate(
-        [
-            jnp.concatenate([cos_t, -sin_t], axis=2),
-            jnp.concatenate([sin_t, cos_t], axis=2),
-        ],
-        axis=1,
+    back = np.concatenate(
+        [np.concatenate([cos_t, -sin_t], axis=2), np.concatenate([sin_t, cos_t], axis=2)], axis=1
     ).reshape(2 * lats, 2 * lats)
-    return fwd.astype(bf16), back.astype(bf16)
+    return jnp.asarray(fwd, bf16), jnp.asarray(back, bf16)
 
 
 def dense_groups(weights):
@@ -557,21 +629,21 @@
     return [z.reshape(bands, count, parts, lanes) for z in zs]
 
 
-def with_halo(cells, sides, width, closed):
-    for axis, dim in sides:
-        count = lax.axis_size(axis)
-        ends = count if closed else count - 1
-        head = lax.slice_in_dim(cells, 0, width, axis=dim)
-        tail = lax.slice_in_dim(cells, cells.shape[dim] - width, cells.shape[dim], axis=dim)
-        cells = jnp.concatenate(
-            [
-                lax.ppermute(tail, axis, [(i, (i + 1) % count) for i in range(ends)]),
-                cells,
-                lax.ppermute(head, axis, [((i + 1) % count, i) for i in range(ends)]),
-            ],
-            axis=dim,
-        )
-    return cells
+def with_halo(cells, reach):
+    side = -(-reach // 8) * 8
+    count = lax.axis_size(quarter)
+    right = [(i, (i + 1) % count) for i in range(count)]
+    left = [((i + 1) % count, i) for i in range(count)]
+    before = lax.ppermute(cells[:, -reach:], quarter, right)
+    after = lax.ppermute(cells[:, :reach], quarter, left)
+    blank = jnp.zeros((cells.shape[0], side - reach, cells.shape[2]), cells.dtype)
+    wide = lambda r: jnp.concatenate([blank[r], before[r], cells[r], after[r], blank[r]], axis=1)
+    count = lax.axis_size("band")
+    down = [(i, i + 1) for i in range(count - 1)]
+    up = [(i + 1, i) for i in range(count - 1)]
+    above = lax.ppermute(wide(slice(-reach, None)), "band", down)
+    below = lax.ppermute(wide(slice(0, reach)), "band", up)
+    return jnp.concatenate([above, wide(slice(None)), below], axis=0)
 
 
 def on_device(
@@ -609,8 +681,9 @@
     lat_fwd, lat_back = lat_matrices(rows * bands, bands, halves, pair)
     weights = dense_groups(spec_weight)
     biases = spec_bias[:, :, :, None, :]
-    heads = lax.all_gather(flux_head, quarter, axis=0, tiled=True)
-    embed = lax.all_gather(patch_embed, quarter, axis=1, tiled=True)
+    heads = spread(flux_head, column_index, slots).reshape(-1, flux_head.shape[1])
+    embed = spread(patch_embed, column_index, slots).transpose(1, 0, 2)
+    embed = product_right(embed.reshape(patch_embed.shape[0], -1))
     gain = lambda b, i: norm_gain[b, i][None]
     shift = lambda b, i: norm_shift[b, i][None]
     cut = lambda x, h: lax.slice_in_dim(x, h * half, (h + 1) * half)
@@ -630,7 +703,7 @@
         lon_forward(streams[h], lon_fwd, bands, waves, pair, stats[h]) for h in range(halves)
     ]
     spectra = modes_of_bands(
-        spectra, lat_fwd, lat_back, weights[0], biases[0], pair, in0 + out0
+        spectra, lat_fwd, lat_back, weights[0], biases[0], pair, in0 + out0 + [heads, embed]
     )
     spectra = [to_band(z) for z in spectra]
     after_one, fluxes = [], []
@@ -648,54 +721,48 @@
     sea_cells = sea_mask.astype(f32)[..., None]
     forcing = jnp.einsum("ijf,fc->ijc", upsampled, flux_embed, precision=full_precision)
     start = (ocean_state.astype(f32) + sea_cells * forcing).astype(bf16)
-    widened = with_halo(start, ((quarter, 1),), 3, True)
-    extended = with_halo(widened, (("band", 0),), 3, False)
-    tile_rows = start.shape[0] // halves
+    reach = depth_kernel.shape[0] // 2
+    extended = with_halo(start, reach)
     tile_columns = start.shape[1]
+    pieces = 2 if halves == 2 and half % 2 == 0 else 1
+    tile_rows = start.shape[0] // (halves * pieces)
     cells = tile_rows * tile_columns
     nexts, surfaces, middles, spectra = [], [], [], []
     for h in range(halves):
-        first = h * tile_rows
-        convolved = jnp.zeros((tile_rows,) + start.shape[1:], f32)
-        for row_step in range(7):
-            for col_step in range(7):
-                convolved = (
-                    convolved
-                    + extended[
-                        first + row_step : first + row_step + tile_rows,
-                        col_step : col_step + tile_columns,
-                    ].astype(f32)
-                    * depth_kernel[row_step, col_step]
-                )
-        normed = layer_norm(convolved, ocean_gain, ocean_shift).astype(bf16)
-        ocean_next, surface = ocean_mlp(
-            normed.reshape(cells, -1),
-            start[first : first + tile_rows].reshape(cells, -1),
-            sea_cells[first : first + tile_rows].reshape(cells, 1),
-            ocean_in,
-            ocean_out,
-            layer_scale,
-            field_head,
-        )
-        nexts.append(ocean_next.reshape((tile_rows,) + start.shape[1:]))
-        surface = surface.reshape(tile_rows, tile_columns, -1)
-        surfaces.append(surface)
-        patches = (
-            surface.reshape(half, 2, part, 2, surface.shape[2])
-            .transpose(0, 2, 4, 1, 3)
-            .reshape(half * part, -1)
-        )
+        patches = []
+        for piece in range(pieces):
+            first = (h * pieces + piece) * tile_rows
+            ocean_next, surface = ocean_block(
+                extended[first : first + tile_rows + 2 * reach],
+                depth_kernel,
+                ocean_gain,
+                ocean_shift,
+                sea_cells[first : first + tile_rows].reshape(cells, 1),
+                ocean_in,
+                ocean_out,
+                layer_scale,
+                field_head,
+                spectra[:1] if piece == pieces - 1 else [],
+            )
+            nexts.append(ocean_next.reshape((tile_rows,) + start.shape[1:]))
+            surface = surface.reshape(tile_rows, tile_columns, -1)
+            surfaces.append(surface)
+            patches.append(
+                surface.reshape(tile_rows // 2, 2, part, 2, surface.shape[2])
+                .transpose(0, 2, 4, 1, 3)
+                .reshape(tile_rows // 2 * part, -1)
+            )
         middle, normed = make_middle(
             after_one[h],
-            product_left(patches),
-            product_right(embed),
+            product_left(jnp.concatenate(patches, axis=0)),
+            embed,
             gain(1, 0),
             shift(1, 0),
             slots,
+            part,
         )
         middles.append(middle)
-        normed = to_quarter(normed).reshape(slots, half, part, slot)
-        spectra.append(lon_forward(normed, lon_fwd, bands, waves, pair))
+        spectra.append(lon_forward(to_quarter(normed), lon_fwd, bands, waves, pair))
     ocean_next = jnp.concatenate(nexts, axis=0)
     surface = jnp.concatenate(surfaces, axis=0)
 
@@ -706,9 +773,9 @@
         restored = lon_back_call(spectra[h], lon_back, slots, pair)
         restored = to_quarter(restored).reshape(slots, half * part, slot)
         out = second_mlp(
-            middles[h], restored, gain(1, 0), shift(1, 0), gain(1, 1), shift(1, 1), in1, out1
+            middles[h], restored, gain(1, 0), shift(1, 0), gain(1, 1), shift(1, 1), in1, out1, part
         )
-        outs.append(to_quarter(out).reshape(slots, half, part, slot))
+        outs.append(to_quarter(out))
     return (assemble(outs), ocean_next, surface)
 
 

time: 1030 us -> 935 us (0.908)
  other arithmetic: 159 us -> 25.1 us
  Pallas kernels: 241 us -> 299 us
  blocking collectives: 53.8 us -> 33 us
    reduce_sum x2 -> x0, other arithmetic: 117 us -> none  [layer_norm(): average = jnp.mean(values, axis=-1, keepdims=True)]
    pallas_call x2 -> x4, Pallas kernels: 37 us -> 94.2 us  [ocean_block(): pl.pallas_call(kernel, grid=(rows // step,), in_specs=[whole(extended.sha...]
    all_gather x2 -> x0, blocking collectives: 53.8 us -> none  [the longest x1 28.9 us: on_device(): embed = lax.all_gather(patch_embed, quarter, axis=1, tiled=True)]
    all_to_all x0 -> x1, blocking collectives: none -> 33 us  [to_quarter(): return lax.all_to_all(x, quarter, split_axis=0, concat_axis=0, tiled=True)]
    concatenate x3 -> x4, local copies, waits for them, and re-layouts: 2.89 us -> 28.5 us  [the longest x3 27.7 us: with_halo(): jnp.concatenate([blank[r], before[r], cells[r], after[r], blank[r]], axis=1)]
    ppermute x12, waiting for transfers between devices: 50.4 us -> 28.3 us  [gathered(): lax.ppermute(part, axis, [(i, (i + d) % n) for i in range(n)])]
    all_to_all x8 -> x7, waiting for transfers between devices: 46.4 us -> 66.4 us  [to_quarter(): return lax.all_to_all(x, quarter, split_axis=0, concat_axis=0, tiled=True)]
    pallas_call x4 -> x0, local copies, waits for them, and re-layouts: 16.7 us -> none  [the longest x2 8.42 us: second_mlp(): pl.pallas_call(functools.partial(second_mlp_kernel, n), grid=(tokens // t...]
  transfers between devices with their start and end apart: 34 -> 37, of which waited for: 19 -> 22; matrix products, arithmetic and copies ran while one was open for 10% -> 10% of each run, Pallas kernels for 14% -> 14%
where the time goes in v3:
time: 935 us; the launch traced here: 926 us
  waiting for transfers between devices  348 us (37%)
  Pallas kernels  299 us (32%)
  local copies, waits for them, and re-layouts  123 us (13%)
  starting transfers between devices  85.1 us (9%)
  blocking collectives  33 us (4%)
  other arithmetic  25.1 us (3%)
  matrix products  11.3 us (1%)
    all_to_all x8, waiting for transfers between devices, to_band(): return lax.all_to_all(x, 'band', split_axis=0, concat_axis=0, tiled=True)  240 us
    pallas_call x4, Pallas kernels, ocean_block(): pl.pallas_call(kernel, grid=(rows // step,), in_specs=[whole(extended.sha...  94.2 us
    all_to_all x7, waiting for transfers between devices, to_quarter(): return lax.all_to_all(x, quarter, split_axis=0, concat_axis=0, tiled=True)  66.4 us
    pallas_call x2, Pallas kernels, second_mlp(): pl.pallas_call(functools.partial(second_mlp_kernel, n), grid=(tokens // t...  47 us
    pallas_call x2, Pallas kernels, first_mlp(): pl.pallas_call(functools.partial(first_mlp_kernel, n), grid=(tokens // ti...  44.8 us
    pallas_call x2, Pallas kernels, mix_modes(): pl.pallas_call(kernel, grid=(waves // step,), in_specs=[pl.BlockSpec((2 *...  44 us
    all_to_all x8, starting transfers between devices, to_band(): return lax.all_to_all(x, 'band', split_axis=0, concat_axis=0, tiled=True)  36.5 us
    all_to_all x1, blocking collectives, to_quarter(): return lax.all_to_all(x, quarter, split_axis=0, concat_axis=0, tiled=True)  33 us
  transfers between devices with their start and end apart: 37, of which 22 were waited for; matrix products, arithmetic and copies ran while one was open for 10% of the time, Pallas kernels for 14%

profile of v3, /device:TPU:0, one launch (start us, length us, event | category | flops | bytes accessed | tf_op | source)
XLA Modules:
  0.0 926.0 jit_solution(6452840309671831794)
XLA Ops:
  19.7 7.4 shard_map.239
  27.1 6.0 all-to-all-start.1
  40.3 7.4 shard_map.238
  47.7 26.2 %all-to-all-done.1 = bf16[8,6,48,384]{3,2,1,0:T(8,128)(2,1)S(1)} async-done(((bf16[8,6,48,384]{3,2,1,0:T(8,128)(2,1)}), bf16[8,6,48,384]{3,2,1,0:T(8,128)(2,1)S(1)}, u32[]{:S(2)}, u32[]{:S(2)}) %all-to-all-start.1) | async-done | bytes 1769504 | tf_op jit(solution)/shard_map/all_to_all | solution.py:616
  89.7 19.3 %collective-permute-done.5.refs_11_.refs_5_ = bf16[768,768]{1,0:T(8,128)(2,1)} collective-permute-done((bf16[768,768]{1,0:T(8,128)(2,1)}, bf16[768,768]{1,0:T(8,128)(2,1)}, u32[]{:S(2)}, u32[]{:S(2)}) %collective-permute-start.5) | collective-permute-done | bytes 1179680 | tf_op jit(solution)/shard_map/ppermute | solution.py:102
  110.8 5.7 collective-permute-done.9
  127.7 22.1 %shard_map.240 = (bf16[24,96,384]{2,1,0:T(8,128)(2,1)}, bf16[24,96,384]{2,1,0:T(8,128)(2,1)}) custom-call(bf16[48,48,384]{2,1,0:T(8,128)(2,1)} %copy.132.refs_0_, bf16[48,48,384]{2,1,0:T(8,128)(2,1)} %copy.133.refs_1_, bf16[384,384]{1,0:T(8,128)(2,1)} %constant.52.clone.refs_2_, bf16[384,384]{1,0:T(8,128)(2,1)} %constant.53.clone.refs_3_, ...), custom_call_target="tpu_custom_call" | custom-call | flops 5435817984 | bytes 7077888 | tf_op jit(solution)/shard_map/pallas_call | solution.py:285
  155.8 5.8 all-to-all-start.4
  166.2 35.5 %all-to-all-done.4.refs_0_ = bf16[8,6,48,384]{3,2,1,0:T(8,128)(2,1)S(1)} async-done(((bf16[8,6,48,384]{3,2,1,0:T(8,128)(2,1)}), bf16[8,6,48,384]{3,2,1,0:T(8,128)(2,1)S(1)}, u32[]{:S(2)}, u32[]{:S(2)}) %all-to-all-start.4) | async-done | bytes 1769504 | tf_op jit(solution)/shard_map/all_to_all | solution.py:616
  208.6 7.5 shard_map.243
  216.1 31.7 %all-to-all-done.2.refs_0_ = bf16[8,6,48,384]{3,2,1,0:T(8,128)(2,1)S(1)} async-done(((bf16[8,6,48,384]{3,2,1,0:T(8,128)(2,1)}), bf16[8,6,48,384]{3,2,1,0:T(8,128)(2,1)S(1)}, u32[]{:S(2)}, u32[]{:S(2)}) %all-to-all-start.2) | async-done | bytes 1769504 | tf_op jit(solution)/shard_map/all_to_all | solution.py:616
  249.0 5.0 all-to-all-start.5
  255.1 6.0 collective-permute-done.15.refs_11_.refs_5_
  265.2 7.5 shard_map.241
  272.6 12.3 %all-to-all-done.5 = bf16[4,12,96,192]{3,2,1,0:T(8,128)(2,1)} async-done(((bf16[4,12,96,192]{3,2,1,0:T(8,128)(2,1)}), bf16[4,12,96,192]{3,2,1,0:T(8,128)(2,1)}, u32[]{:S(2)}, u32[]{:S(2)}) %all-to-all-start.5) | async-done | bytes 1769504 | tf_op jit(solution)/shard_map/all_to_all | solution.py:620
  288.6 22.4 %shard_map.244 = (bf16[1152,768]{1,0:T(8,128)(2,1)}, f32[1152,8]{1,0:T(8,128)}) custom-call(bf16[4,1152,192]{2,1,0:T(8,128)(2,1)} %bitcast.24.u_ref, f32[1,768]{1,0:T(1,128)} %get-tuple-element.94.gain, f32[1,768]{1,0:T(1,128)} %get-tuple-element.90.shift, bf16[768,8]{1,0:T(8,128)(2,1)} %bitcast.148, bf16[768,768]{1,0:T(8,128)(2,1)} %get-tuple-element.70.refs_6_.refs_0_, ...), custom_call_target="tpu_custom_call" | custom-call | flops 10871635968 | bytes 12976128 | tf_op jit(solution)/shard_map/pallas_call | solution.py:135
  312.3 4.7 all-to-all-done.3
  318.4 22.4 %shard_map.242 = (bf16[1152,768]{1,0:T(8,128)(2,1)}, f32[1152,8]{1,0:T(8,128)}) custom-call(bf16[4,1152,192]{2,1,0:T(8,128)(2,1)} %bitcast.131, f32[1,768]{1,0:T(1,128)} %get-tuple-element.94.gain, f32[1,768]{1,0:T(1,128)} %get-tuple-element.90.shift, bf16[768,8]{1,0:T(8,128)(2,1)} %bitcast.149, bf16[768,768]{1,0:T(8,128)(2,1)} %get-tuple-element.70.refs_6_.refs_0_, ...), custom_call_target="tpu_custom_call" | custom-call | flops 10871635968 | bytes 12976128 | tf_op jit(solution)/shard_map/pallas_call | solution.py:135
  342.8 11.3 %add_convert_fusion = bf16[48,192,256]{2,1,0:T(8,128)(2,1)S(1)} fusion(bf16[48,192,256]{2,1,0:T(8,128)(2,1)} %param.32, f32[48,192]{1,0:T(8,128)S(1)} %convert_element_type.52, f32[48,192,8]{1,2,0:T(8,128)S(1)} %copy.141, f32[8,256]{1,0:T(8,128)S(1)} %copy-done), kind=kOutput, calls=%fused_computation | convolution fusion | flops 235929600 | bytes 9777152 | tf_op jit(solution)/shard_map/ijf,fc->ijc/dot_general | solution.py:722
  362.1 4.6 collective-permute-start.20
  371.8 27.4 %concatenate.54 = bf16[48,208,256]{2,1,0:T(8,128)(2,1)} concatenate(bf16[48,5,256]{2,1,0:T(8,128)(2,1)S(1)} %broadcast_in_dim.111, bf16[48,3,256]{2,1,0:T(4,128)(2,1)S(1)} %collective-permute-done.18, bf16[48,192,256]{2,1,0:T(8,128)(2,1)} %copy-done.2, bf16[48,3,256]{2,1,0:T(4,128)(2,1)S(1)} %collective-permute-done.19, bf16[48,5,256]{2,1,0:T(8,128)(2,1)S(1)} %broadcast_in_dim.111), dimensions={1} | concatenate | bytes 10223616 | tf_op jit(solution)/shard_map/concatenate | solution.py:640
  399.1 5.3 fusion.16
  405.3 23.5 %shard_map.245 = (bf16[2304,256]{1,0:T(8,128)(2,1)}, f32[2304,4]{1,0:T(8,128)}) custom-call(bf16[18,208,256]{2,1,0:T(8,128)(2,1)} %get-tuple-element.58.refs_0_, bf16[49,16,128]{2,1,0:T(8,128)(2,1)} %bitcast.143, f32[1,256]{1,0:T(1,128)} %bitcast.152, f32[1,256]{1,0:T(1,128)} %bitcast.156, f32[2304,1]{1,0:T(8,128)} %reshape.220.refs_4_, ...), custom_call_target="tpu_custom_call" | custom-call | flops 2474901504 | bytes 4718592 | tf_op jit(solution)/shard_map/pallas_call | solution.py:540
  430.5 23.5 %shard_map.246 = (bf16[2304,256]{1,0:T(8,128)(2,1)}, f32[2304,4]{1,0:T(8,128)}) custom-call(bf16[18,208,256]{2,1,0:T(8,128)(2,1)} %get-tuple-element.59.refs_0_, bf16[49,16,128]{2,1,0:T(8,128)(2,1)} %bitcast.144, f32[1,256]{1,0:T(1,128)} %bitcast.153, f32[1,256]{1,0:T(1,128)} %bitcast.157, f32[2304,1]{1,0:T(8,128)} %reshape.221.refs_4_, ...), custom_call_target="tpu_custom_call" | custom-call | flops 2474901504 | bytes 4718592 | tf_op jit(solution)/shard_map/pallas_call | solution.py:540
  456.8 5.0 shard_map.247
  469.9 23.5 %shard_map.249 = (bf16[2304,256]{1,0:T(8,128)(2,1)}, f32[2304,4]{1,0:T(8,128)}) custom-call(bf16[18,208,256]{2,1,0:T(8,128)(2,1)} %get-tuple-element.57.refs_0_, bf16[49,16,128]{2,1,0:T(8,128)(2,1)} %bitcast.145, f32[1,256]{1,0:T(1,128)} %bitcast.154, f32[1,256]{1,0:T(1,128)} %bitcast.158, f32[2304,1]{1,0:T(8,128)} %reshape.222.refs_4_, ...), custom_call_target="tpu_custom_call" | custom-call | flops 2474901504 | bytes 4718592 | tf_op jit(solution)/shard_map/pallas_call | solution.py:540
  496.5 5.9 shard_map.248.refs_9_
  502.4 23.6 %shard_map.250 = (bf16[2304,256]{1,0:T(8,128)(2,1)}, f32[2304,4]{1,0:T(8,128)}) custom-call(bf16[18,208,256]{2,1,0:T(8,128)(2,1)} %get-tuple-element.60.refs_0_, bf16[49,16,128]{2,1,0:T(8,128)(2,1)} %bitcast.146, f32[1,256]{1,0:T(1,128)} %bitcast.155, f32[1,256]{1,0:T(1,128)} %bitcast.159, f32[2304,1]{1,0:T(8,128)} %reshape.223.refs_4_, ...), custom_call_target="tpu_custom_call" | custom-call | flops 2474901504 | bytes 4718592 | tf_op jit(solution)/shard_map/pallas_call | solution.py:540
  528.7 5.1 shard_map.251
  533.8 33.0 %all_to_all.80.refs_0_ = bf16[4,12,96,192]{3,2,1,0:T(8,128)(2,1)} all-to-all(bf16[4,12,96,192]{3,2,1,0:T(8,128)(2,1)} %get-tuple-element.35), channel_id=1, replica_groups=mesh['band'=8,'comp'=2,'tile'=2] {'comp','tile'}, dimensions={0} | all-to-all | bytes 3538944 | tf_op jit(solution)/shard_map/all_to_all | solution.py:620
  566.8 5.7 all-to-all-start.7
  572.5 5.9 shard_map.252
  578.4 34.9 %all-to-all-done.7 = bf16[8,6,48,384]{3,2,1,0:T(8,128)(2,1)S(1)} async-done(((bf16[8,6,48,384]{3,2,1,0:T(8,128)(2,1)}), bf16[8,6,48,384]{3,2,1,0:T(8,128)(2,1)S(1)}, u32[]{:S(2)}, u32[]{:S(2)}) %all-to-all-start.7) | async-done | bytes 1769504 | tf_op jit(solution)/shard_map/all_to_all | solution.py:616
  619.6 39.2 %all-to-all-done.9 = bf16[8,6,48,384]{3,2,1,0:T(8,128)(2,1)S(1)} async-done(((bf16[8,6,48,384]{3,2,1,0:T(8,128)(2,1)}), bf16[8,6,48,384]{3,2,1,0:T(8,128)(2,1)S(1)}, u32[]{:S(2)}, u32[]{:S(2)}) %all-to-all-start.9) | async-done | bytes 1769504 | tf_op jit(solution)/shard_map/all_to_all | solution.py:616
  660.3 22.0 %shard_map.253 = (bf16[24,96,384]{2,1,0:T(8,128)(2,1)}, bf16[24,96,384]{2,1,0:T(8,128)(2,1)}) custom-call(bf16[48,48,384]{2,1,0:T(8,128)(2,1)} %copy.157.refs_0_, bf16[48,48,384]{2,1,0:T(8,128)(2,1)} %copy.158.refs_1_, bf16[384,384]{1,0:T(8,128)(2,1)} %constant.52.clone.refs_2_, bf16[384,384]{1,0:T(8,128)(2,1)} %constant.53.clone.refs_3_, ...), custom_call_target="tpu_custom_call" | custom-call | flops 5435817984 | bytes 7077888 | tf_op jit(solution)/shard_map/pallas_call | solution.py:285
  696.6 36.9 %all-to-all-done.13.refs_0_ = bf16[8,6,48,384]{3,2,1,0:T(8,128)(2,1)S(1)} async-done(((bf16[8,6,48,384]{3,2,1,0:T(8,128)(2,1)}), bf16[8,6,48,384]{3,2,1,0:T(8,128)(2,1)S(1)}, u32[]{:S(2)}, u32[]{:S(2)}) %all-to-all-start.13) | async-done | bytes 1769504 | tf_op jit(solution)/shard_map/all_to_all | solution.py:616
  738.3 5.9 shard_map.256
  744.2 35.5 %all-to-all-done.10.refs_0_ = bf16[8,6,48,384]{3,2,1,0:T(8,128)(2,1)S(1)} async-done(((bf16[8,6,48,384]{3,2,1,0:T(8,128)(2,1)}), bf16[8,6,48,384]{3,2,1,0:T(8,128)(2,1)S(1)}, u32[]{:S(2)}, u32[]{:S(2)}) %all-to-all-start.10) | async-done | bytes 1769504 | tf_op jit(solution)/shard_map/all_to_all | solution.py:616
  781.0 4.5 all-to-all-start.14
  785.5 5.9 shard_map.254
  791.5 22.6 %all-to-all-done.14 = bf16[4,12,96,192]{3,2,1,0:T(8,128)(2,1)} async-done(((bf16[4,12,96,192]{3,2,1,0:T(8,128)(2,1)}), bf16[4,12,96,192]{3,2,1,0:T(8,128)(2,1)}, u32[]{:S(2)}, u32[]{:S(2)}) %all-to-all-start.14) | async-done | bytes 1769504 | tf_op jit(solution)/shard_map/all_to_all | solution.py:620
  817.9 23.5 %shard_map.257 = bf16[4,12,96,192]{3,2,1,0:T(8,128)(2,1)} custom-call(bf16[1152,768]{1,0:T(8,128)(2,1)} %get-tuple-element.37.v_ref, bf16[4,1152,192]{2,1,0:T(8,128)(2,1)} %bitcast.56.r_ref, f32[1,768]{1,0:T(1,128)} %get-tuple-element.96.gain.gain0, f32[1,768]{1,0:T(1,128)} %get-tuple-element.92.shift.shift0, f32[1,768]{1,0:T(1,128)} %get-tuple-element.93.gain, ...), custom_call_target="tpu_custom_call" | custom-call | flops 10871635968 | bytes 14745600 | tf_op jit(solution)/shard_map/pallas_call | solution.py:180
  841.4 5.0 all-to-all-done.11
  851.4 23.5 %shard_map.255 = bf16[4,12,96,192]{3,2,1,0:T(8,128)(2,1)} custom-call(bf16[1152,768]{1,0:T(8,128)(2,1)} %get-tuple-element.30.v_ref, bf16[4,1152,192]{2,1,0:T(8,128)(2,1)} %bitcast.130, f32[1,768]{1,0:T(1,128)} %get-tuple-element.96.gain.gain0, f32[1,768]{1,0:T(1,128)} %get-tuple-element.92.shift.shift0, f32[1,768]{1,0:T(1,128)} %get-tuple-element.93.gain, ...), custom_call_target="tpu_custom_call" | custom-call | flops 10871635968 | bytes 14745600 | tf_op jit(solution)/shard_map/pallas_call | solution.py:180
  874.9 4.9 all-to-all-done.15.refs_1_
  897.5 16.8 %all-to-all-done.12.refs_0_ = bf16[4,12,96,192]{3,2,1,0:T(8,128)(2,1)} async-done(((bf16[4,12,96,192]{3,2,1,0:T(8,128)(2,1)}), bf16[4,12,96,192]{3,2,1,0:T(8,128)(2,1)}, u32[]{:S(2)}, u32[]{:S(2)}) %all-to-all-start.12) | async-done | bytes 1769504 | tf_op jit(solution)/shard_map/all_to_all | solution.py:620
  914.4 5.1 shard_map.258
  919.4 6.4 copy.167
  (226 shorter events, 173.7 us)
Async XLA Ops:
  0.6 342.2 %copy-start = (f32[8,256]{1,0:T(8,128)S(1)}, f32[8,256]{1,0:T(8,128)}, u32[]{:S(2)}) copy-start(f32[8,256]{1,0:T(8,128)} %param.31) | copy-start | bytes 24580
  4.7 5.9 collective-permute-start
  11.5 5.5 collective-permute-start.1
  27.1 46.9 %all-to-all-start.1 = ((bf16[8,6,48,384]{3,2,1,0:T(8,128)(2,1)}), bf16[8,6,48,384]{3,2,1,0:T(8,128)(2,1)S(1)}, u32[]{:S(2)}, u32[]{:S(2)}) async-start(bf16[8,6,48,384]{3,2,1,0:T(8,128)(2,1)} %shard_map.239), calls=%async_computation.1 | async-start | bytes 3538944 | tf_op jit(solution)/shard_map/all_to_all | solution.py:616
  36.3 52.9 %collective-permute-start.2 = (bf16[768,768]{1,0:T(8,128)(2,1)}, bf16[768,768]{1,0:T(8,128)(2,1)}, u32[]{:S(2)}, u32[]{:S(2)}) collective-permute-start(bf16[768,768]{1,0:T(8,128)(2,1)} %get-tuple-element.70.refs_6_.refs_0_), channel_id=1, source_target_pairs={{0,2},{2,0},{1,3},{3,1},{4,6},{6,4},{5,7},{7,5},{8,10},{10,8},{9,1... | collective-permute-start | bytes 3538952 | tf_op jit(solution)/shard_map/ppermute | solution.py:102
  37.8 89.8 %collective-permute-start.3 = (bf16[768,768]{1,0:T(8,128)(2,1)}, bf16[768,768]{1,0:T(8,128)(2,1)}, u32[]{:S(2)}, u32[]{:S(2)}) collective-permute-start(bf16[768,768]{1,0:T(8,128)(2,1)} %get-tuple-element.70.refs_6_.refs_0_), channel_id=1, source_target_pairs={{0,1},{1,0},{2,3},{3,2},{4,5},{5,4},{6,7},{7,6},{8,9},{9,8},{10,11... | collective-permute-start | bytes 3538952 | tf_op jit(solution)/shard_map/ppermute | solution.py:102
  73.9 52.1 %all-to-all-start = ((bf16[8,6,48,384]{3,2,1,0:T(8,128)(2,1)}), bf16[8,6,48,384]{3,2,1,0:T(8,128)(2,1)S(1)}, u32[]{:S(2)}, u32[]{:S(2)}) async-start(bf16[8,6,48,384]{3,2,1,0:T(8,128)(2,1)} %shard_map.238), calls=%async_computation | async-start | bytes 3538944 | tf_op jit(solution)/shard_map/all_to_all | solution.py:616
  81.1 27.9 %collective-permute-start.5 = (bf16[768,768]{1,0:T(8,128)(2,1)}, bf16[768,768]{1,0:T(8,128)(2,1)}, u32[]{:S(2)}, u32[]{:S(2)}) collective-permute-start(bf16[768,768]{1,0:T(8,128)(2,1)} %get-tuple-element.68.refs_10_.refs_4_), channel_id=1, source_target_pairs={{0,2},{2,0},{1,3},{3,1},{4,6},{6,4},{5,7},{7,5},{8,10},{10,8},{9,1... | collective-permute-start | bytes 3538952 | tf_op jit(solution)/shard_map/ppermute | solution.py:102
  82.6 45.1 %collective-permute-start.6 = (bf16[768,768]{1,0:T(8,128)(2,1)}, bf16[768,768]{1,0:T(8,128)(2,1)}, u32[]{:S(2)}, u32[]{:S(2)}) collective-permute-start(bf16[768,768]{1,0:T(8,128)(2,1)} %get-tuple-element.68.refs_10_.refs_4_), channel_id=1, source_target_pairs={{0,1},{1,0},{2,3},{3,2},{4,5},{5,4},{6,7},{7,6},{8,9},{9,8},{10,11... | collective-permute-start | bytes 3538952 | tf_op jit(solution)/shard_map/ppermute | solution.py:102
  83.3 25.7 %copy-start.24 = (bf16[192,8]{1,0:T(8,128)(2,1)S(1)}, bf16[192,8]{1,0:T(8,128)(2,1)}, u32[]{:S(2)}) copy-start(bf16[192,8]{1,0:T(8,128)(2,1)} %copy.131) | copy-start | bytes 9220
  84.3 4.9 collective-permute-start.8
  85.8 24.8 %copy-start.27 = (f32[16,192]{1,0:T(8,128)S(1)}, f32[16,192]{1,0:T(8,128)}, u32[]{:S(2)}) copy-start(f32[16,192]{1,0:T(8,128)} %param.41) | copy-start | bytes 36868
  89.2 19.9 %collective-permute-start.10 = (f32[4,16,192]{2,0,1:T(4,128)S(1)}, f32[4,16,192]{2,0,1:T(4,128)S(1)}, u32[]{:S(2)}, u32[]{:S(2)}) collective-permute-start(f32[4,16,192]{2,0,1:T(4,128)S(1)} %broadcast_select_fusion.1), channel_id=1, source_target_pairs={{0,1},{1,0},{2,3},{3,2},{4,5},{5,4},{6,7},{7,6},{8,9},{9,8},{10,11... | collective-permute-start | bytes 147464 | tf_op jit(solution)/shard_map/ppermute | solution.py:88
  89.2 38.5 %collective-permute-start.4 = (bf16[768,768]{1,0:T(8,128)(2,1)}, bf16[768,768]{1,0:T(8,128)(2,1)}, u32[]{:S(2)}, u32[]{:S(2)}) collective-permute-start(bf16[768,768]{1,0:T(8,128)(2,1)} %collective-permute-done.2.refs_7_.refs_1_), channel_id=1, source_target_pairs={{0,1},{1,0},{2,3},{3,2},{4,5},{5,4},{6,7},{7,6},{8,9},{9,8},{10,11... | collective-permute-start | bytes 3538952 | tf_op jit(solution)/shard_map/ppermute | solution.py:102
  109.0 18.7 %collective-permute-start.7 = (bf16[768,768]{1,0:T(8,128)(2,1)}, bf16[768,768]{1,0:T(8,128)(2,1)}, u32[]{:S(2)}, u32[]{:S(2)}) collective-permute-start(bf16[768,768]{1,0:T(8,128)(2,1)} %collective-permute-done.5.refs_11_.refs_5_), channel_id=1, source_target_pairs={{0,1},{1,0},{2,3},{3,2},{4,5},{5,4},{6,7},{7,6},{8,9},{9,8},{10,11... | collective-permute-start | bytes 3538952 | tf_op jit(solution)/shard_map/ppermute | solution.py:102
  109.1 7.4 collective-permute-start.9
  116.5 4.3 collective-permute-start.11
  155.8 5.8 copy-start.17
  155.8 45.9 %all-to-all-start.4 = ((bf16[8,6,48,384]{3,2,1,0:T(8,128)(2,1)}), bf16[8,6,48,384]{3,2,1,0:T(8,128)(2,1)S(1)}, u32[]{:S(2)}, u32[]{:S(2)}) async-start(bf16[8,6,48,384]{3,2,1,0:T(8,128)(2,1)} %reshape.190), calls=%async_computation.4 | async-start | bytes 3538944 | tf_op jit(solution)/shard_map/all_to_all | solution.py:616
  202.9 44.9 %all-to-all-start.2 = ((bf16[8,6,48,384]{3,2,1,0:T(8,128)(2,1)}), bf16[8,6,48,384]{3,2,1,0:T(8,128)(2,1)S(1)}, u32[]{:S(2)}, u32[]{:S(2)}) async-start(bf16[8,6,48,384]{3,2,1,0:T(8,128)(2,1)} %reshape.186), calls=%async_computation.2 | async-start | bytes 3538944 | tf_op jit(solution)/shard_map/all_to_all | solution.py:616
  206.5 48.1 %collective-permute-start.12 = (bf16[768,768]{1,0:T(8,128)(2,1)}, bf16[768,768]{1,0:T(8,128)(2,1)}, u32[]{:S(2)}, u32[]{:S(2)}) collective-permute-start(bf16[768,768]{1,0:T(8,128)(2,1)} %get-tuple-element.69.refs_6_.refs_0_), channel_id=1, source_target_pairs={{0,2},{2,0},{1,3},{3,1},{4,6},{6,4},{5,7},{7,5},{8,10},{10,8},{9,1... | collective-permute-start | bytes 3538952 | tf_op jit(solution)/shard_map/ppermute | solution.py:102
  208.1 53.0 %collective-permute-start.15 = (bf16[768,768]{1,0:T(8,128)(2,1)}, bf16[768,768]{1,0:T(8,128)(2,1)}, u32[]{:S(2)}, u32[]{:S(2)}) collective-permute-start(bf16[768,768]{1,0:T(8,128)(2,1)} %get-tuple-element.67.refs_10_.refs_4_), channel_id=1, source_target_pairs={{0,2},{2,0},{1,3},{3,1},{4,6},{6,4},{5,7},{7,5},{8,10},{10,8},{9,1... | collective-permute-start | bytes 3538952 | tf_op jit(solution)/shard_map/ppermute | solution.py:102
  216.1 37.9 %copy-start.10 = (bf16[768,768]{1,0:T(8,128)(2,1)S(1)}, bf16[768,768]{1,0:T(8,128)(2,1)}, u32[]{:S(2)}) copy-start(bf16[768,768]{1,0:T(8,128)(2,1)} %get-tuple-element.69.refs_6_.refs_0_) | copy-start | bytes 3538948
  249.0 35.9 %all-to-all-start.5 = ((bf16[4,12,96,192]{3,2,1,0:T(8,128)(2,1)}), bf16[4,12,96,192]{3,2,1,0:T(8,128)(2,1)}, u32[]{:S(2)}, u32[]{:S(2)}) async-start(bf16[4,12,96,192]{3,2,1,0:T(8,128)(2,1)} %shard_map.243), calls=%async_computation.5 | async-start | bytes 4718592 | tf_op jit(solution)/shard_map/all_to_all | solution.py:620
  254.0 7.0 collective-permute-start.13
  254.6 6.5 collective-permute-start.16
  254.7 6.6 collective-permute-start.14
  261.1 3.1 collective-permute-start.17
  272.6 15.9 %copy-start.29 = (s32[48,192]{1,0:T(8,128)S(1)}, s32[48,192]{1,0:T(8,128)}, u32[]{:S(2)}) copy-start(s32[48,192]{1,0:T(8,128)} %param.33) | copy-start | bytes 110596
  272.6 15.9 %copy-start.33 = (f32[256,4]{0,1:T(4,128)S(1)}, f32[256,4]{0,1:T(4,128)}, u32[]{:S(2)}) copy-start(f32[256,4]{0,1:T(4,128)} %param.40) | copy-start | bytes 12292
  284.9 32.1 %all-to-all-start.3 = ((bf16[4,12,96,192]{3,2,1,0:T(8,128)(2,1)}), bf16[4,12,96,192]{3,2,1,0:T(8,128)(2,1)S(1)}, u32[]{:S(2)}, u32[]{:S(2)}) async-start(bf16[4,12,96,192]{3,2,1,0:T(8,128)(2,1)} %shard_map.241), calls=%async_computation.3 | async-start | bytes 4718592 | tf_op jit(solution)/shard_map/all_to_all | solution.py:620
  354.2 15.3 %copy-start.28 = (f32[7,7,256]{2,1,0:T(8,128)S(1)}, f32[7,7,256]{2,1,0:T(8,128)}, u32[]{:S(2)}) copy-start(f32[7,7,256]{2,1,0:T(8,128)} %param.34) | copy-start | bytes 150532
  354.2 2.3 collective-permute-start.19
  356.4 4.1 collective-permute-start.18
  360.6 38.5 %collective-permute-start.21 = (bf16[3,208,256]{2,1,0:T(8,128)(2,1)S(1)}, bf16[3,208,256]{2,1,0:T(8,128)(2,1)S(1)}, u32[]{:S(2)}, u32[]{:S(2)}) collective-permute-start(bf16[3,208,256]{2,1,0:T(8,128)(2,1)S(1)} %concatenate.59), channel_id=1, source_target_pairs={{4,0},{8,4},{12,8},{16,12},{20,16},{24,20},{28,24},{5,1},{9,5},{13... | collective-permute-start | bytes 958472 | tf_op jit(solution)/shard_map/ppermute | solution.py:645
  362.1 37.1 %collective-permute-start.20 = (bf16[3,208,256]{2,1,0:T(8,128)(2,1)S(1)}, bf16[3,208,256]{2,1,0:T(8,128)(2,1)S(1)}, u32[]{:S(2)}, u32[]{:S(2)}) collective-permute-start(bf16[3,208,256]{2,1,0:T(8,128)(2,1)S(1)} %concatenate.53), channel_id=1, source_target_pairs={{0,4},{4,8},{8,12},{12,16},{16,20},{20,24},{24,28},{1,5},{5,9},{9,... | collective-permute-start | bytes 958472 | tf_op jit(solution)/shard_map/ppermute | solution.py:644
  461.8 33.3 %all-to-all-start.6 = ((bf16[4,12,96,192]{3,2,1,0:T(8,128)(2,1)}), bf16[4,12,96,192]{3,2,1,0:T(8,128)(2,1)S(1)}, u32[]{:S(2)}, u32[]{:S(2)}) async-start(bf16[4,12,96,192]{3,2,1,0:T(8,128)(2,1)} %get-tuple-element.31), calls=%async_computation.6 | async-start | bytes 4718592 | tf_op jit(solution)/shard_map/all_to_all | solution.py:620
  566.8 46.6 %all-to-all-start.7 = ((bf16[8,6,48,384]{3,2,1,0:T(8,128)(2,1)}), bf16[8,6,48,384]{3,2,1,0:T(8,128)(2,1)S(1)}, u32[]{:S(2)}, u32[]{:S(2)}) async-start(bf16[8,6,48,384]{3,2,1,0:T(8,128)(2,1)} %shard_map.248.refs_9_), calls=%async_computation.7 | async-start | bytes 3538944 | tf_op jit(solution)/shard_map/all_to_all | solution.py:616
  613.3 45.4 %all-to-all-start.9 = ((bf16[8,6,48,384]{3,2,1,0:T(8,128)(2,1)}), bf16[8,6,48,384]{3,2,1,0:T(8,128)(2,1)S(1)}, u32[]{:S(2)}, u32[]{:S(2)}) async-start(bf16[8,6,48,384]{3,2,1,0:T(8,128)(2,1)} %shard_map.252), calls=%async_computation.9 | async-start | bytes 3538944 | tf_op jit(solution)/shard_map/all_to_all | solution.py:616
  688.3 45.2 %all-to-all-start.13 = ((bf16[8,6,48,384]{3,2,1,0:T(8,128)(2,1)}), bf16[8,6,48,384]{3,2,1,0:T(8,128)(2,1)S(1)}, u32[]{:S(2)}, u32[]{:S(2)}) async-start(bf16[8,6,48,384]{3,2,1,0:T(8,128)(2,1)} %reshape.209), calls=%async_computation.13 | async-start | bytes 3538944 | tf_op jit(solution)/shard_map/all_to_all | solution.py:616
  734.7 45.0 %all-to-all-start.10 = ((bf16[8,6,48,384]{3,2,1,0:T(8,128)(2,1)}), bf16[8,6,48,384]{3,2,1,0:T(8,128)(2,1)S(1)}, u32[]{:S(2)}, u32[]{:S(2)}) async-start(bf16[8,6,48,384]{3,2,1,0:T(8,128)(2,1)} %reshape.206), calls=%async_computation.10 | async-start | bytes 3538944 | tf_op jit(solution)/shard_map/all_to_all | solution.py:616
  781.0 33.1 %all-to-all-start.14 = ((bf16[4,12,96,192]{3,2,1,0:T(8,128)(2,1)}), bf16[4,12,96,192]{3,2,1,0:T(8,128)(2,1)}, u32[]{:S(2)}, u32[]{:S(2)}) async-start(bf16[4,12,96,192]{3,2,1,0:T(8,128)(2,1)} %shard_map.256), calls=%async_computation.14 | async-start | bytes 4718592 | tf_op jit(solution)/shard_map/all_to_all | solution.py:620
  814.1 32.3 %all-to-all-start.11 = ((bf16[4,12,96,192]{3,2,1,0:T(8,128)(2,1)}), bf16[4,12,96,192]{3,2,1,0:T(8,128)(2,1)S(1)}, u32[]{:S(2)}, u32[]{:S(2)}) async-start(bf16[4,12,96,192]{3,2,1,0:T(8,128)(2,1)} %shard_map.254), calls=%async_computation.11 | async-start | bytes 4718592 | tf_op jit(solution)/shard_map/all_to_all | solution.py:620
  847.8 32.1 %all-to-all-start.15 = ((bf16[4,12,96,192]{3,2,1,0:T(8,128)(2,1)}), bf16[4,12,96,192]{3,2,1,0:T(8,128)(2,1)S(1)}, u32[]{:S(2)}, u32[]{:S(2)}) async-start(bf16[4,12,96,192]{3,2,1,0:T(8,128)(2,1)} %shard_map.257), calls=%async_computation.15 | async-start | bytes 4718592 | tf_op jit(solution)/shard_map/all_to_all | solution.py:620
  874.9 10.9 %copy-start.11 = (f32[2304,4]{1,0:T(8,128)S(1)}, f32[2304,4]{1,0:T(8,128)}, u32[]{:S(2)}) copy-start(f32[2304,4]{1,0:T(8,128)} %get-tuple-element.28) | copy-start | bytes 110596
  881.3 33.1 %all-to-all-start.12 = ((bf16[4,12,96,192]{3,2,1,0:T(8,128)(2,1)}), bf16[4,12,96,192]{3,2,1,0:T(8,128)(2,1)}, u32[]{:S(2)}, u32[]{:S(2)}) async-start(bf16[4,12,96,192]{3,2,1,0:T(8,128)(2,1)} %shard_map.255), calls=%async_computation.12 | async-start | bytes 4718592 | tf_op jit(solution)/shard_map/all_to_all | solution.py:620
  886.9 6.2 copy-start.22
  919.4 6.4 copy-start.1
  (24 other events, 55.9 us)

commit v4 on v3

--- a/solution.py
+++ b/solution.py
@@ -113,8 +113,12 @@
 def mlp_rows(filtered, gain, shift, w_in, w_out):
     n2 = layer_norm(filtered, gain, shift).astype(bf16)
     total = filtered
-    for a, b in zip(w_in, w_out):
-        total = total + dot(gelu(dot(n2, a[...])).astype(bf16), b[...])
+    hidden = dot(n2, w_in[0][...])
+    for at, b in enumerate(w_out):
+        ready = hidden
+        if at + 1 < len(w_in):
+            hidden = dot(n2, w_in[at + 1][...])
+        total = total + dot(gelu(ready).astype(bf16), b[...])
     return total.astype(bf16)
 
 
@@ -314,7 +318,7 @@
     return pl.BlockSpec((1, bands * 2 * waves, lanes), lambda i: (i, 0, 0))
 
 
-def lon_forward(source, matrix, bands, waves, pair, stats=None):
+def lon_forward(source, matrix, bands, waves, pair, stats=None, early=()):
     if stats is None:
         _, rows, part, width = source.shape
     else:
@@ -363,7 +367,7 @@
     out = pl.pallas_call(
         kernel,
         grid=(count,),
-        in_specs=specs,
+        in_specs=specs + [pl.BlockSpec(memory_space=pl.ANY)] * len(early),
         out_specs=spectrum_block(bands, waves, lanes),
         out_shape=jax.ShapeDtypeStruct(shape, bf16),
         compiler_params=pltpu.CompilerParams(vmem_limit_bytes=vmem_bytes),
@@ -372,7 +376,7 @@
             bytes_accessed=4 * rows * matrix.shape[0] * width,
             transcendentals=0,
         ),
-    )(*args)
+    )(*args, *early)
     if not aligned(waves):
         out = out.reshape(count, bands, 2 * waves, lanes).transpose(1, 0, 2, 3)
     return out
@@ -620,6 +624,24 @@
     return lax.all_to_all(x, quarter, split_axis=0, concat_axis=0, tiled=True)
 
 
+def to_quarter_steps(x, index):
+    n = x.shape[0]
+    take = lambda a, i: lax.dynamic_index_in_dim(a, i % n, 0, keepdims=False)
+    parts = [take(x, index)]
+    for d in range(1, n):
+        pairs = [(i, (i + d) % n) for i in range(n)]
+        parts.append(lax.ppermute(take(x, index + d), quarter, pairs))
+    here = [take_of(parts, (index - i) % n) for i in range(n)]
+    return jnp.stack(here)
+
+
+def take_of(parts, which):
+    out = parts[0]
+    for d in range(1, len(parts)):
+        out = jnp.where(which == d, parts[d], out)
+    return out
+
+
 def modes_of_bands(xs, fwd, back, weights, biases, pair, early):
     bands, count, parts, lanes = xs[0].shape
     xs = [to_band(x) for x in xs]
@@ -634,10 +656,9 @@
     count = lax.axis_size(quarter)
     right = [(i, (i + 1) % count) for i in range(count)]
     left = [((i + 1) % count, i) for i in range(count)]
-    before = lax.ppermute(cells[:, -reach:], quarter, right)
-    after = lax.ppermute(cells[:, :reach], quarter, left)
-    blank = jnp.zeros((cells.shape[0], side - reach, cells.shape[2]), cells.dtype)
-    wide = lambda r: jnp.concatenate([blank[r], before[r], cells[r], after[r], blank[r]], axis=1)
+    before = lax.ppermute(cells[:, -side:], quarter, right)
+    after = lax.ppermute(cells[:, :side], quarter, left)
+    wide = lambda r: jnp.concatenate([before[r], cells[r], after[r]], axis=1)
     count = lax.axis_size("band")
     down = [(i, i + 1) for i in range(count - 1)]
     up = [(i + 1, i) for i in range(count - 1)]
@@ -711,7 +732,8 @@
         u = lon_back_call(
             spectra[h], lon_back, slots, pair, streams[h], stats[h], in1 + out1 if h == 0 else ()
         )
-        u = to_quarter(u).reshape(slots, half * part, slot)
+        u = to_quarter_steps(u, column_index) if h + 1 < halves else to_quarter(u)
+        u = u.reshape(slots, half * part, slot)
         a, f = first_mlp(u, gain(0, 1), shift(0, 1), heads, in0, out0)
         after_one.append(a)
         fluxes.append(f.reshape(half, part, -1))
@@ -727,7 +749,7 @@
     pieces = 2 if halves == 2 and half % 2 == 0 else 1
     tile_rows = start.shape[0] // (halves * pieces)
     cells = tile_rows * tile_columns
-    nexts, surfaces, middles, spectra = [], [], [], []
+    nexts, surfaces, middles, spectra, waiting = [], [], [], [], []
     for h in range(halves):
         patches = []
         for piece in range(pieces):
@@ -744,6 +766,10 @@
                 field_head,
                 spectra[:1] if piece == pieces - 1 else [],
             )
+            if waiting:
+                spectra.append(
+                    lon_forward(waiting.pop(), lon_fwd, bands, waves, pair, early=(ocean_next,))
+                )
             nexts.append(ocean_next.reshape((tile_rows,) + start.shape[1:]))
             surface = surface.reshape(tile_rows, tile_columns, -1)
             surfaces.append(surface)
@@ -762,7 +788,8 @@
             part,
         )
         middles.append(middle)
-        spectra.append(lon_forward(to_quarter(normed), lon_fwd, bands, waves, pair))
+        waiting.append(to_quarter_steps(normed, column_index))
+    spectra.append(lon_forward(waiting.pop(), lon_fwd, bands, waves, pair))
     ocean_next = jnp.concatenate(nexts, axis=0)
     surface = jnp.concatenate(surfaces, axis=0)
 
@@ -771,7 +798,9 @@
     outs = []
     for h in range(halves):
         restored = lon_back_call(spectra[h], lon_back, slots, pair)
-        restored = to_quarter(restored).reshape(slots, half * part, slot)
+        last = h + 1 == halves
+        restored = to_quarter(restored) if last else to_quarter_steps(restored, column_index)
+        restored = restored.reshape(slots, half * part, slot)
         out = second_mlp(
             middles[h], restored, gain(1, 0), shift(1, 0), gain(1, 1), shift(1, 1), in1, out1, part
         )

time: 935 us -> 859 us (0.919)
  blocking collectives: 33 us -> 0 us
  waiting for transfers between devices: 348 us -> 324 us
  local copies, waits for them, and re-layouts: 123 us -> 99.5 us
  other arithmetic: 25.1 us -> 40.5 us
    all_to_all x8, waiting for transfers between devices: 240 us -> 168 us  [to_band(): return lax.all_to_all(x, 'band', split_axis=0, concat_axis=0, tiled=True)]
    ppermute x12, waiting for transfers between devices: 28.3 us -> 72.2 us  [gathered(): lax.ppermute(part, axis, [(i, (i + d) % n) for i in range(n)])]
    all_to_all x7 -> x4, waiting for transfers between devices: 66.4 us -> 23.9 us  [to_quarter(): return lax.all_to_all(x, quarter, split_axis=0, concat_axis=0, tiled=True)]
    ppermute x2 -> x14, waiting for transfers between devices: 4.02 us -> 43.4 us  [the longest x12 39.3 us: to_quarter_steps(): parts.append(lax.ppermute(take(x, index + d), quarter, pairs))]
    all_to_all x1 -> x0, blocking collectives: 33 us -> none  [to_quarter(): return lax.all_to_all(x, quarter, split_axis=0, concat_axis=0, tiled=True)]
    concatenate x3 -> x0, local copies, waits for them, and re-layouts: 27.7 us -> none  [with_halo(): jnp.concatenate([blank[r], before[r], cells[r], after[r], blank[r]], axis=1)]
    all_to_all x7 -> x4, starting transfers between devices: 28.9 us -> 15.6 us  [to_quarter(): return lax.all_to_all(x, quarter, split_axis=0, concat_axis=0, tiled=True)]
    another operation x1 -> x7, other arithmetic: 0.01 us -> 11.4 us  [the longest x6 10.8 us: to_quarter_steps(): return jnp.stack(here)]
  transfers between devices with their start and end apart: 37 -> 46, of which waited for: 22 -> 21; matrix products, arithmetic and copies ran while one was open for 10% -> 11% of each run, Pallas kernels for 14% -> 18%
where the time goes in v4:
time: 859 us; the launch traced here: 851 us
  waiting for transfers between devices  324 us (38%)
  Pallas kernels  291 us (34%)
  local copies, waits for them, and re-layouts  99.5 us (12%)
  starting transfers between devices  83 us (10%)
  other arithmetic  40.5 us (5%)
  matrix products  11.3 us (1%)
    all_to_all x8, waiting for transfers between devices, to_band(): return lax.all_to_all(x, 'band', split_axis=0, concat_axis=0, tiled=True)  168 us
    pallas_call x4, Pallas kernels, ocean_block(): pl.pallas_call(kernel, grid=(rows // step,), in_specs=[whole(extended.sha...  94.6 us
    ppermute x12, waiting for transfers between devices, gathered(): lax.ppermute(part, axis, [(i, (i + d) % n) for i in range(n)])  72.2 us
    pallas_call x2, Pallas kernels, mix_modes(): pl.pallas_call(kernel, grid=(waves // step,), in_specs=[pl.BlockSpec((2 *...  44 us
    pallas_call x2, Pallas kernels, second_mlp(): pl.pallas_call(functools.partial(second_mlp_kernel, n), grid=(tokens // t...  43.5 us
    pallas_call x2, Pallas kernels, first_mlp(): pl.pallas_call(functools.partial(first_mlp_kernel, n), grid=(tokens // ti...  40 us
    ppermute x12, waiting for transfers between devices, to_quarter_steps(): parts.append(lax.ppermute(take(x, index + d), quarter, pairs))  39.3 us
    all_to_all x8, starting transfers between devices, to_band(): return lax.all_to_all(x, 'band', split_axis=0, concat_axis=0, tiled=True)  39 us
  transfers between devices with their start and end apart: 46, of which 21 were waited for; matrix products, arithmetic and copies ran while one was open for 11% of the time, Pallas kernels for 18%

profile of v4, /device:TPU:0, one launch (start us, length us, event | category | flops | bytes accessed | tf_op | source)
XLA Modules:
  0.0 851.0 jit_solution(10668123629558312862)
XLA Ops:
  19.7 7.4 shard_map.239
  27.1 6.0 all-to-all-start.1
  40.3 7.4 shard_map.238
  47.7 26.3 %all-to-all-done.1 = bf16[8,6,48,384]{3,2,1,0:T(8,128)(2,1)S(1)} async-done(((bf16[8,6,48,384]{3,2,1,0:T(8,128)(2,1)}), bf16[8,6,48,384]{3,2,1,0:T(8,128)(2,1)S(1)}, u32[]{:S(2)}, u32[]{:S(2)}) %all-to-all-start.1) | async-done | bytes 1769504 | tf_op jit(solution)/shard_map/all_to_all | solution.py:620
  74.0 3.8 all-to-all-start
  90.5 18.6 %collective-permute-done.5.refs_11_.refs_5_ = bf16[768,768]{1,0:T(8,128)(2,1)} collective-permute-done((bf16[768,768]{1,0:T(8,128)(2,1)}, bf16[768,768]{1,0:T(8,128)(2,1)}, u32[]{:S(2)}, u32[]{:S(2)}) %collective-permute-start.5) | collective-permute-done | bytes 1179680 | tf_op jit(solution)/shard_map/ppermute | solution.py:102
  110.8 5.7 collective-permute-done.9
  127.8 22.0 %shard_map.240 = (bf16[24,96,384]{2,1,0:T(8,128)(2,1)}, bf16[24,96,384]{2,1,0:T(8,128)(2,1)}) custom-call(bf16[48,48,384]{2,1,0:T(8,128)(2,1)} %copy.132.refs_0_, bf16[48,48,384]{2,1,0:T(8,128)(2,1)} %copy.133.refs_1_, bf16[384,384]{1,0:T(8,128)(2,1)} %constant.177.clone.refs_2_, bf16[384,384]{1,0:T(8,128)(2,1)} %constant.178.clone.refs_3_, ...), custom_call_target="tpu_custom_call" | custom-call | flops 5435817984 | bytes 7077888 | tf_op jit(solution)/shard_map/pallas_call | solution.py:289
  155.8 5.9 all-to-all-start.2
  166.3 35.5 %all-to-all-done.2.refs_0_ = bf16[8,6,48,384]{3,2,1,0:T(8,128)(2,1)S(1)} async-done(((bf16[8,6,48,384]{3,2,1,0:T(8,128)(2,1)}), bf16[8,6,48,384]{3,2,1,0:T(8,128)(2,1)S(1)}, u32[]{:S(2)}, u32[]{:S(2)}) %all-to-all-start.2) | async-done | bytes 1769504 | tf_op jit(solution)/shard_map/all_to_all | solution.py:620
  208.0 26.7 %collective-permute-done.12.refs_7_.refs_1_ = bf16[768,768]{1,0:T(8,128)(2,1)} collective-permute-done((bf16[768,768]{1,0:T(8,128)(2,1)}, bf16[768,768]{1,0:T(8,128)(2,1)}, u32[]{:S(2)}, u32[]{:S(2)}) %collective-permute-start.12) | collective-permute-done | bytes 1179680 | tf_op jit(solution)/shard_map/ppermute | solution.py:102
  234.7 23.7 %collective-permute-done.15.refs_11_.refs_5_ = bf16[768,768]{1,0:T(8,128)(2,1)} collective-permute-done((bf16[768,768]{1,0:T(8,128)(2,1)}, bf16[768,768]{1,0:T(8,128)(2,1)}, u32[]{:S(2)}, u32[]{:S(2)}) %collective-permute-start.15) | collective-permute-done | bytes 1179680 | tf_op jit(solution)/shard_map/ppermute | solution.py:102
  261.6 7.5 shard_map.241
  276.5 7.5 shard_map.243
  287.6 13.1 %collective-permute-done.19 = bf16[12,96,192]{2,1,0:T(8,128)(2,1)} collective-permute-done((bf16[12,96,192]{2,1,0:T(8,128)(2,1)}, bf16[12,96,192]{2,1,0:T(8,128)(2,1)}, u32[]{:S(2)}, u32[]{:S(2)}) %collective-permute-start.19) | collective-permute-done | bytes 442400 | tf_op jit(solution)/shard_map/ppermute | solution.py:633
  304.6 20.0 %shard_map.242 = (bf16[1152,768]{1,0:T(8,128)(2,1)}, f32[1152,8]{1,0:T(8,128)}) custom-call(bf16[4,1152,192]{2,1,0:T(8,128)(2,1)} %pad_maximum_fusion.1.u_ref, f32[1,768]{1,0:T(1,128)} %get-tuple-element.122.gain, f32[1,768]{1,0:T(1,128)} %get-tuple-element.118.shift, bf16[768,8]{1,0:T(8,128)(2,1)} %bitcast.302, ...), custom_call_target="tpu_custom_call" | custom-call | flops 10871635968 | bytes 12976128 | tf_op jit(solution)/shard_map/pallas_call | solution.py:139
  327.3 20.0 %shard_map.244 = (bf16[1152,768]{1,0:T(8,128)(2,1)}, f32[1152,8]{1,0:T(8,128)}) custom-call(bf16[4,1152,192]{2,1,0:T(8,128)(2,1)} %bitcast.286, f32[1,768]{1,0:T(1,128)} %get-tuple-element.122.gain, f32[1,768]{1,0:T(1,128)} %get-tuple-element.118.shift, bf16[768,8]{1,0:T(8,128)(2,1)} %bitcast.303, bf16[768,768]{1,0:T(8,128)(2,1)} %get-tuple-element.98.refs_6_.refs_0_, ...), custom_call_target="tpu_custom_call" | custom-call | flops 10871635968 | bytes 12976128 | tf_op jit(solution)/shard_map/pallas_call | solution.py:139
  349.3 11.3 %add_convert_fusion = bf16[48,192,256]{2,1,0:T(8,128)(2,1)S(1)} fusion(bf16[48,192,256]{2,1,0:T(8,128)(2,1)} %param.32, f32[48,192]{1,0:T(8,128)S(1)} %copy-done.20, f32[48,192,8]{1,2,0:T(8,128)S(1)} %copy.141, f32[8,256]{1,0:T(8,128)S(1)} %copy-done), kind=kOutput, calls=%fused_computation | convolution fusion | flops 235929600 | bytes 9777152 | tf_op jit(solution)/shard_map/ijf,fc->ijc/dot_general | solution.py:744
  377.6 7.6 collective-permute-done.23
  385.2 5.3 pad_maximum_fusion.5
  391.3 23.5 %shard_map.245 = (bf16[2304,256]{1,0:T(8,128)(2,1)}, f32[2304,4]{1,0:T(8,128)}) custom-call(bf16[18,208,256]{2,1,0:T(8,128)(2,1)} %get-tuple-element.58.refs_0_, bf16[49,16,128]{2,1,0:T(8,128)(2,1)} %bitcast.297, f32[1,256]{1,0:T(1,128)} %bitcast.306, f32[1,256]{1,0:T(1,128)} %bitcast.310, f32[2304,1]{1,0:T(8,128)} %reshape.230.refs_4_, ...), custom_call_target="tpu_custom_call" | custom-call | flops 2474901504 | bytes 4718592 | tf_op jit(solution)/shard_map/pallas_call | solution.py:544
  416.5 23.6 %shard_map.246 = (bf16[2304,256]{1,0:T(8,128)(2,1)}, f32[2304,4]{1,0:T(8,128)}) custom-call(bf16[18,208,256]{2,1,0:T(8,128)(2,1)} %get-tuple-element.60.refs_0_, bf16[49,16,128]{2,1,0:T(8,128)(2,1)} %bitcast.298, f32[1,256]{1,0:T(1,128)} %bitcast.307, f32[1,256]{1,0:T(1,128)} %bitcast.311, f32[2304,1]{1,0:T(8,128)} %reshape.231.refs_4_, ...), custom_call_target="tpu_custom_call" | custom-call | flops 2474901504 | bytes 4718592 | tf_op jit(solution)/shard_map/pallas_call | solution.py:544
  442.9 5.1 shard_map.247
  454.1 23.9 %shard_map.248 = (bf16[2304,256]{1,0:T(8,128)(2,1)}, f32[2304,4]{1,0:T(8,128)}) custom-call(bf16[18,208,256]{2,1,0:T(8,128)(2,1)} %get-tuple-element.59.refs_0_, bf16[49,16,128]{2,1,0:T(8,128)(2,1)} %bitcast.299, f32[1,256]{1,0:T(1,128)} %bitcast.308, f32[1,256]{1,0:T(1,128)} %bitcast.312, f32[2304,1]{1,0:T(8,128)} %reshape.232.refs_4_, ...), custom_call_target="tpu_custom_call" | custom-call | flops 2474901504 | bytes 4718592 | tf_op jit(solution)/shard_map/pallas_call | solution.py:544
  481.5 5.9 shard_map.249.refs_9_
  487.4 6.5 all-to-all-start.5
  496.7 23.6 %shard_map.250 = (bf16[2304,256]{1,0:T(8,128)(2,1)}, f32[2304,4]{1,0:T(8,128)}) custom-call(bf16[18,208,256]{2,1,0:T(8,128)(2,1)} %get-tuple-element.57.refs_0_, bf16[49,16,128]{2,1,0:T(8,128)(2,1)} %bitcast.300, f32[1,256]{1,0:T(1,128)} %bitcast.309, f32[1,256]{1,0:T(1,128)} %bitcast.313, f32[2304,1]{1,0:T(8,128)} %reshape.233.refs_4_, ...), custom_call_target="tpu_custom_call" | custom-call | flops 2474901504 | bytes 4718592 | tf_op jit(solution)/shard_map/pallas_call | solution.py:544
  523.0 5.1 shard_map.251
  532.7 12.0 %collective-permute-done.28 = bf16[12,96,192]{2,1,0:T(8,128)(2,1)S(1)} collective-permute-done((bf16[12,96,192]{2,1,0:T(8,128)(2,1)S(1)}, bf16[12,96,192]{2,1,0:T(8,128)(2,1)S(1)}, u32[]{:S(2)}, u32[]{:S(2)}) %collective-permute-start.28) | collective-permute-done | bytes 442400 | tf_op jit(solution)/shard_map/ppermute | solution.py:633
  544.7 14.2 %collective-permute-done.29 = bf16[12,96,192]{2,1,0:T(8,128)(2,1)S(1)} collective-permute-done((bf16[12,96,192]{2,1,0:T(8,128)(2,1)S(1)}, bf16[12,96,192]{2,1,0:T(8,128)(2,1)S(1)}, u32[]{:S(2)}, u32[]{:S(2)}) %collective-permute-start.29) | collective-permute-done | bytes 442400 | tf_op jit(solution)/shard_map/ppermute | solution.py:633
  562.3 5.9 shard_map.252
  568.2 5.7 all-to-all-start.6
  576.1 37.8 %all-to-all-done.6 = bf16[8,6,48,384]{3,2,1,0:T(8,128)(2,1)S(1)} async-done(((bf16[8,6,48,384]{3,2,1,0:T(8,128)(2,1)}), bf16[8,6,48,384]{3,2,1,0:T(8,128)(2,1)S(1)}, u32[]{:S(2)}, u32[]{:S(2)}) %all-to-all-start.6) | async-done | bytes 1769504 | tf_op jit(solution)/shard_map/all_to_all | solution.py:620
  615.4 21.9 %shard_map.253 = (bf16[24,96,384]{2,1,0:T(8,128)(2,1)}, bf16[24,96,384]{2,1,0:T(8,128)(2,1)}) custom-call(bf16[48,48,384]{2,1,0:T(8,128)(2,1)} %copy.157.refs_0_, bf16[48,48,384]{2,1,0:T(8,128)(2,1)} %copy.158.refs_1_, bf16[384,384]{1,0:T(8,128)(2,1)} %constant.177.clone.refs_2_, bf16[384,384]{1,0:T(8,128)(2,1)} %constant.178.clone.refs_3_, ...), custom_call_target="tpu_custom_call" | custom-call | flops 5435817984 | bytes 7077888 | tf_op jit(solution)/shard_map/pallas_call | solution.py:289
  643.4 3.7 all-to-all-start.7
  651.7 36.6 %all-to-all-done.7.refs_0_ = bf16[8,6,48,384]{3,2,1,0:T(8,128)(2,1)S(1)} async-done(((bf16[8,6,48,384]{3,2,1,0:T(8,128)(2,1)}), bf16[8,6,48,384]{3,2,1,0:T(8,128)(2,1)S(1)}, u32[]{:S(2)}, u32[]{:S(2)}) %all-to-all-start.7) | async-done | bytes 1769504 | tf_op jit(solution)/shard_map/all_to_all | solution.py:620
  691.9 5.9 shard_map.254
  702.0 31.3 %all-to-all-done.9.refs_0_ = bf16[8,6,48,384]{3,2,1,0:T(8,128)(2,1)S(1)} async-done(((bf16[8,6,48,384]{3,2,1,0:T(8,128)(2,1)}), bf16[8,6,48,384]{3,2,1,0:T(8,128)(2,1)S(1)}, u32[]{:S(2)}, u32[]{:S(2)}) %all-to-all-start.9) | async-done | bytes 1769504 | tf_op jit(solution)/shard_map/all_to_all | solution.py:620
  734.5 6.0 shard_map.256
  740.5 3.8 all-to-all-start.10
  748.0 21.7 %shard_map.255 = bf16[4,12,96,192]{3,2,1,0:T(8,128)(2,1)} custom-call(bf16[1152,768]{1,0:T(8,128)(2,1)} %get-tuple-element.30.v_ref, bf16[4,1152,192]{2,1,0:T(8,128)(2,1)} %pad_maximum_fusion.4.r_ref, f32[1,768]{1,0:T(1,128)} %get-tuple-element.124.gain.gain0, f32[1,768]{1,0:T(1,128)} %get-tuple-element.120.shift.shift0, f32[1,768]{1,0:T(1,128)} %get-tuple-element.121.gain, ...), custom_call_target="tpu_custom_call" | custom-call | flops 10871635968 | bytes 14745600 | tf_op jit(solution)/shard_map/pallas_call | solution.py:184
  777.9 21.8 %shard_map.257 = bf16[4,12,96,192]{3,2,1,0:T(8,128)(2,1)} custom-call(bf16[1152,768]{1,0:T(8,128)(2,1)} %get-tuple-element.38.v_ref, bf16[4,1152,192]{2,1,0:T(8,128)(2,1)} %bitcast.285, f32[1,768]{1,0:T(1,128)} %get-tuple-element.124.gain.gain0, f32[1,768]{1,0:T(1,128)} %get-tuple-element.120.shift.shift0, f32[1,768]{1,0:T(1,128)} %get-tuple-element.121.gain, ...), custom_call_target="tpu_custom_call" | custom-call | flops 10871635968 | bytes 14745600 | tf_op jit(solution)/shard_map/pallas_call | solution.py:184
  799.6 6.7 all-to-all-done.8.refs_0_
  806.3 4.5 all-to-all-start.11
  820.9 4.4 pad_maximum_fusion
  825.3 14.1 %all-to-all-done.11.refs_1_ = bf16[4,12,96,192]{3,2,1,0:T(8,128)(2,1)} async-done(((bf16[4,12,96,192]{3,2,1,0:T(8,128)(2,1)}), bf16[4,12,96,192]{3,2,1,0:T(8,128)(2,1)}, u32[]{:S(2)}, u32[]{:S(2)}) %all-to-all-start.11) | async-done | bytes 1769504 | tf_op jit(solution)/shard_map/all_to_all | solution.py:624
  839.4 5.0 shard_map.258
  844.4 6.3 copy.167
  (244 shorter events, 181.4 us)
Async XLA Ops:
  0.6 348.6 %copy-start = (f32[8,256]{1,0:T(8,128)S(1)}, f32[8,256]{1,0:T(8,128)}, u32[]{:S(2)}) copy-start(f32[8,256]{1,0:T(8,128)} %param.31) | copy-start | bytes 24580
  4.7 5.9 collective-permute-start
  11.5 5.5 collective-permute-start.1
  27.1 46.9 %all-to-all-start.1 = ((bf16[8,6,48,384]{3,2,1,0:T(8,128)(2,1)}), bf16[8,6,48,384]{3,2,1,0:T(8,128)(2,1)S(1)}, u32[]{:S(2)}, u32[]{:S(2)}) async-start(bf16[8,6,48,384]{3,2,1,0:T(8,128)(2,1)} %shard_map.239), calls=%async_computation.1 | async-start | bytes 3538944 | tf_op jit(solution)/shard_map/all_to_all | solution.py:620
  36.3 53.7 %collective-permute-start.2 = (bf16[768,768]{1,0:T(8,128)(2,1)}, bf16[768,768]{1,0:T(8,128)(2,1)}, u32[]{:S(2)}, u32[]{:S(2)}) collective-permute-start(bf16[768,768]{1,0:T(8,128)(2,1)} %get-tuple-element.98.refs_6_.refs_0_), channel_id=1, source_target_pairs={{0,2},{2,0},{1,3},{3,1},{4,6},{6,4},{5,7},{7,5},{8,10},{10,8},{9,1... | collective-permute-start | bytes 3538952 | tf_op jit(solution)/shard_map/ppermute | solution.py:102
  37.8 89.9 %collective-permute-start.3 = (bf16[768,768]{1,0:T(8,128)(2,1)}, bf16[768,768]{1,0:T(8,128)(2,1)}, u32[]{:S(2)}, u32[]{:S(2)}) collective-permute-start(bf16[768,768]{1,0:T(8,128)(2,1)} %get-tuple-element.98.refs_6_.refs_0_), channel_id=1, source_target_pairs={{0,1},{1,0},{2,3},{3,2},{4,5},{5,4},{6,7},{7,6},{8,9},{9,8},{10,11... | collective-permute-start | bytes 3538952 | tf_op jit(solution)/shard_map/ppermute | solution.py:102
  74.0 52.1 %all-to-all-start = ((bf16[8,6,48,384]{3,2,1,0:T(8,128)(2,1)}), bf16[8,6,48,384]{3,2,1,0:T(8,128)(2,1)S(1)}, u32[]{:S(2)}, u32[]{:S(2)}) async-start(bf16[8,6,48,384]{3,2,1,0:T(8,128)(2,1)} %shard_map.238), calls=%async_computation | async-start | bytes 3538944 | tf_op jit(solution)/shard_map/all_to_all | solution.py:620
  81.1 27.9 %collective-permute-start.5 = (bf16[768,768]{1,0:T(8,128)(2,1)}, bf16[768,768]{1,0:T(8,128)(2,1)}, u32[]{:S(2)}, u32[]{:S(2)}) collective-permute-start(bf16[768,768]{1,0:T(8,128)(2,1)} %get-tuple-element.96.refs_10_.refs_4_), channel_id=1, source_target_pairs={{0,2},{2,0},{1,3},{3,1},{4,6},{6,4},{5,7},{7,5},{8,10},{10,8},{9,1... | collective-permute-start | bytes 3538952 | tf_op jit(solution)/shard_map/ppermute | solution.py:102
  82.6 45.1 %collective-permute-start.6 = (bf16[768,768]{1,0:T(8,128)(2,1)}, bf16[768,768]{1,0:T(8,128)(2,1)}, u32[]{:S(2)}, u32[]{:S(2)}) collective-permute-start(bf16[768,768]{1,0:T(8,128)(2,1)} %get-tuple-element.96.refs_10_.refs_4_), channel_id=1, source_target_pairs={{0,1},{1,0},{2,3},{3,2},{4,5},{5,4},{6,7},{7,6},{8,9},{9,8},{10,11... | collective-permute-start | bytes 3538952 | tf_op jit(solution)/shard_map/ppermute | solution.py:102
  84.3 5.6 collective-permute-start.8
  89.9 19.2 %collective-permute-start.10 = (f32[4,16,192]{2,0,1:T(4,128)S(1)}, f32[4,16,192]{2,0,1:T(4,128)S(1)}, u32[]{:S(2)}, u32[]{:S(2)}) collective-permute-start(f32[4,16,192]{2,0,1:T(4,128)S(1)} %broadcast_select_fusion.1), channel_id=1, source_target_pairs={{0,1},{1,0},{2,3},{3,2},{4,5},{5,4},{6,7},{7,6},{8,9},{9,8},{10,11... | collective-permute-start | bytes 147464 | tf_op jit(solution)/shard_map/ppermute | solution.py:88
  90.0 37.8 %collective-permute-start.4 = (bf16[768,768]{1,0:T(8,128)(2,1)}, bf16[768,768]{1,0:T(8,128)(2,1)}, u32[]{:S(2)}, u32[]{:S(2)}) collective-permute-start(bf16[768,768]{1,0:T(8,128)(2,1)} %collective-permute-done.2.refs_7_.refs_1_), channel_id=1, source_target_pairs={{0,1},{1,0},{2,3},{3,2},{4,5},{5,4},{6,7},{7,6},{8,9},{9,8},{10,11... | collective-permute-start | bytes 3538952 | tf_op jit(solution)/shard_map/ppermute | solution.py:102
  109.0 18.7 %collective-permute-start.7 = (bf16[768,768]{1,0:T(8,128)(2,1)}, bf16[768,768]{1,0:T(8,128)(2,1)}, u32[]{:S(2)}, u32[]{:S(2)}) collective-permute-start(bf16[768,768]{1,0:T(8,128)(2,1)} %collective-permute-done.5.refs_11_.refs_5_), channel_id=1, source_target_pairs={{0,1},{1,0},{2,3},{3,2},{4,5},{5,4},{6,7},{7,6},{8,9},{9,8},{10,11... | collective-permute-start | bytes 3538952 | tf_op jit(solution)/shard_map/ppermute | solution.py:102
  109.1 7.4 collective-permute-start.9
  116.5 4.3 collective-permute-start.11
  155.8 46.0 %all-to-all-start.2 = ((bf16[8,6,48,384]{3,2,1,0:T(8,128)(2,1)}), bf16[8,6,48,384]{3,2,1,0:T(8,128)(2,1)S(1)}, u32[]{:S(2)}, u32[]{:S(2)}) async-start(bf16[8,6,48,384]{3,2,1,0:T(8,128)(2,1)} %reshape.198), calls=%async_computation.2 | async-start | bytes 3538944 | tf_op jit(solution)/shard_map/all_to_all | solution.py:620
  201.8 59.8 %copy-start.5 = (bf16[8,6,48,384]{3,2,1,0:T(8,128)(2,1)}, bf16[8,6,48,384]{3,2,1,0:T(8,128)(2,1)S(1)}, u32[]{:S(2)}) copy-start(bf16[8,6,48,384]{3,2,1,0:T(8,128)(2,1)S(1)} %all-to-all-done.2.refs_0_) | copy-start | bytes 5308420
  201.8 73.5 %all-to-all-start.3 = ((bf16[8,6,48,384]{3,2,1,0:T(8,128)(2,1)}), bf16[8,6,48,384]{3,2,1,0:T(8,128)(2,1)S(1)}, u32[]{:S(2)}, u32[]{:S(2)}) async-start(bf16[8,6,48,384]{3,2,1,0:T(8,128)(2,1)} %reshape.201), calls=%async_computation.3 | async-start | bytes 3538944 | tf_op jit(solution)/shard_map/all_to_all | solution.py:620
  205.4 29.3 %collective-permute-start.12 = (bf16[768,768]{1,0:T(8,128)(2,1)}, bf16[768,768]{1,0:T(8,128)(2,1)}, u32[]{:S(2)}, u32[]{:S(2)}) collective-permute-start(bf16[768,768]{1,0:T(8,128)(2,1)} %get-tuple-element.97.refs_6_.refs_0_), channel_id=1, source_target_pairs={{0,2},{2,0},{1,3},{3,1},{4,6},{6,4},{5,7},{7,5},{8,10},{10,8},{9,1... | collective-permute-start | bytes 3538952 | tf_op jit(solution)/shard_map/ppermute | solution.py:102
  207.0 51.4 %collective-permute-start.15 = (bf16[768,768]{1,0:T(8,128)(2,1)}, bf16[768,768]{1,0:T(8,128)(2,1)}, u32[]{:S(2)}, u32[]{:S(2)}) collective-permute-start(bf16[768,768]{1,0:T(8,128)(2,1)} %get-tuple-element.95.refs_10_.refs_4_), channel_id=1, source_target_pairs={{0,2},{2,0},{1,3},{3,1},{4,6},{6,4},{5,7},{7,5},{8,10},{10,8},{9,1... | collective-permute-start | bytes 3538952 | tf_op jit(solution)/shard_map/ppermute | solution.py:102
  207.5 50.9 %collective-permute-start.13 = (bf16[768,768]{1,0:T(8,128)(2,1)}, bf16[768,768]{1,0:T(8,128)(2,1)}, u32[]{:S(2)}, u32[]{:S(2)}) collective-permute-start(bf16[768,768]{1,0:T(8,128)(2,1)} %get-tuple-element.97.refs_6_.refs_0_), channel_id=1, source_target_pairs={{0,1},{1,0},{2,3},{3,2},{4,5},{5,4},{6,7},{7,6},{8,9},{9,8},{10,11... | collective-permute-start | bytes 3538952 | tf_op jit(solution)/shard_map/ppermute | solution.py:102
  207.5 50.9 %collective-permute-start.16 = (bf16[768,768]{1,0:T(8,128)(2,1)}, bf16[768,768]{1,0:T(8,128)(2,1)}, u32[]{:S(2)}, u32[]{:S(2)}) collective-permute-start(bf16[768,768]{1,0:T(8,128)(2,1)} %get-tuple-element.95.refs_10_.refs_4_), channel_id=1, source_target_pairs={{0,1},{1,0},{2,3},{3,2},{4,5},{5,4},{6,7},{7,6},{8,9},{9,8},{10,11... | collective-permute-start | bytes 3538952 | tf_op jit(solution)/shard_map/ppermute | solution.py:102
  234.7 23.8 %collective-permute-start.14 = (bf16[768,768]{1,0:T(8,128)(2,1)}, bf16[768,768]{1,0:T(8,128)(2,1)}, u32[]{:S(2)}, u32[]{:S(2)}) collective-permute-start(bf16[768,768]{1,0:T(8,128)(2,1)} %collective-permute-done.12.refs_7_.refs_1_), channel_id=1, source_target_pairs={{0,1},{1,0},{2,3},{3,2},{4,5},{5,4},{6,7},{7,6},{8,9},{9,8},{10,11... | collective-permute-start | bytes 3538952 | tf_op jit(solution)/shard_map/ppermute | solution.py:102
  258.4 3.2 collective-permute-start.17
  271.8 15.8 %collective-permute-start.18 = (bf16[12,96,192]{2,1,0:T(8,128)(2,1)}, bf16[12,96,192]{2,1,0:T(8,128)(2,1)}, u32[]{:S(2)}, u32[]{:S(2)}) collective-permute-start(bf16[12,96,192]{2,1,0:T(8,128)(2,1)} %get-tuple-element.94), channel_id=1, source_target_pairs={{0,3},{1,0},{2,1},{3,2},{4,7},{5,4},{6,5},{7,6},{8,11},{9,8},{10,9... | collective-permute-start | bytes 1327112 | tf_op jit(solution)/shard_map/ppermute | solution.py:633
  273.1 27.6 %collective-permute-start.19 = (bf16[12,96,192]{2,1,0:T(8,128)(2,1)}, bf16[12,96,192]{2,1,0:T(8,128)(2,1)}, u32[]{:S(2)}, u32[]{:S(2)}) collective-permute-start(bf16[12,96,192]{2,1,0:T(8,128)(2,1)} %get-tuple-element.93), channel_id=1, source_target_pairs={{0,2},{1,3},{2,0},{3,1},{4,6},{5,7},{6,4},{7,5},{8,10},{9,11},{10,... | collective-permute-start | bytes 1327112 | tf_op jit(solution)/shard_map/ppermute | solution.py:633
  273.6 27.1 %collective-permute-start.20 = (bf16[12,96,192]{2,1,0:T(8,128)(2,1)}, bf16[12,96,192]{2,1,0:T(8,128)(2,1)}, u32[]{:S(2)}, u32[]{:S(2)}) collective-permute-start(bf16[12,96,192]{2,1,0:T(8,128)(2,1)} %get-tuple-element.92), channel_id=1, source_target_pairs={{0,1},{1,2},{2,3},{3,0},{4,5},{5,6},{6,7},{7,4},{8,9},{9,10},{10,1... | collective-permute-start | bytes 1327112 | tf_op jit(solution)/shard_map/ppermute | solution.py:633
  284.0 41.9 %all-to-all-start.4 = ((bf16[4,12,96,192]{3,2,1,0:T(8,128)(2,1)}), bf16[4,12,96,192]{3,2,1,0:T(8,128)(2,1)S(1)}, u32[]{:S(2)}, u32[]{:S(2)}) async-start(bf16[4,12,96,192]{3,2,1,0:T(8,128)(2,1)} %shard_map.243), calls=%async_computation.4 | async-start | bytes 4718592 | tf_op jit(solution)/shard_map/all_to_all | solution.py:624
  360.7 5.4 collective-permute-start.21
  360.8 6.2 collective-permute-start.22
  367.0 18.2 %collective-permute-start.23 = (bf16[3,208,256]{2,1,0:T(8,128)(2,1)S(1)}, bf16[3,208,256]{2,1,0:T(8,128)(2,1)S(1)}, u32[]{:S(2)}, u32[]{:S(2)}) collective-permute-start(bf16[3,208,256]{2,1,0:T(8,128)(2,1)S(1)} %pad_maximum_fusion.14), channel_id=1, source_target_pairs={{0,4},{4,8},{8,12},{12,16},{16,20},{20,24},{24,28},{1,5},{5,9},{9,... | collective-permute-start | bytes 958472 | tf_op jit(solution)/shard_map/ppermute | solution.py:665
  370.7 14.5 %collective-permute-start.27 = (bf16[3,208,256]{2,1,0:T(8,128)(2,1)S(1)}, bf16[3,208,256]{2,1,0:T(8,128)(2,1)S(1)}, u32[]{:S(2)}, u32[]{:S(2)}) collective-permute-start(bf16[3,208,256]{2,1,0:T(8,128)(2,1)S(1)} %pad_maximum_fusion.15), channel_id=1, source_target_pairs={{4,0},{8,4},{12,8},{16,12},{20,16},{24,20},{28,24},{5,1},{9,5},{13... | collective-permute-start | bytes 958472 | tf_op jit(solution)/shard_map/ppermute | solution.py:666
  449.5 28.6 %collective-permute-start.24 = (bf16[12,96,192]{2,1,0:T(8,128)(2,1)S(1)}, bf16[12,96,192]{2,1,0:T(8,128)(2,1)S(1)}, u32[]{:S(2)}, u32[]{:S(2)}) collective-permute-start(bf16[12,96,192]{2,1,0:T(8,128)(2,1)S(1)} %get-tuple-element.91), channel_id=1, source_target_pairs={{0,3},{1,0},{2,1},{3,2},{4,7},{5,4},{6,5},{7,6},{8,11},{9,8},{10,9... | collective-permute-start | bytes 1327112 | tf_op jit(solution)/shard_map/ppermute | solution.py:633
  450.4 27.6 %collective-permute-start.25 = (bf16[12,96,192]{2,1,0:T(8,128)(2,1)S(1)}, bf16[12,96,192]{2,1,0:T(8,128)(2,1)S(1)}, u32[]{:S(2)}, u32[]{:S(2)}) collective-permute-start(bf16[12,96,192]{2,1,0:T(8,128)(2,1)S(1)} %get-tuple-element.90), channel_id=1, source_target_pairs={{0,2},{1,3},{2,0},{3,1},{4,6},{5,7},{6,4},{7,5},{8,10},{9,11},{10,... | collective-permute-start | bytes 1327112 | tf_op jit(solution)/shard_map/ppermute | solution.py:633
  451.1 26.9 %collective-permute-start.26 = (bf16[12,96,192]{2,1,0:T(8,128)(2,1)S(1)}, bf16[12,96,192]{2,1,0:T(8,128)(2,1)S(1)}, u32[]{:S(2)}, u32[]{:S(2)}) collective-permute-start(bf16[12,96,192]{2,1,0:T(8,128)(2,1)S(1)} %get-tuple-element.89), channel_id=1, source_target_pairs={{0,1},{1,2},{2,3},{3,0},{4,5},{5,6},{6,7},{7,4},{8,9},{9,10},{10,1... | collective-permute-start | bytes 1327112 | tf_op jit(solution)/shard_map/ppermute | solution.py:633
  487.4 80.8 %all-to-all-start.5 = ((bf16[8,6,48,384]{3,2,1,0:T(8,128)(2,1)}), bf16[8,6,48,384]{3,2,1,0:T(8,128)(2,1)S(1)}, u32[]{:S(2)}, u32[]{:S(2)}) async-start(bf16[8,6,48,384]{3,2,1,0:T(8,128)(2,1)} %shard_map.249.refs_9_), calls=%async_computation.5 | async-start | bytes 3538944 | tf_op jit(solution)/shard_map/all_to_all | solution.py:620
  529.6 15.1 %collective-permute-start.28 = (bf16[12,96,192]{2,1,0:T(8,128)(2,1)S(1)}, bf16[12,96,192]{2,1,0:T(8,128)(2,1)S(1)}, u32[]{:S(2)}, u32[]{:S(2)}) collective-permute-start(bf16[12,96,192]{2,1,0:T(8,128)(2,1)S(1)} %get-tuple-element.88), channel_id=1, source_target_pairs={{0,3},{1,0},{2,1},{3,2},{4,7},{5,4},{6,5},{7,6},{8,11},{9,8},{10,9... | collective-permute-start | bytes 1327112 | tf_op jit(solution)/shard_map/ppermute | solution.py:633
  531.1 27.8 %collective-permute-start.29 = (bf16[12,96,192]{2,1,0:T(8,128)(2,1)S(1)}, bf16[12,96,192]{2,1,0:T(8,128)(2,1)S(1)}, u32[]{:S(2)}, u32[]{:S(2)}) collective-permute-start(bf16[12,96,192]{2,1,0:T(8,128)(2,1)S(1)} %get-tuple-element.87), channel_id=1, source_target_pairs={{0,2},{1,3},{2,0},{3,1},{4,6},{5,7},{6,4},{7,5},{8,10},{9,11},{10,... | collective-permute-start | bytes 1327112 | tf_op jit(solution)/shard_map/ppermute | solution.py:633
  532.6 26.3 %collective-permute-start.30 = (bf16[12,96,192]{2,1,0:T(8,128)(2,1)S(1)}, bf16[12,96,192]{2,1,0:T(8,128)(2,1)S(1)}, u32[]{:S(2)}, u32[]{:S(2)}) collective-permute-start(bf16[12,96,192]{2,1,0:T(8,128)(2,1)S(1)} %get-tuple-element.86), channel_id=1, source_target_pairs={{0,1},{1,2},{2,3},{3,0},{4,5},{5,6},{6,7},{7,4},{8,9},{9,10},{10,1... | collective-permute-start | bytes 1327112 | tf_op jit(solution)/shard_map/ppermute | solution.py:633
  568.2 45.7 %all-to-all-start.6 = ((bf16[8,6,48,384]{3,2,1,0:T(8,128)(2,1)}), bf16[8,6,48,384]{3,2,1,0:T(8,128)(2,1)S(1)}, u32[]{:S(2)}, u32[]{:S(2)}) async-start(bf16[8,6,48,384]{3,2,1,0:T(8,128)(2,1)} %shard_map.252), calls=%async_computation.6 | async-start | bytes 3538944 | tf_op jit(solution)/shard_map/all_to_all | solution.py:620
  643.4 44.9 %all-to-all-start.7 = ((bf16[8,6,48,384]{3,2,1,0:T(8,128)(2,1)}), bf16[8,6,48,384]{3,2,1,0:T(8,128)(2,1)S(1)}, u32[]{:S(2)}, u32[]{:S(2)}) async-start(bf16[8,6,48,384]{3,2,1,0:T(8,128)(2,1)} %reshape.217), calls=%async_computation.7 | async-start | bytes 3538944 | tf_op jit(solution)/shard_map/all_to_all | solution.py:620
  688.3 45.0 %all-to-all-start.9 = ((bf16[8,6,48,384]{3,2,1,0:T(8,128)(2,1)}), bf16[8,6,48,384]{3,2,1,0:T(8,128)(2,1)S(1)}, u32[]{:S(2)}, u32[]{:S(2)}) async-start(bf16[8,6,48,384]{3,2,1,0:T(8,128)(2,1)} %reshape.219), calls=%async_computation.9 | async-start | bytes 3538944 | tf_op jit(solution)/shard_map/all_to_all | solution.py:620
  700.6 43.7 %collective-permute-start.31 = (bf16[12,96,192]{2,1,0:T(8,128)(2,1)}, bf16[12,96,192]{2,1,0:T(8,128)(2,1)S(1)}, u32[]{:S(2)}, u32[]{:S(2)}) collective-permute-start(bf16[12,96,192]{2,1,0:T(8,128)(2,1)} %get-tuple-element.85), channel_id=1, source_target_pairs={{0,3},{1,0},{2,1},{3,2},{4,7},{5,4},{6,5},{7,6},{8,11},{9,8},{10,9... | collective-permute-start | bytes 1327112 | tf_op jit(solution)/shard_map/ppermute | solution.py:633
  700.8 43.6 %collective-permute-start.32 = (bf16[12,96,192]{2,1,0:T(8,128)(2,1)}, bf16[12,96,192]{2,1,0:T(8,128)(2,1)S(1)}, u32[]{:S(2)}, u32[]{:S(2)}) collective-permute-start(bf16[12,96,192]{2,1,0:T(8,128)(2,1)} %get-tuple-element.84), channel_id=1, source_target_pairs={{0,2},{1,3},{2,0},{3,1},{4,6},{5,7},{6,4},{7,5},{8,10},{9,11},{10,... | collective-permute-start | bytes 1327112 | tf_op jit(solution)/shard_map/ppermute | solution.py:633
  702.0 42.4 %collective-permute-start.33 = (bf16[12,96,192]{2,1,0:T(8,128)(2,1)}, bf16[12,96,192]{2,1,0:T(8,128)(2,1)}, u32[]{:S(2)}, u32[]{:S(2)}) collective-permute-start(bf16[12,96,192]{2,1,0:T(8,128)(2,1)} %get-tuple-element.83), channel_id=1, source_target_pairs={{0,1},{1,2},{2,3},{3,0},{4,5},{5,6},{6,7},{7,4},{8,9},{9,10},{10,1... | collective-permute-start | bytes 1327112 | tf_op jit(solution)/shard_map/ppermute | solution.py:633
  740.5 32.3 %all-to-all-start.10 = ((bf16[4,12,96,192]{3,2,1,0:T(8,128)(2,1)}), bf16[4,12,96,192]{3,2,1,0:T(8,128)(2,1)S(1)}, u32[]{:S(2)}, u32[]{:S(2)}) async-start(bf16[4,12,96,192]{3,2,1,0:T(8,128)(2,1)} %shard_map.256), calls=%async_computation.10 | async-start | bytes 4718592 | tf_op jit(solution)/shard_map/all_to_all | solution.py:624
  774.2 32.1 %all-to-all-start.8 = ((bf16[4,12,96,192]{3,2,1,0:T(8,128)(2,1)}), bf16[4,12,96,192]{3,2,1,0:T(8,128)(2,1)S(1)}, u32[]{:S(2)}, u32[]{:S(2)}) async-start(bf16[4,12,96,192]{3,2,1,0:T(8,128)(2,1)} %shard_map.255), calls=%async_computation.8 | async-start | bytes 4718592 | tf_op jit(solution)/shard_map/all_to_all | solution.py:624
  806.3 33.1 %all-to-all-start.11 = ((bf16[4,12,96,192]{3,2,1,0:T(8,128)(2,1)}), bf16[4,12,96,192]{3,2,1,0:T(8,128)(2,1)}, u32[]{:S(2)}, u32[]{:S(2)}) async-start(bf16[4,12,96,192]{3,2,1,0:T(8,128)(2,1)} %shard_map.257), calls=%async_computation.11 | async-start | bytes 4718592 | tf_op jit(solution)/shard_map/all_to_all | solution.py:624
  (29 other events, 190.8 us)
